TPU v7x, 128 devices: a whole 4x4x4 slice. The times are simulated.
128 devices in a mesh: replica: 32 (over x, y, core), section: 4 (over z).
Axes of the slice: x: 4, y: 4, z: 4, core: 2. Of those that a mesh axis runs over, the one named last changes fastest.
Arguments:
- acts_in: bfloat16 [4096, 7168], P('replica'), may hold values from -6 to 6
- cotangent: bfloat16 [4096, 7168], P('replica'), may hold values from -6 to 6
- old_blocks: bfloat16 [128, 112, 128, 256], P(('replica', 'section')), may hold values from -6 to 6
- send_slot: int32 [128, 224], P(('replica', 'section')), may hold values from 0 to 111, as said below
- send_dest: int32 [128, 224], P(('replica', 'section')), may hold values from -1 to 127, as said below
- send_block: int32 [128, 224], P(('replica', 'section')), may hold values from 0 to 111, as said below
- old_first: float32 [128, 4, 128, 256], P(('replica', 'section')), may hold values from -6 to 6
- old_second: float32 [128, 4, 128, 256], P(('replica', 'section')), may hold values from 0.5 to 4
- moment_dest: int32 [128, 4], P(('replica', 'section')), may hold values from 0 to 15, as said below
Outputs:
- new_weight: bfloat16 [4, 128, 128, 256], P('section', 'replica')
- new_first: float32 [4, 128, 128, 256], P('section', 'replica')
- new_second: float32 [4, 128, 128, 256], P('section', 'replica')
Inputs may be any that keep to these rules, and one draw needn't show every extreme that they name: `send_dest`: device numbers are replica times 4 plus section; -1 marks an empty entry. Every device is named with each block index 0 to 111 exactly once over all devices' lists. No device has more than 2 entries for one destination, and some device has exactly 2 for some destination. One device has no entries; one has 224. `send_slot`: 0 where the entry is empty. `send_block`: 0 where the entry is empty. `moment_dest`: within each replica the 4 x 4 entries are each value once.
All inputs are finite; a program needn't handle non-finite values.
Results may differ from a plain program's by a relative error of at most 0.022.
Values may be sent and summed in bfloat16 or wider, within the bound.
No kernel may reach another device: no remote copies, remote signals or barrier semaphores. Data moves between devices by JAX's collectives and lax.ppermute only.
A program may use at most 192 MiB of HBM per device.

v0:
```python
import jax
import jax.numpy as jnp
from jax import lax
from jax.sharding import PartitionSpec as P

MB_TOK = 64
MICRO = 2


rms_eps = 1e-05
beta_first = 0.9
beta_second = 0.95
step_size = 0.1
adam_eps = 1e-08


def passed_along(block, axis, distance):
    devices = range(lax.axis_size(axis))
    route = [(i - distance, i) for i in devices if i - distance in devices]
    return lax.ppermute(block, axis, route)


def gelu_tanh(values):
    return jax.nn.gelu(values, approximate=True)


def section_forward(layer_in, up_matrix, out_matrix):
    scale_in = up_matrix.shape[0] ** (-0.5)
    scale_out = up_matrix.shape[1] ** (-0.5)
    input_wide = layer_in.astype(jnp.float32)
    root_mean = jnp.sqrt(jnp.mean(input_wide * input_wide, axis=-1, keepdims=True) + rms_eps)
    normed_low = (input_wide / root_mean).astype(jnp.bfloat16)
    pre_act = jnp.dot(normed_low, up_matrix, preferred_element_type=jnp.float32) * scale_in
    activated = gelu_tanh(pre_act).astype(jnp.bfloat16)
    branch = lax.dot_general(
        activated, out_matrix, (((1,), (1,)), ((), ())), preferred_element_type=jnp.float32
    )
    return (input_wide + branch * scale_out).astype(jnp.bfloat16)


def section_backward(layer_in, grad_out, up_matrix, out_matrix):
    scale_in = up_matrix.shape[0] ** (-0.5)
    scale_out = up_matrix.shape[1] ** (-0.5)
    input_wide = layer_in.astype(jnp.float32)
    root_mean = jnp.sqrt(jnp.mean(input_wide * input_wide, axis=-1, keepdims=True) + rms_eps)
    normed_wide = input_wide / root_mean
    normed_low = normed_wide.astype(jnp.bfloat16)
    pre_act = jnp.dot(normed_low, up_matrix, preferred_element_type=jnp.float32) * scale_in
    activated = gelu_tanh(pre_act).astype(jnp.bfloat16)
    grad_back = (
        lax.dot_general(
            grad_out, activated, (((0,), (0,)), ((), ())), preferred_element_type=jnp.float32
        )
        * scale_out
    )
    grad_act = jnp.dot(grad_out, out_matrix, preferred_element_type=jnp.float32) * scale_out
    pulled = jax.vjp(gelu_tanh, pre_act)[1](grad_act)[0]
    grad_pre = pulled.astype(jnp.bfloat16)
    grad_up = (
        lax.dot_general(
            normed_low, grad_pre, (((0,), (0,)), ((), ())), preferred_element_type=jnp.float32
        )
        * scale_in
    )
    grad_norm = (
        lax.dot_general(
            grad_pre, up_matrix, (((1,), (1,)), ((), ())), preferred_element_type=jnp.float32
        )
        * scale_in
    )
    correction = jnp.mean(grad_norm * normed_wide, axis=-1, keepdims=True)
    grad_in = grad_out.astype(jnp.float32) + (grad_norm - normed_wide * correction) / root_mean
    return (grad_in.astype(jnp.bfloat16), grad_up, grad_back)


def route_blocks(
    old_blocks, send_slot, send_dest, send_block, replicas, sections, capacity, block_count
):
    devices = replicas * sections
    held = old_blocks[0]
    block_rows = held.shape[1]
    hidden = held.shape[2]
    slots = send_slot.reshape(-1)
    targets = send_dest.reshape(-1)
    block_ids = send_block.reshape(-1)
    entry_count = targets.shape[0]
    entry_order = jnp.arange(entry_count, dtype=jnp.int32)
    is_valid = targets >= 0
    earlier = (
        (targets[None, :] == targets[:, None])
        & (entry_order[None, :] < entry_order[:, None])
        & is_valid[None, :]
    )
    slot_rank = jnp.sum(earlier.astype(jnp.int32), axis=1)
    slot_place = jnp.where(is_valid, targets * capacity + slot_rank, -1)
    positions = jnp.arange(devices * capacity, dtype=jnp.int32)
    slot_hits = slot_place[None, :] == positions[:, None]
    present = jnp.any(slot_hits, axis=1)
    chosen = jnp.sum(jnp.where(slot_hits, entry_order[None, :], 0), axis=1)
    buffer = jnp.take(held, jnp.take(slots, chosen), axis=0)
    buffer = jnp.where(present[:, None, None], buffer, jnp.zeros_like(buffer))
    labels = jnp.where(present, jnp.take(block_ids, chosen), -1).astype(jnp.bfloat16)
    buffer = buffer.reshape(devices, capacity, block_rows, hidden)
    labels = labels.reshape(devices, capacity)
    received, got_labels = (
        lax.all_to_all(buffer, ("replica", "section"), split_axis=0, concat_axis=0, tiled=True),
        lax.all_to_all(labels, ("replica", "section"), split_axis=0, concat_axis=0, tiled=True),
    )
    received = received.reshape(devices * capacity, block_rows, hidden)
    label_ints = got_labels.reshape(-1).astype(jnp.int32)
    label_match = label_ints[None, :] == jnp.arange(block_count, dtype=jnp.int32)[:, None]
    located = jnp.sum(jnp.where(label_match, positions[None, :], 0), axis=1)
    return jnp.take(received, located, axis=0)


def route_moments(old_first, old_second, moment_dest, sections):
    owner_slots = old_first.shape[1]
    targets = moment_dest.reshape(-1)
    wanted = jnp.arange(sections * owner_slots, dtype=jnp.int32)
    slot_hits = targets[None, :] == wanted[:, None]
    present = jnp.any(slot_hits, axis=1)
    chosen = jnp.sum(
        jnp.where(slot_hits, jnp.arange(owner_slots, dtype=jnp.int32)[None, :], 0), axis=1
    )
    first_buf = jnp.take(old_first[0], chosen, axis=0)
    second_buf = jnp.take(old_second[0], chosen, axis=0)
    first_buf = jnp.where(present[:, None, None], first_buf, jnp.zeros_like(first_buf))
    second_buf = jnp.where(present[:, None, None], second_buf, jnp.zeros_like(second_buf))
    shape_out = (sections, owner_slots) + first_buf.shape[1:]
    first_in, second_in = (
        lax.all_to_all(
            first_buf.reshape(shape_out).astype(jnp.bfloat16),
            "section",
            split_axis=0,
            concat_axis=0,
            tiled=True,
        ).astype(jnp.float32),
        lax.all_to_all(
            second_buf.reshape(shape_out).astype(jnp.bfloat16),
            "section",
            split_axis=0,
            concat_axis=0,
            tiled=True,
        ).astype(jnp.float32),
    )
    return (jnp.sum(first_in, axis=0), jnp.sum(second_in, axis=0))


def on_device(
    acts_in,
    cotangent,
    old_blocks,
    send_slot,
    send_dest,
    send_block,
    old_first,
    old_second,
    moment_dest,
):
    model_width = acts_in.shape[1]
    block_rows = old_blocks.shape[2]
    hidden = old_blocks.shape[3]
    block_count = 2 * model_width // block_rows
    half_count = block_count // 2
    sections = lax.axis_size("section")
    replicas = lax.axis_size("replica")
    devices = sections * replicas
    group_size = max(1, -(-block_count // devices))
    capacity = 2 * group_size
    owner_slots = old_first.shape[1]
    padded_count = owner_slots * replicas
    section_idx = lax.axis_index("section")
    replica_idx = lax.axis_index("replica")
    blocks = route_blocks(
        old_blocks, send_slot, send_dest, send_block, replicas, sections, capacity, block_count
    )
    up_matrix = blocks[:half_count].reshape(model_width, hidden)
    out_matrix = blocks[half_count:].reshape(model_width, hidden)
    first_owned, second_owned = route_moments(old_first, old_second, moment_dest, sections)
    micro_inputs = acts_in.reshape(MICRO, MB_TOK, model_width)
    micro_cots = cotangent.reshape(MICRO, MB_TOK, model_width)
    ticks = sections + MICRO - 1
    saved = jnp.zeros((MICRO, MB_TOK, model_width), jnp.bfloat16)
    incoming = jnp.zeros((MB_TOK, model_width), jnp.bfloat16)
    for tick_index in range(ticks):
        micro_index = tick_index - section_idx
        is_valid = (micro_index >= 0) & (micro_index < MICRO)
        clipped = jnp.clip(micro_index, 0, MICRO - 1)
        own_input = lax.dynamic_index_in_dim(micro_inputs, clipped, 0, keepdims=False)
        current = jnp.where(section_idx == 0, own_input, incoming)
        saved = jnp.where(
            is_valid, lax.dynamic_update_index_in_dim(saved, current, clipped, 0), saved
        )
        if tick_index < ticks - 1:
            produced = section_forward(current, up_matrix, out_matrix)
            incoming = passed_along(produced, "section", 1)
    grad_up_sum = jnp.zeros((model_width, hidden), jnp.float32)
    grad_back_sum = jnp.zeros((model_width, hidden), jnp.float32)
    back_input = jnp.zeros((MB_TOK, model_width), jnp.bfloat16)
    for tick_index in range(ticks):
        micro_index = tick_index - (sections - 1 - section_idx)
        is_valid = (micro_index >= 0) & (micro_index < MICRO)
        clipped = jnp.clip(micro_index, 0, MICRO - 1)
        own_cot = lax.dynamic_index_in_dim(micro_cots, clipped, 0, keepdims=False)
        grad_y = jnp.where(section_idx == sections - 1, own_cot, back_input)
        layer_in = lax.dynamic_index_in_dim(saved, clipped, 0, keepdims=False)
        grad_in, grad_up, grad_back = section_backward(layer_in, grad_y, up_matrix, out_matrix)
        grad_up_sum = jnp.where(is_valid, grad_up_sum + grad_up, grad_up_sum)
        grad_back_sum = jnp.where(is_valid, grad_back_sum + grad_back, grad_back_sum)
        if tick_index < ticks - 1:
            back_input = passed_along(grad_in, "section", -1)
    gradients = jnp.concatenate(
        [
            grad_up_sum.reshape(half_count, block_rows, hidden),
            grad_back_sum.reshape(half_count, block_rows, hidden),
            jnp.zeros((padded_count - block_count, block_rows, hidden), jnp.float32),
        ],
        axis=0,
    )
    summed = lax.psum(gradients.astype(jnp.bfloat16), "replica").astype(jnp.float32)
    owned_grad = lax.dynamic_slice_in_dim(summed, replica_idx * owner_slots, owner_slots, 0)
    padded_blocks = jnp.concatenate(
        [blocks, jnp.zeros((padded_count - block_count, block_rows, hidden), jnp.bfloat16)], axis=0
    )
    owned_weight = lax.dynamic_slice_in_dim(
        padded_blocks, replica_idx * owner_slots, owner_slots, 0
    )
    new_first = beta_first * first_owned + (1.0 - beta_first) * owned_grad
    new_second = beta_second * second_owned + (1.0 - beta_second) * owned_grad * owned_grad
    new_weight = (
        owned_weight.astype(jnp.float32) - step_size * new_first / (jnp.sqrt(new_second) + adam_eps)
    ).astype(jnp.bfloat16)
    return (new_weight[None], new_first[None], new_second[None])


def solution(mesh):
    in_specs = (
        P("replica", None),
        P("replica", None),
        P(("replica", "section"), None, None, None),
        P(("replica", "section"), None),
        P(("replica", "section"), None),
        P(("replica", "section"), None),
        P(("replica", "section"), None, None, None),
        P(("replica", "section"), None, None, None),
        P(("replica", "section"), None),
    )
    out_specs = (
        P("section", "replica", None, None),
        P("section", "replica", None, None),
        P("section", "replica", None, None),
    )
    return jax.shard_map(
        on_device, mesh=mesh, in_specs=in_specs, out_specs=out_specs, check_vma=False
    )
```

profile of v0, /device:TPU:8, one launch (start us, length us, event | category | flops | bytes accessed | tf_op | source)
XLA Modules:
  0.0 692.9 jit_solution(1831383465547246651)
XLA Ops:
  12.6 10.4 %all-to-all-start = ((bf16[128,1,2]{2,1,0:T(2,128)(2,1)}), bf16[128,1,2]{2,1,0:T(2,128)(2,1)S(1)}, u32[]{:S(2)}, u32[]{:S(2)}) async-start(bf16[128,1,2]{2,1,0:T(2,128)(2,1)} %all_to_all.20), calls=%async_computation | async-start | bytes 131072 | tf_op jit(solution)/shard_map/all_to_all | solution.py:107
  25.4 12.4 %gather_fusion = bf16[256,128,256]{2,1,0:T(8,128)(2,1)} fusion(bf16[112,128,256]{2,1,0:T(8,128)(2,1)} %bitcast.232, s32[1024]{0:T(1024)S(1)} %pad_clamp_fusion.2), kind=kCustom, calls=%fused_computation.4 | custom fusion | bytes 33555456 | tf_op jit(solution)/shard_map/jit(_take)/gather | solution.py:100
  37.8 14.4 %select_select_fusion = bf16[128,2,128,256]{3,2,1,0:T(8,128)(2,1)} fusion(bf16[128,2,128,256]{3,2,1,0:T(8,128)(2,1)} %bitcast.231, pred[128,2]{1,0:T(8,128)(4,1)S(1)} %broadcast_in_dim.170, pred[128,2]{1,0:T(8,128)(4,1)S(1)} %broadcast_in_dim.168), kind=kLoop, calls=%fused_computation.6 | loop fusion | flops 16777216 | bytes 33554944 | tf_op jit(solution)/shard_map/jit(_where)/select_n | solution.py:101
  52.2 10.2 %all-to-all-start.1 = ((bf16[128,2,128,256]{3,2,1,0:T(8,128)(2,1)}), bf16[128,2,128,256]{3,2,1,0:T(8,128)(2,1)}, u32[]{:S(2)}, u32[]{:S(2)}) async-start(bf16[128,2,128,256]{3,2,1,0:T(8,128)(2,1)} %select_select_fusion), calls=%async_computation.1 | async-start | bytes 33554432 | tf_op jit(solution)/shard_map/all_to_all | solution.py:106
  63.4 220.1 %all-to-all-done.1 = bf16[128,2,128,256]{3,2,1,0:T(8,128)(2,1)} async-done(((bf16[128,2,128,256]{3,2,1,0:T(8,128)(2,1)}), bf16[128,2,128,256]{3,2,1,0:T(8,128)(2,1)}, u32[]{:S(2)}, u32[]{:S(2)}) %all-to-all-start.1) | async-done | bytes 16777248 | tf_op jit(solution)/shard_map/all_to_all | solution.py:106
  283.5 12.1 %gather_fusion.1 = bf16[112,128,256]{2,1,0:T(8,128)(2,1)} fusion(bf16[256,128,256]{2,1,0:T(8,128)(2,1)} %bitcast.7, s32[1024]{0:T(1024)S(1)} %pad_clamp_fusion.1), kind=kCustom, calls=%fused_computation.5 | custom fusion | bytes 14680512 | tf_op jit(solution)/shard_map/jit(_take)/gather | solution.py:113
  299.4 3.8 fusion.309
  304.6 5.9 fusion.8
  315.8 16.6 %collective-permute-done = bf16[64,7168]{1,0:T(8,128)(2,1)} collective-permute-done((bf16[64,7168]{1,0:T(8,128)(2,1)S(1)}, bf16[64,7168]{1,0:T(8,128)(2,1)}, u32[]{:S(2)}, u32[]{:S(2)}) %collective-permute-start) | collective-permute-done | bytes 917536 | tf_op jit(solution)/shard_map/ppermute | solution.py:20
  332.9 6.9 fusion.9
  339.8 10.2 %collective-permute-start.1 = (bf16[64,7168]{1,0:T(8,128)(2,1)}, bf16[64,7168]{1,0:T(8,128)(2,1)S(1)}, u32[]{:S(2)}, u32[]{:S(2)}) collective-permute-start(bf16[64,7168]{1,0:T(8,128)(2,1)} %fusion.9), channel_id=1, source_target_pairs={{0,1},{1,2},{2,3},{4,5},{5,6},{6,7},{8,9},{9,10},{10,11},{12,13},{... | collective-permute-start | bytes 2752520 | tf_op jit(solution)/shard_map/ppermute | solution.py:20
  350.2 18.0 %collective-permute-done.1 = bf16[64,7168]{1,0:T(8,128)(2,1)S(1)} collective-permute-done((bf16[64,7168]{1,0:T(8,128)(2,1)}, bf16[64,7168]{1,0:T(8,128)(2,1)S(1)}, u32[]{:S(2)}, u32[]{:S(2)}) %collective-permute-start.1) | collective-permute-done | bytes 917536 | tf_op jit(solution)/shard_map/ppermute | solution.py:20
  368.7 6.9 fusion.10
  375.5 4.7 collective-permute-start.2
  380.5 17.0 %collective-permute-done.2 = bf16[64,7168]{1,0:T(8,128)(2,1)S(1)} collective-permute-done((bf16[64,7168]{1,0:T(8,128)(2,1)}, bf16[64,7168]{1,0:T(8,128)(2,1)S(1)}, u32[]{:S(2)}, u32[]{:S(2)}) %collective-permute-start.2) | collective-permute-done | bytes 917536 | tf_op jit(solution)/shard_map/ppermute | solution.py:20
  398.0 6.9 fusion.11
  404.9 4.5 collective-permute-start.3
  409.6 16.1 %collective-permute-done.3 = bf16[64,7168]{1,0:T(8,128)(2,1)S(1)} collective-permute-done((bf16[64,7168]{1,0:T(8,128)(2,1)}, bf16[64,7168]{1,0:T(8,128)(2,1)S(1)}, u32[]{:S(2)}, u32[]{:S(2)}) %collective-permute-start.3) | collective-permute-done | bytes 917536 | tf_op jit(solution)/shard_map/ppermute | solution.py:20
  433.3 4.2 fusion
  439.6 12.5 %collective-permute-done.4 = bf16[64,7168]{1,0:T(8,128)(2,1)S(1)} collective-permute-done((bf16[64,7168]{1,0:T(8,128)(2,1)S(1)}, bf16[64,7168]{1,0:T(8,128)(2,1)S(1)}, u32[]{:S(2)}, u32[]{:S(2)}) %collective-permute-start.4) | collective-permute-done | bytes 917536 | tf_op jit(solution)/shard_map/ppermute | solution.py:20
  458.3 16.2 %collective-permute-done.5 = bf16[64,7168]{1,0:T(8,128)(2,1)S(1)} collective-permute-done((bf16[64,7168]{1,0:T(8,128)(2,1)S(1)}, bf16[64,7168]{1,0:T(8,128)(2,1)S(1)}, u32[]{:S(2)}, u32[]{:S(2)}) %collective-permute-start.5) | collective-permute-done | bytes 917536 | tf_op jit(solution)/shard_map/ppermute | solution.py:20
  479.4 4.1 convolution_multiply_fusion.2
  484.8 10.8 %collective-permute-done.6 = bf16[64,7168]{1,0:T(8,128)(2,1)S(1)} collective-permute-done((bf16[64,7168]{1,0:T(8,128)(2,1)S(1)}, bf16[64,7168]{1,0:T(8,128)(2,1)S(1)}, u32[]{:S(2)}, u32[]{:S(2)}) %collective-permute-start.6) | collective-permute-done | bytes 917536 | tf_op jit(solution)/shard_map/ppermute | solution.py:20
  500.7 4.1 convolution_multiply_fusion.1
  504.8 4.2 add_select_fusion.5
  509.1 7.5 %collective-permute-done.7 = bf16[64,7168]{1,0:T(8,128)(2,1)S(1)} collective-permute-done((bf16[64,7168]{1,0:T(8,128)(2,1)S(1)}, bf16[64,7168]{1,0:T(8,128)(2,1)S(1)}, u32[]{:S(2)}, u32[]{:S(2)}) %collective-permute-start.7) | collective-permute-done | bytes 917536 | tf_op jit(solution)/shard_map/ppermute | solution.py:20
  517.8 10.7 %fusion.3 = bf16[7168,256]{1,0:T(8,128)(2,1)} fusion(f32[7168,256]{1,0:T(8,128)S(1)} %convolution_multiply_fusion, f32[7168,256]{1,0:T(8,128)} %convolution_multiply_fusion.1, f32[7168,256]{1,0:T(8,128)} %convolution_multiply_fusion.2, f32[7168,256]{1,0:T(8,128)} %fusion, bf16[64,7168]{1,0:T(8,128)(2,1)S(1)} %bitcast_select_fusion.3, pred[]{:T(512)S(6)} %and.74, ...), kind=kOutput, calls=%fused_computation.28 | convolution fusion | flops 253378560 | bytes 34013188 | tf_op jit(solution)/shard_map/dot_general | solution.py:51
  528.4 9.3 %fusion.2 = bf16[7168,256]{1,0:T(8,128)(2,1)} fusion(f32[7168,256]{1,0:T(8,128)} %add_select_fusion.5, pred[]{:T(512)S(6)} %and.71, f32[64]{0:T(128)S(1)} %add_sqrt_fusion, bf16[2,64,7168]{2,1,0:T(8,128)(2,1)S(1)} %fusion.62, s32[]{:T(128)S(6)} %min.40, f32[64,256]{1,0:T(8,128)S(1)} %convolution_multiply_fusion.18, bf16[7168,256]{1,0:T(8,128)(2,1)} %bitcast.226, ...), kind=kOutput, calls=%fused_computation.27 | convolution fusion | flops 479281152 | bytes 17500672 | tf_op jit(solution)/shard_map/dot_general | solution.py:60
  537.7 7.0 %maximum_maximum_fusion = bf16[128,128,256]{2,1,0:T(8,128)(2,1)} fusion(bf16[56,128,256]{2,1,0:T(8,128)(2,1)} %bitcast.248, bf16[56,128,256]{2,1,0:T(8,128)(2,1)} %bitcast.263, bf16[128]{0:T(256)(128)(2,1)S(1)} %pad.3.clone), kind=kLoop, calls=%fused_computation.29 | loop fusion | flops 8388608 | bytes 15728896 | tf_op jit(solution)/shard_map/concatenate | solution.py:212
  548.6 15.8 %all_to_all.25 = bf16[4,4,128,256]{3,2,1,0:T(8,128)(2,1)S(1)} all-to-all(bf16[4,4,128,256]{3,2,1,0:T(8,128)(2,1)S(1)} %bitcast.249), channel_id=1, replica_groups=mesh['replica'=32,'section'=4] {'section'}, dimensions={0} | all-to-all | bytes 2097152 | tf_op jit(solution)/shard_map/all_to_all | solution.py:138
  568.1 10.7 %all-to-all-done.2 = bf16[4,4,128,256]{3,2,1,0:T(8,128)(2,1)S(1)} async-done(((bf16[4,4,128,256]{3,2,1,0:T(8,128)(2,1)}), bf16[4,4,128,256]{3,2,1,0:T(8,128)(2,1)S(1)}, u32[]{:S(2)}, u32[]{:S(2)}) %all-to-all-start.2) | async-done | bytes 1048608 | tf_op jit(solution)/shard_map/all_to_all | solution.py:131
  578.9 104.4 %all-reduce.3.cloned.1.call-done = bf16[128,128,256]{2,1,0:T(8,128)(2,1)} async-done(((bf16[128,128,256]{2,1,0:T(8,128)(2,1)}), bf16[128,128,256]{2,1,0:T(8,128)(2,1)}) %all-reduce.3.cloned.1.call-update) | async-done | bytes 8388624 | tf_op jit(solution)/shard_map/psum | solution.py:220
  (118 shorter events, 59.3 us)
Async XLA Ops:
  7.2 538.3 %copy-start = (f32[1,4,128,256]{3,2,1,0:T(8,128)S(1)}, f32[1,4,128,256]{3,2,1,0:T(8,128)}, u32[]{:S(2)}) copy-start(f32[1,4,128,256]{3,2,1,0:T(8,128)} %param.19) | copy-start | bytes 1572868
  7.2 16.1 %copy-start.1 = (s32[1,224]{1,0:T(1,128)S(1)}, s32[1,224]{1,0:T(1,128)}, u32[]{:S(2)}) copy-start(s32[1,224]{1,0:T(1,128)} %param.16) | copy-start | bytes 2692
  12.6 39.6 %all-to-all-start = ((bf16[128,1,2]{2,1,0:T(2,128)(2,1)}), bf16[128,1,2]{2,1,0:T(2,128)(2,1)S(1)}, u32[]{:S(2)}, u32[]{:S(2)}) async-start(bf16[128,1,2]{2,1,0:T(2,128)(2,1)} %all_to_all.20), calls=%async_computation | async-start | bytes 131072 | tf_op jit(solution)/shard_map/all_to_all | solution.py:107
  52.2 10.3 %copy-start.5 = (bf16[128,7168]{1,0:T(8,128)(2,1)S(1)}, bf16[128,7168]{1,0:T(8,128)(2,1)}, u32[]{:S(2)}) copy-start(bf16[128,7168]{1,0:T(8,128)(2,1)} %param.13) | copy-start | bytes 5505028
  52.2 231.3 %all-to-all-start.1 = ((bf16[128,2,128,256]{3,2,1,0:T(8,128)(2,1)}), bf16[128,2,128,256]{3,2,1,0:T(8,128)(2,1)}, u32[]{:S(2)}, u32[]{:S(2)}) async-start(bf16[128,2,128,256]{3,2,1,0:T(8,128)(2,1)} %select_select_fusion), calls=%async_computation.1 | async-start | bytes 33554432 | tf_op jit(solution)/shard_map/all_to_all | solution.py:106
  62.5 620.9 %all-reduce.3.cloned.1.call-start = ((), (), s32[]{:S(2)}) async-start(), calls=%async_computation.4 | async-start | bytes 16777216 | tf_op jit(solution)/shard_map/psum | solution.py:220
  299.4 5.2 copy-start.3
  310.6 21.9 %collective-permute-start = (bf16[64,7168]{1,0:T(8,128)(2,1)S(1)}, bf16[64,7168]{1,0:T(8,128)(2,1)}, u32[]{:S(2)}, u32[]{:S(2)}) collective-permute-start(bf16[64,7168]{1,0:T(8,128)(2,1)S(1)} %fusion.8), channel_id=1, source_target_pairs={{0,1},{1,2},{2,3},{4,5},{5,6},{6,7},{8,9},{9,10},{10,11},{12,13},{... | collective-permute-start | bytes 2752520 | tf_op jit(solution)/shard_map/ppermute | solution.py:20
  314.1 1.5 copy-start.6
  339.8 28.4 %copy-start.7 = (bf16[128,7168]{1,0:T(8,128)(2,1)S(1)}, bf16[128,7168]{1,0:T(8,128)(2,1)}, u32[]{:S(2)}) copy-start(bf16[128,7168]{1,0:T(8,128)(2,1)} %param.13) | copy-start | bytes 5505028
  339.8 28.4 %collective-permute-start.1 = (bf16[64,7168]{1,0:T(8,128)(2,1)}, bf16[64,7168]{1,0:T(8,128)(2,1)S(1)}, u32[]{:S(2)}, u32[]{:S(2)}) collective-permute-start(bf16[64,7168]{1,0:T(8,128)(2,1)} %fusion.9), channel_id=1, source_target_pairs={{0,1},{1,2},{2,3},{4,5},{5,6},{6,7},{8,9},{9,10},{10,11},{12,13},{... | collective-permute-start | bytes 2752520 | tf_op jit(solution)/shard_map/ppermute | solution.py:20
  375.5 22.0 %copy-start.8 = (bf16[128,7168]{1,0:T(8,128)(2,1)S(1)}, bf16[128,7168]{1,0:T(8,128)(2,1)}, u32[]{:S(2)}) copy-start(bf16[128,7168]{1,0:T(8,128)(2,1)} %param.13) | copy-start | bytes 5505028
  375.5 22.0 %collective-permute-start.2 = (bf16[64,7168]{1,0:T(8,128)(2,1)}, bf16[64,7168]{1,0:T(8,128)(2,1)S(1)}, u32[]{:S(2)}, u32[]{:S(2)}) collective-permute-start(bf16[64,7168]{1,0:T(8,128)(2,1)} %fusion.10), channel_id=1, source_target_pairs={{0,1},{1,2},{2,3},{4,5},{5,6},{6,7},{8,9},{9,10},{10,11},{12,13},{... | collective-permute-start | bytes 2752520 | tf_op jit(solution)/shard_map/ppermute | solution.py:20
  404.9 20.9 %copy-start.9 = (bf16[128,7168]{1,0:T(8,128)(2,1)S(1)}, bf16[128,7168]{1,0:T(8,128)(2,1)}, u32[]{:S(2)}) copy-start(bf16[128,7168]{1,0:T(8,128)(2,1)} %param.13) | copy-start | bytes 5505028
  404.9 20.9 %collective-permute-start.3 = (bf16[64,7168]{1,0:T(8,128)(2,1)}, bf16[64,7168]{1,0:T(8,128)(2,1)S(1)}, u32[]{:S(2)}, u32[]{:S(2)}) collective-permute-start(bf16[64,7168]{1,0:T(8,128)(2,1)} %fusion.11), channel_id=1, source_target_pairs={{0,1},{1,2},{2,3},{4,5},{5,6},{6,7},{8,9},{9,10},{10,11},{12,13},{... | collective-permute-start | bytes 2752520 | tf_op jit(solution)/shard_map/ppermute | solution.py:20
  409.6 16.9 %copy-start.10 = (bf16[56,128,256]{2,1,0:T(8,128)(2,1)S(1)}, bf16[56,128,256]{2,1,0:T(8,128)(2,1)}, u32[]{:S(2)}) copy-start(bf16[56,128,256]{2,1,0:T(8,128)(2,1)} %get-tuple-element.25) | copy-start | bytes 11010052
  426.5 2.0 copy-start.2
  426.5 2.6 copy-start.4
  431.8 20.3 %collective-permute-start.4 = (bf16[64,7168]{1,0:T(8,128)(2,1)S(1)}, bf16[64,7168]{1,0:T(8,128)(2,1)S(1)}, u32[]{:S(2)}, u32[]{:S(2)}) collective-permute-start(bf16[64,7168]{1,0:T(8,128)(2,1)S(1)} %add_convert_fusion.3), channel_id=1, source_target_pairs={{1,0},{2,1},{3,2},{5,4},{6,5},{7,6},{9,8},{10,9},{11,10},{13,12},{... | collective-permute-start | bytes 2752520 | tf_op jit(solution)/shard_map/ppermute | solution.py:20
  454.9 19.6 %collective-permute-start.5 = (bf16[64,7168]{1,0:T(8,128)(2,1)S(1)}, bf16[64,7168]{1,0:T(8,128)(2,1)S(1)}, u32[]{:S(2)}, u32[]{:S(2)}) collective-permute-start(bf16[64,7168]{1,0:T(8,128)(2,1)S(1)} %add_convert_fusion.2), channel_id=1, source_target_pairs={{1,0},{2,1},{3,2},{5,4},{6,5},{7,6},{9,8},{10,9},{11,10},{13,12},{... | collective-permute-start | bytes 2752520 | tf_op jit(solution)/shard_map/ppermute | solution.py:20
  477.2 18.3 %collective-permute-start.6 = (bf16[64,7168]{1,0:T(8,128)(2,1)S(1)}, bf16[64,7168]{1,0:T(8,128)(2,1)S(1)}, u32[]{:S(2)}, u32[]{:S(2)}) collective-permute-start(bf16[64,7168]{1,0:T(8,128)(2,1)S(1)} %add_convert_fusion.1), channel_id=1, source_target_pairs={{1,0},{2,1},{3,2},{5,4},{6,5},{7,6},{9,8},{10,9},{11,10},{13,12},{... | collective-permute-start | bytes 2752520 | tf_op jit(solution)/shard_map/ppermute | solution.py:20
  499.2 17.4 %collective-permute-start.7 = (bf16[64,7168]{1,0:T(8,128)(2,1)S(1)}, bf16[64,7168]{1,0:T(8,128)(2,1)S(1)}, u32[]{:S(2)}, u32[]{:S(2)}) collective-permute-start(bf16[64,7168]{1,0:T(8,128)(2,1)S(1)} %add_convert_fusion), channel_id=1, source_target_pairs={{1,0},{2,1},{3,2},{5,4},{6,5},{7,6},{9,8},{10,9},{11,10},{13,12},{... | collective-permute-start | bytes 2752520 | tf_op jit(solution)/shard_map/ppermute | solution.py:20
  544.7 0.7 copy-start.12
  544.7 1.4 copy-start.11
  564.4 14.4 %all-to-all-start.2 = ((bf16[4,4,128,256]{3,2,1,0:T(8,128)(2,1)}), bf16[4,4,128,256]{3,2,1,0:T(8,128)(2,1)S(1)}, u32[]{:S(2)}, u32[]{:S(2)}) async-start(bf16[4,4,128,256]{3,2,1,0:T(8,128)(2,1)} %bitcast.12), calls=%async_computation.2 | async-start | bytes 2097152 | tf_op jit(solution)/shard_map/all_to_all | solution.py:131
Sparse Core Ops, SparseCore 0:
  544.8 138.4 all-reduce.2
where the time goes:
time: 703 us; the launch traced here: 693 us
  waiting for transfers between devices  450 us (64%)
  matrix products  80.9 us (12%)
  starting transfers between devices  52.5 us (7%)
  local copies, waits for them, and re-layouts  40.1 us (6%)
  other arithmetic  38.7 us (6%)
  blocking collectives  15.8 us (2%)
  between operations  14.9 us (2%)
    all_to_all x1, waiting for transfers between devices, route_blocks(): lax.all_to_all(buffer, ('replica', 'section'), split_axis=0, concat_axis=...  220 us
    ppermute x8, waiting for transfers between devices, passed_along(): return lax.ppermute(block, axis, route)  115 us
    psum x1, waiting for transfers between devices, on_device(): lax.psum(gradients.astype(jnp.bfloat16), 'replica').astype(jnp.float32)  104 us
    ppermute x8, starting transfers between devices, passed_along(): return lax.ppermute(block, axis, route)  28.3 us
    dot_general x4, matrix products, section_forward(): lax.dot_general(activated, out_matrix, (((1,), (1,)), ((), ())), preferre...  26.6 us
    dot_general x5, matrix products, section_backward(): lax.dot_general(grad_out, activated, (((0,), (0,)), ((), ())), preferred_...  24.2 us
    dot_general x5, matrix products, section_backward(): lax.dot_general(normed_low, grad_pre, (((0,), (0,)), ((), ())), preferred...  17.4 us
    all_to_all x1, blocking collectives, route_moments(): lax.all_to_all(second_buf.reshape(shape_out).astype(jnp.bfloat16), 'secti...  15.8 us
  transfers between devices with their start and end apart: 12, of which 11 were waited for; matrix products, arithmetic and copies ran while one was open for 8% of the time, Pallas kernels for 0%

commit v1 on v0

v1 whole, which is shorter than its diff:
```python
import functools

import jax
import jax.numpy as jnp
from jax import lax
from jax.experimental import pallas as pl
from jax.experimental.pallas import tpu as pltpu
from jax.sharding import PartitionSpec as P


D = 7168
HID = 256
TOK = 128
NBLK = 112
HALF = 56
PIECE = 32
LOCAL = HALF * PIECE
GROUPS = LOCAL // 128
SECTIONS = 4
REPLICAS = 32
DEVICES = 128
OWN = 4
REAL_OWNERS = NBLK // OWN
BIG = 1 << 20
EVERY = ("replica", "section")

rms_eps = 1e-05
beta_first = 0.9
beta_second = 0.95
step_size = 0.1
adam_eps = 1e-08
SCALE_IN = D ** (-0.5)
SCALE_OUT = HID ** (-0.5)

f32 = jnp.float32
bf16 = jnp.bfloat16
ANY = pl.BlockSpec(memory_space=pl.ANY)
SMEM = pl.BlockSpec(memory_space=pltpu.SMEM)
VMEM = pl.BlockSpec(memory_space=pltpu.VMEM)
LIMIT = 12 * 1024 * 1024


def struct(shape, dtype):
    return jax.ShapeDtypeStruct(shape, dtype)


def call(kernel, out_shape, in_specs, out_specs, scratch=(), after=()):
    waits = len(after)

    def body(*refs):
        kernel(*refs[waits:])

    run = pl.pallas_call(
        body,
        out_shape=out_shape,
        in_specs=[ANY] * waits + in_specs,
        out_specs=out_specs,
        scratch_shapes=list(scratch),
        compiler_params=pltpu.CompilerParams(vmem_limit_bytes=LIMIT),
    )
    return lambda *arrays: run(*after, *arrays)


def replica_at(x, y, core):
    return ((x % 4) * 4 + (y % 4)) * 2 + core


def shift_xy(block, step_x, step_y):
    route = [
        (replica_at(x, y, c), replica_at(x + step_x, y + step_y, c))
        for x in range(4)
        for y in range(4)
        for c in range(2)
    ]
    return lax.ppermute(block, "replica", route)


def shift_z(block, step):
    return lax.ppermute(block, "section", [(i, (i + step) % 4) for i in range(4)])


def from_sibling(block):
    return lax.ppermute(block, "replica", [(i, i ^ 1) for i in range(REPLICAS)])


def pack_kernel(slots, blocks, out, room, came, went):
    def start(d, carry):
        r = d // 4
        pltpu.make_async_copy(
            blocks.at[slots[d]], room.at[r, :, d % 4], came.at[r // 4]
        ).start()
        return carry

    lax.fori_loop(0, DEVICES, start, 0)
    for part in range(8):
        rows = pl.ds(part * 4, 4)
        pltpu.make_async_copy(room.at[rows], room.at[rows], came.at[part]).wait()
        pltpu.make_async_copy(room.at[rows], out.at[rows], went.at[part]).start()
    for part in range(8):
        rows = pl.ds(part * 4, 4)
        pltpu.make_async_copy(room.at[rows], out.at[rows], went.at[part]).wait()


def pack(slots, blocks):
    shape = (REPLICAS, 4, SECTIONS, PIECE, HID)
    return call(
        pack_kernel,
        struct(shape, bf16),
        [SMEM, ANY],
        ANY,
        [
            pltpu.VMEM(shape, bf16),
            pltpu.SemaphoreType.DMA((8,)),
            pltpu.SemaphoreType.DMA((8,)),
        ],
    )(slots, blocks)


def pack_second_kernel(flag, slots, blocks, out_0, out_1, out_2, out_3, room, came, went):
    outs = (out_0, out_1, out_2, out_3)

    @pl.when(flag[0] == 1)
    def _():
        for s in range(SECTIONS):

            def start(r, carry):
                pltpu.make_async_copy(
                    blocks.at[slots[r * 4 + s]], room.at[s, r], came.at[s]
                ).start()
                return carry

            lax.fori_loop(0, REPLICAS, start, 0)
        for s in range(SECTIONS):
            pltpu.make_async_copy(room.at[s], room.at[s], came.at[s]).wait()
            pltpu.make_async_copy(room.at[s], outs[s], went.at[s]).start()
        for s in range(SECTIONS):
            pltpu.make_async_copy(room.at[s], outs[s], went.at[s]).wait()


def pack_second(flag, slots, blocks):
    return call(
        pack_second_kernel,
        [struct((REPLICAS, 4, PIECE, HID), bf16)] * 4,
        [SMEM, SMEM, ANY],
        [ANY] * 4,
        [
            pltpu.VMEM((SECTIONS, REPLICAS, 4, PIECE, HID), bf16),
            pltpu.SemaphoreType.DMA((4,)),
            pltpu.SemaphoreType.DMA((4,)),
        ],
    )(flag, slots, blocks)


def choose_kernel(which, in_0, in_1, in_2, in_3, out, room, sem):
    for k, ref in enumerate((in_0, in_1, in_2, in_3)):

        @pl.when(which[0] == k)
        def _():
            come = pltpu.make_async_copy(ref, room, sem.at[0])
            come.start()
            come.wait()
            go = pltpu.make_async_copy(room, out, sem.at[1])
            go.start()
            go.wait()


def choose(which, arrays):
    return call(
        choose_kernel,
        struct((REPLICAS, 4, PIECE, HID), bf16),
        [SMEM] + [ANY] * 4,
        ANY,
        [pltpu.VMEM((REPLICAS, 4, PIECE, HID), bf16), pltpu.SemaphoreType.DMA((2,))],
    )(which, *arrays)


def blank_kernel(flag, out):
    pass


def blank(flag):
    return call(blank_kernel, struct((DEVICES * 4, PIECE, HID), bf16), [SMEM], ANY)(flag)


def gather_kernel(places, first, relayed, second, out, sem):
    def start(b, carry):
        place = places[b]

        @pl.when(place < 512)
        def _():
            pltpu.make_async_copy(first.at[place], out.at[b], sem).start()

        @pl.when((place >= 512) & (place < 640))
        def _():
            pltpu.make_async_copy(relayed.at[place - 512], out.at[b], sem).start()

        @pl.when(place >= 640)
        def _():
            pltpu.make_async_copy(second.at[place - 640], out.at[b], sem).start()

        return carry

    lax.fori_loop(0, NBLK, start, 0)
    pltpu.make_async_copy(out, out, sem).wait()


def gather(places, first, relayed, second):
    return call(
        gather_kernel,
        struct((NBLK, PIECE, HID), bf16),
        [SMEM, ANY, ANY, ANY],
        ANY,
        [pltpu.SemaphoreType.DMA],
    )(places, first, relayed, second)


def send_tables(send_slot, send_dest, send_block):
    code = send_slot.reshape(1, -1) * 128 + send_block.reshape(1, -1)
    match = send_dest.reshape(1, -1) == jnp.arange(DEVICES, dtype=jnp.int32)[:, None]
    low = jnp.min(jnp.where(match, code, BIG), axis=1)
    high = jnp.max(jnp.where(match, code, -1), axis=1)
    first = jnp.where(low < BIG, low, -1)
    second = jnp.where(high > low, high, -1)
    return first, second


def route_blocks(old_blocks, send_slot, send_dest, send_block, moment_dest):
    me_r = lax.axis_index("replica")
    me_z = lax.axis_index("section")
    blocks = old_blocks.reshape(NBLK, 4, PIECE, HID)
    first, second = send_tables(send_slot, send_dest, send_block)
    has_second = jnp.any(second >= 0).astype(jnp.int32)
    first_slots = jnp.maximum(first, 0) // 128
    second_slots = jnp.maximum(second, 0) // 128

    def labels_of(codes):
        return jnp.where(codes >= 0, codes % 128 + 1, 0).reshape(REPLICAS, 1, SECTIONS)

    note = jnp.concatenate([has_second.reshape(1), moment_dest.reshape(-1), jnp.zeros((3,), jnp.int32)])
    labels = jnp.concatenate(
        [
            labels_of(first),
            labels_of(second),
            jnp.broadcast_to(note, (REPLICAS, 1, 8)),
        ],
        axis=2,
    )
    labels = jnp.broadcast_to(labels, (REPLICAS, 4, 16)).reshape(DEVICES, 16)

    got = lax.all_to_all(labels, EVERY, 0, 0, tiled=True)
    buffer = pack(first_slots, blocks).reshape(DEVICES, 4 * PIECE, HID)
    buffer, got, flag = lax.optimization_barrier((buffer, got, has_second.reshape(1)))
    parts = pack_second(flag, second_slots, blocks)
    relays = (parts[0], from_sibling(parts[1]), shift_xy(parts[2], 1, 0), shift_xy(parts[3], 0, 1))
    arrived = lax.all_to_all(buffer, EVERY, 0, 0, tiled=True).reshape(DEVICES * 4, PIECE, HID)

    holders = got[:, 8]
    alone = jnp.sum(holders) == 1
    numbers = jnp.arange(DEVICES, dtype=jnp.int32)
    busy = jnp.sum(jnp.where(holders > 0, numbers, 0))
    busy = jnp.where(alone, busy, 0)
    busy_r, busy_z = busy // 4, busy % 4
    busy_x, busy_y, busy_c = busy_r // 8, (busy_r // 2) % 4, busy_r % 2

    def relay(k):
        r = (
            busy_r,
            busy_r + 1 - 2 * busy_c,
            ((busy_x + 1) % 4) * 8 + busy_y * 2 + busy_c,
            busy_x * 8 + ((busy_y + 1) % 4) * 2 + busy_c,
        )[k]
        return r * 4 + busy_z

    me = me_r * 4 + me_z
    which = jnp.int32(0)
    for k in range(1, 4):
        which = jnp.where(relay(k) == me, k, which)
    relayed = choose(which.reshape(1).astype(jnp.int32), relays)
    relayed, arrived = lax.optimization_barrier((relayed, arrived))
    relayed = lax.all_to_all(
        relayed.reshape(DEVICES, PIECE, HID), EVERY, 0, 0, tiled=True
    )

    def second_round():
        again = pack(second_slots, blocks).reshape(DEVICES, 4 * PIECE, HID)
        return lax.all_to_all(again, EVERY, 0, 0, tiled=True).reshape(DEVICES * 4, PIECE, HID)

    spare = lax.cond(alone, lambda: blank(has_second.reshape(1)), second_round)

    wanted = jnp.arange(1, NBLK + 1, dtype=jnp.int32)[None, None, :]
    in_first = got[:, 0:4, None] == wanted
    in_second = got[:, 4:8, None] == wanted
    sections = jnp.arange(SECTIONS, dtype=jnp.int32)[None, :, None]
    flat = numbers[:, None, None] * 4 + sections
    via = jnp.stack([relay(k) for k in range(4)])[None, :, None] + 512
    later = jnp.where(alone, via, flat + 640)
    places = jnp.sum(jnp.where(in_first, flat, 0) + jnp.where(in_second, later, 0), axis=0)
    places = jnp.clip(places, 0, 1151)
    weights = [gather(places[s], arrived, relayed, spare) for s in range(SECTIONS)]
    return weights, got


def quarter_kernel(pick, acts, cots, acts_out, cots_out):
    chosen = pick[...]
    for j in range(GROUPS):
        wide = slice(j * 512, (j + 1) * 512)
        narrow = slice(j * 128, (j + 1) * 128)
        acts_out[:, narrow] = jnp.dot(
            acts[:, wide], chosen, preferred_element_type=f32
        ).astype(bf16)
        cots_out[:, narrow] = jnp.dot(
            cots[:, wide], chosen, preferred_element_type=f32
        ).astype(bf16)


def quarter(acts, cots, q):
    rows = jnp.arange(512, dtype=jnp.int32)[:, None]
    columns = jnp.arange(128, dtype=jnp.int32)[None, :]
    pick = (rows == (columns // 32) * 128 + q * 32 + columns % 32).astype(bf16)
    return call(
        quarter_kernel,
        [struct((TOK, LOCAL), bf16)] * 2,
        [VMEM] * 3,
        [VMEM] * 2,
    )(pick, acts, cots)


def up_of(weight):
    return weight[:HALF].reshape(LOCAL, HID)


def out_of(weight):
    return weight[HALF:].reshape(LOCAL, HID)


def put_forward(message, layer_in, up_matrix):
    wide = layer_in.astype(f32)
    squares = jnp.sum(wide * wide, axis=1, keepdims=True)
    high = squares.astype(bf16)
    low = (squares - high.astype(f32)).astype(bf16)
    lane = lax.broadcasted_iota(jnp.int32, (TOK, 128), 1)
    message[:, 0:HID] = jnp.dot(layer_in, up_matrix, preferred_element_type=f32).astype(bf16)
    message[:, HID : HID + 128] = jnp.where(
        lane == 0, high.astype(f32), jnp.where(lane == 1, low.astype(f32), 0.0)
    ).astype(bf16)


def take_forward(total):
    squares = total[:, HID : HID + 1] + total[:, HID + 1 : HID + 2]
    inverse = lax.rsqrt(squares * (1.0 / D) + rms_eps)
    pre = total[:, 0:HID] * inverse * SCALE_IN
    return pre, jax.nn.gelu(pre, approximate=True).astype(bf16), inverse


def gelu_slope(v):
    root = 0.7978845608028654
    t = jnp.tanh(root * (v + 0.044715 * v * v * v))
    return 0.5 * (1.0 + t) + 0.5 * v * (1.0 - t * t) * root * (1.0 + 0.134145 * v * v)


def times_t(a, b):
    return lax.dot_general(a, b, (((1,), (1,)), ((), ())), preferred_element_type=f32)


def summed(refs):
    return sum([ref[...].astype(f32) for ref in refs[1:]], refs[0][...].astype(f32))


def open_kernel(layer_in, weight, message):
    put_forward(message, layer_in[...], up_of(weight))


def forward_kernel(last, *refs):
    messages, refs = refs[:4], refs[4:]
    if last:
        layer_in, weight, weight_next, cots, pair, pre, inverse, layer_out, message = refs
    else:
        layer_in, weight, weight_next, pair, pre, inverse, layer_out, message = refs
    pre_value, act_value, inverse_value = take_forward(summed(messages))
    pair[:, 0:LOCAL] = layer_in[...]
    pair[:, LOCAL:] = act_value
    pre[...] = pre_value
    inverse[...] = jnp.broadcast_to(inverse_value, (TOK, 128))
    branch = times_t(act_value, out_of(weight))
    result = (layer_in[...].astype(f32) + branch * SCALE_OUT).astype(bf16)
    layer_out[...] = result
    put_forward(message, result, up_of(weight_next))
    if last:
        message[:, HID + 128 :] = jnp.dot(
            cots[...], out_of(weight_next), preferred_element_type=f32
        ).astype(bf16)


def backward_kernel(from_forward, *refs):
    messages, refs = refs[:4], refs[4:]
    total = summed(messages)
    if from_forward:
        grad_out, layer_in, weight, weight_next, pair, back, grad_in, message = refs
        pre_value, act_value, inverse_value = take_forward(total)
        pair[:, 0:LOCAL] = layer_in[...]
        pair[:, LOCAL:] = act_value
        grad_act = total[:, HID + 128 :] * SCALE_OUT
    else:
        pre, inverse, grad_out, layer_in, weight, weight_next, back, grad_in, message = refs
        pre_value = pre[...]
        inverse_value = inverse[:, 0:1]
        grad_act = total * SCALE_OUT
    pulled = (grad_act * gelu_slope(pre_value)).astype(bf16)
    back[:, 0:LOCAL] = grad_out[...]
    back[:, LOCAL:] = (pulled.astype(f32) * inverse_value).astype(bf16)
    correction = jnp.sum(pulled.astype(f32) * pre_value, axis=1, keepdims=True) * (1.0 / D)
    grad_norm = times_t(pulled, up_of(weight)) * SCALE_IN
    normed = layer_in[...].astype(f32) * inverse_value
    result = grad_out[...].astype(f32) + (grad_norm - normed * correction) * inverse_value
    result = result.astype(bf16)
    grad_in[...] = result
    message[...] = jnp.dot(result, out_of(weight_next), preferred_element_type=f32).astype(bf16)


def close_kernel(*refs):
    messages, (pre, inverse, grad_out, back) = refs[:4], refs[4:]
    grad_act = summed(messages) * SCALE_OUT
    pulled = (grad_act * gelu_slope(pre[...])).astype(bf16)
    back[:, 0:LOCAL] = grad_out[...]
    back[:, LOCAL:] = (pulled.astype(f32) * inverse[:, 0:1]).astype(bf16)


def all_of(message):
    return [message] + [shift_z(message, k) for k in (1, 3, 2)]


def gradient_kernel(x_first, place, pair, back, pair_sib, back_sib, *refs):
    outs, chosen, table = refs[:4], refs[4], refs[5]
    core = place[2]
    small = slice(LOCAL, LOCAL + HID)
    half = GROUPS // 2

    def product(left, left_sib, right, right_sib, scale, start):
        both = jnp.concatenate([left[:, small], left_sib[:, small]], axis=0)
        turned = both.astype(f32).T.astype(bf16)
        for g in range(half):
            columns = pl.ds(pl.multiple_of((2 * g + core) * 128, 128), 128)
            chosen[0:TOK, g * 128 : (g + 1) * 128] = right[:, columns]
            chosen[TOK:, g * 128 : (g + 1) * 128] = right_sib[:, columns]
        result = jnp.dot(turned, chosen[...], preferred_element_type=f32) * scale
        for g in range(half):
            table[start + g] = result[:, g * 128 : (g + 1) * 128].astype(bf16)

    product(back, back_sib, pair, pair_sib, SCALE_IN, 0)
    product(pair, pair_sib, back, back_sib, SCALE_OUT, half)
    table[2 * half] = jnp.zeros((HID, 128), bf16)
    table[2 * half + 1] = jnp.zeros((HID, 128), bf16)
    for k in range(4):
        for j in range(4):
            if x_first:
                owner = lax.rem(place[0] + k, 4) * 4 + j
            else:
                owner = j * 4 + lax.rem(place[1] + k, 4)
            outs[k][j] = table[owner]


def halve_kernel(x_first, count, place, *refs):
    mine = place[1] if x_first else place[0]
    outs = refs[4 * count :]
    for k in range(4):
        chunk = lax.rem(mine + k, 4)
        for n in range(count):
            four = refs[4 * n : 4 * n + 4]
            total = sum([ref[chunk].astype(f32) for ref in four[1:]], four[0][chunk].astype(f32))
            outs[k][n] = total.astype(outs[k].dtype)


def section_gradient(s, place, own, sib):
    x_first = s % 2 == 1
    chunks = call(
        functools.partial(gradient_kernel, x_first),
        [struct((4, HID, 128), bf16)] * 4,
        [SMEM] + [VMEM] * 4,
        [VMEM] * 4,
        [pltpu.VMEM((2 * TOK, LOCAL // 2), bf16), pltpu.VMEM((16, HID, 128), bf16)],
    )(place, *own, *sib)
    step = (1, 0) if x_first else (0, 1)
    moved = [shift_xy(chunks[k], k * step[0], k * step[1]) for k in (1, 2, 3)]
    return [chunks[0]] + moved, chunks[0]


def second_half(x_first, place, sections):
    count = len(sections)
    kept, *sends = call(
        functools.partial(halve_kernel, x_first, count),
        [struct((count, HID, 128), f32)] + [struct((count, HID, 128), bf16)] * 3,
        [SMEM] + [VMEM] * (4 * count),
        [VMEM] * 4,
    )(place, *[v for section in sections for v in section])
    step = (0, 1) if x_first else (1, 0)
    return [kept] + [shift_xy(sends[k - 1], k * step[0], k * step[1]) for k in (1, 2, 3)]


def finish_kernel(place, *refs):
    odd, even, refs = refs[:4], refs[4:8], refs[8:]
    kept, sends, table = refs[0], refs[1:4], refs[4]
    for n in range(2):
        table[2 * n + 1] = sum([ref[n].astype(f32) for ref in odd[1:]], odd[0][n])
        table[2 * n] = sum([ref[n].astype(f32) for ref in even[1:]], even[0][n])
    for k in range(4):
        value = table[lax.rem(place[3] + k, 4)]
        if k == 0:
            kept[...] = value
        else:
            sends[k - 1][...] = value.astype(bf16)


def split_moments_kernel(place, first, second, *outs):
    for k in range(4):
        rows = pl.ds(pl.multiple_of(lax.rem(place[3] + k, 4) * PIECE, PIECE), PIECE)
        for a in range(OWN):
            outs[k][0, a] = first[a, rows, :].astype(bf16)
            outs[k][1, a] = second[a, rows, :].astype(bf16)


def order_kernel(place, source, *refs):
    moments, outs, table = refs[:4], refs[4:8], refs[8]
    for k in range(4):
        table[k] = moments[k][...]
    for k in range(4):
        section = lax.rem(place[3] + k, 4)
        for i in range(OWN):
            held = source[section * OWN + i]
            outs[k][0, i] = table[held // OWN, 0, lax.rem(held, OWN)]
            outs[k][1, i] = table[held // OWN, 1, lax.rem(held, OWN)]


def owned_kernel(place, *refs):
    weights, outs = refs[:4], refs[4:8]
    start = jnp.minimum(place[4], REAL_OWNERS - 1) * OWN
    for k in range(4):
        section = lax.rem(place[3] + k, 4)
        for s in range(SECTIONS):

            @pl.when(section == s)
            def _():
                outs[k][...] = weights[s][pl.ds(start, OWN)]


def adam_kernel(place, *refs):
    gradients, held, weights = refs[:4], refs[4:8], refs[8:12]
    weight_out, first_out, second_out = refs[12:]
    real = place[4] < REAL_OWNERS
    for k in range(4):
        q = lax.rem(place[3] + 4 - k, 4)
        rows = pl.ds(pl.multiple_of(q * PIECE, PIECE), PIECE)
        turned = jnp.where(real, gradients[k][...].astype(f32).T, 0.0)
        for i in range(OWN):
            gradient = turned[i * PIECE : (i + 1) * PIECE, :]
            weight = jnp.where(real, weights[k][i].astype(f32), 0.0)
            first = beta_first * held[k][0, i].astype(f32) + (1.0 - beta_first) * gradient
            second = beta_second * held[k][1, i].astype(f32) + (
                (1.0 - beta_second) * gradient * gradient
            )
            first_out[i, rows, :] = first
            second_out[i, rows, :] = second
            weight_out[i, rows, :] = (
                weight - step_size * first / (jnp.sqrt(second) + adam_eps)
            ).astype(bf16)


def on_device(
    acts_in,
    cotangent,
    old_blocks,
    send_slot,
    send_dest,
    send_block,
    old_first,
    old_second,
    moment_dest,
):
    me_r = lax.axis_index("replica")
    me_z = lax.axis_index("section")
    place = jnp.stack([me_r // 8, (me_r // 2) % 4, me_r % 2, me_z, me_r]).astype(jnp.int32)

    split = call(
        split_moments_kernel,
        [struct((2, OWN, PIECE, HID), bf16)] * 4,
        [SMEM, VMEM, VMEM],
        [VMEM] * 4,
    )(place, old_first[0], old_second[0])
    pieces = [split[0]] + [shift_z(split[k], k) for k in (1, 2, 3)]

    weights, labels = route_blocks(old_blocks, send_slot, send_dest, send_block, moment_dest)
    table = lax.dynamic_slice_in_dim(labels, me_r * 4, 4, 0)[:, 9:13]
    distance = (me_z - jnp.arange(SECTIONS, dtype=jnp.int32)) % 4
    held = (distance[:, None] * OWN + jnp.arange(OWN, dtype=jnp.int32)[None, :]).reshape(-1)
    slots = jnp.arange(SECTIONS * OWN, dtype=jnp.int32)
    source = jnp.sum(jnp.where(table.reshape(1, -1) == slots[:, None], held[None, :], 0), axis=1)
    ordered = call(
        order_kernel,
        [struct((2, OWN, PIECE, HID), bf16)] * 4,
        [SMEM, SMEM] + [VMEM] * 4,
        [VMEM] * 4,
        [pltpu.VMEM((4, 2, OWN, PIECE, HID), bf16)],
    )(place, source, *pieces)
    moments = [ordered[0]] + [shift_z(ordered[k], k) for k in (1, 2, 3)]

    layer_0, cots = quarter(acts_in, cotangent, me_z)
    message = call(
        open_kernel, struct((TOK, HID + 128), bf16), [VMEM] * 2, VMEM, after=moments[1:]
    )(layer_0, weights[0])
    layers = [layer_0]
    pairs, pairs_sib, pres, inverses = [], [], [], []
    for s in range(SECTIONS - 1):
        last = s == SECTIONS - 2
        width = 2 * HID + 128 if last else HID + 128
        extra = (cots,) if last else ()
        pair, pre, inverse, layer, message = call(
            functools.partial(forward_kernel, last),
            [
                struct((TOK, LOCAL + HID), bf16),
                struct((TOK, HID), f32),
                struct((TOK, 128), f32),
                struct((TOK, LOCAL), bf16),
                struct((TOK, width), bf16),
            ],
            [VMEM] * (7 + len(extra)),
            [VMEM] * 5,
        )(*all_of(message), layers[s], weights[s], weights[s + 1], *extra)
        layers.append(layer)
        pairs.append(pair)
        pairs_sib.append(from_sibling(pair))
        pres.append(pre)
        inverses.append(inverse)

    owned = call(
        owned_kernel,
        [struct((OWN, PIECE, HID), bf16)] * 4,
        [SMEM] + [VMEM] * 4,
        [VMEM] * 4,
    )(place, *weights)
    owned = [owned[0]] + [shift_z(owned[k], k) for k in (1, 2, 3)]

    grad = cots
    done = []
    parts = [None] * SECTIONS
    for s in reversed(range(SECTIONS)):
        messages = all_of(message)
        wide = struct((TOK, LOCAL + HID), bf16)
        if s == 0:
            back = call(close_kernel, wide, [VMEM] * 7, VMEM, after=done)(
                *messages, pres[0], inverses[0], grad
            )
        elif s == SECTIONS - 1:
            pair, back, grad, message = call(
                functools.partial(backward_kernel, True),
                [wide, wide, struct((TOK, LOCAL), bf16), struct((TOK, HID), bf16)],
                [VMEM] * 8,
                [VMEM] * 4,
            )(*messages, grad, layers[s], weights[s], weights[s - 1])
            pairs.append(pair)
            pairs_sib.append(from_sibling(pair))
        else:
            back, grad, message = call(
                functools.partial(backward_kernel, False),
                [wide, struct((TOK, LOCAL), bf16), struct((TOK, HID), bf16)],
                [VMEM] * 10,
                [VMEM] * 3,
                after=done,
            )(*messages, pres[s], inverses[s], grad, layers[s], weights[s], weights[s - 1])
        own, sib = (pairs[s], back), (pairs_sib[s], from_sibling(back))
        parts[s], chunk = section_gradient(s, place, own, sib)
        done = [chunk]

    odd = second_half(True, place, [parts[1], parts[3]])
    even = second_half(False, place, [parts[0], parts[2]])
    kept, *sends = call(
        finish_kernel,
        [struct((HID, 128), f32)] + [struct((HID, 128), bf16)] * 3,
        [SMEM] + [VMEM] * 8,
        [VMEM] * 4,
        [pltpu.VMEM((SECTIONS, HID, 128), f32)],
    )(place, *odd, *even)
    gradients = [kept] + [shift_z(sends[k - 1], k) for k in (1, 2, 3)]
    new_weight, new_first, new_second = call(
        adam_kernel,
        [
            struct((OWN, 128, HID), bf16),
            struct((OWN, 128, HID), f32),
            struct((OWN, 128, HID), f32),
        ],
        [SMEM] + [VMEM] * 12,
        [VMEM] * 3,
    )(place, *gradients, *moments, *owned)
    return (new_weight[None], new_first[None], new_second[None])


def solution(mesh):
    in_specs = (
        P("replica", None),
        P("replica", None),
        P(("replica", "section"), None, None, None),
        P(("replica", "section"), None),
        P(("replica", "section"), None),
        P(("replica", "section"), None),
        P(("replica", "section"), None, None, None),
        P(("replica", "section"), None, None, None),
        P(("replica", "section"), None),
    )
    out_specs = (
        P("section", "replica", None, None),
        P("section", "replica", None, None),
        P("section", "replica", None, None),
    )
    return jax.shard_map(
        on_device, mesh=mesh, in_specs=in_specs, out_specs=out_specs, check_vma=False
    )
```

time: 703 us -> 375 us (0.53); the launches traced: 693 us -> 375 us
  waiting for transfers between devices: 450 us -> 185 us
  matrix products: 80.9 us -> 0 us
  starting transfers between devices: 52.5 us -> 123 us
  Pallas kernels: 0 us -> 39.3 us
  other arithmetic: 38.7 us -> 8.31 us
  local copies, waits for them, and re-layouts: 40.1 us -> 14.8 us
  blocking collectives: 15.8 us -> 0 us
  between operations: 14.9 us -> 3.37 us
    all_to_all x3, waiting for transfers between devices: 231 us -> 9.45 us  [the longest x1 8.65 us: route_blocks(): lax.all_to_all(relayed.reshape(DEVICES, PIECE, HID), EVERY, 0, 0, tiled=T...]
    psum x1 -> x0, waiting for transfers between devices: 104 us -> none  [on_device(): lax.psum(gradients.astype(jnp.bfloat16), 'replica').astype(jnp.float32)]
    dot_general x27 -> x0, matrix products: 80.9 us -> none  [the longest x4 26.6 us: section_forward(): lax.dot_general(activated, out_matrix, (((1,), (1,)), ((), ())), preferre...]
    ppermute x8 -> x62, waiting for transfers between devices: 115 us -> 176 us  [the longest x20 146 us: shift_xy(): return lax.ppermute(block, 'replica', route)]
    ppermute x8 -> x62, starting transfers between devices: 28.3 us -> 84.8 us  [the longest x33 42.3 us: shift_z(): lax.ppermute(block, 'section', [(i, (i + step) % 4) for i in range(4)])]
    pallas_call x0 -> x28, Pallas kernels: none -> 39.3 us  [call(): return lambda *arrays: run(*after, *arrays)]
    gather x6 -> x0, local copies, waits for them, and re-layouts: 29.7 us -> none  [the longest x2 14.4 us: route_blocks(): buffer = jnp.take(held, jnp.take(slots, chosen), axis=0)]
    select_n x14 -> x2, other arithmetic: 20.7 us -> 0.03 us  [the longest x1 0.02 us: labels_of(): jnp.where(codes >= 0, codes % 128 + 1, 0).reshape(REPLICAS, 1, SECTIONS)]
  transfers between devices with their start and end apart: 12 -> 65, of which waited for: 11 -> 29; matrix products, arithmetic and copies ran while one was open for 8% -> 3% of each run, Pallas kernels for 0% -> 9%
where the time goes in v1:
time: 375 us
  waiting for transfers between devices  185 us (49%)
  starting transfers between devices  123 us (33%)
  Pallas kernels  39.3 us (10%)
  local copies, waits for them, and re-layouts  14.8 us (4%)
  other arithmetic  8.31 us (2%)
    ppermute x20, waiting for transfers between devices, shift_xy(): return lax.ppermute(block, 'replica', route)  146 us
    ppermute x33, starting transfers between devices, shift_z(): lax.ppermute(block, 'section', [(i, (i + step) % 4) for i in range(4)])  42.3 us
    ppermute x20, starting transfers between devices, shift_xy(): return lax.ppermute(block, 'replica', route)  40.9 us
    pallas_call x28, Pallas kernels, call(): return lambda *arrays: run(*after, *arrays)  39.3 us
    ppermute x33, waiting for transfers between devices, shift_z(): lax.ppermute(block, 'section', [(i, (i + step) % 4) for i in range(4)])  30.3 us
    all_to_all x1, starting transfers between devices, route_blocks(): lax.all_to_all(relayed.reshape(DEVICES, PIECE, HID), EVERY, 0, 0, tiled=T...  14.6 us
    all_to_all x1, starting transfers between devices, route_blocks(): lax.all_to_all(buffer, EVERY, 0, 0, tiled=True)  13.4 us
    all_to_all x1, starting transfers between devices, route_blocks(): got = lax.all_to_all(labels, EVERY, 0, 0, tiled=True)  10.4 us
  transfers between devices with their start and end apart: 65, of which 29 were waited for; matrix products, arithmetic and copies ran while one was open for 3% of the time, Pallas kernels for 9%

profile of v1, /device:TPU:8, one launch (start us, length us, event | category | flops | bytes accessed | tf_op | source)
XLA Modules:
  0.0 374.6 jit_solution(12594545466353348214)
XLA Ops:
  5.2 10.4 %all-to-all-start.1 = ((s32[128,1,16]{2,1,0:T(1,128)}), s32[128,1,16]{2,1,0:T(1,128)S(1)}, u32[]{:S(2)}, u32[]{:S(2)}) async-start(s32[128,1,16]{2,1,0:T(1,128)} %bitcast.16), calls=%async_computation.1 | async-start | bytes 131072 | tf_op jit(solution)/shard_map/all_to_all | solution.py:250
  15.7 4.5 %shard_map.112 = bf16[32,4,4,32,256]{4,3,2,1,0:T(8,128)(2,1)S(1)} custom-call(s32[128]{0:T(128)S(1)} %get-tuple-element.182.refs_0_, bf16[112,4,32,256]{3,2,1,0:T(8,128)(2,1)} %bitcast.48), custom_call_target="tpu_custom_call" | custom-call | tf_op jit(solution)/shard_map/pallas_call | solution.py:61
  20.2 3.3 copy-done
  25.7 13.4 %all-to-all-start.2 = ((bf16[128,128,256]{2,1,0:T(8,128)(2,1)}), bf16[128,128,256]{2,1,0:T(8,128)(2,1)}, u32[]{:S(2)}, u32[]{:S(2)}) async-start(bf16[128,128,256]{2,1,0:T(8,128)(2,1)} %bitcast.40), calls=%async_computation.2 | async-start | bytes 16777216 | tf_op jit(solution)/shard_map/all_to_all | solution.py:255
  46.7 3.2 collective-permute-start.1
  53.0 126.1 %collective-permute-done.7.refs_3_ = bf16[32,4,32,256]{3,2,1,0:T(8,128)(2,1)} collective-permute-done((bf16[32,4,32,256]{3,2,1,0:T(8,128)(2,1)}, bf16[32,4,32,256]{3,2,1,0:T(8,128)(2,1)}, u32[]{:S(2)}, u32[]{:S(2)}) %collective-permute-start.7) | collective-permute-done | bytes 2097184 | tf_op jit(solution)/shard_map/ppermute | solution.py:75
  179.1 4.9 %collective-permute-done.8.refs_4_ = bf16[32,4,32,256]{3,2,1,0:T(8,128)(2,1)} collective-permute-done((bf16[32,4,32,256]{3,2,1,0:T(8,128)(2,1)}, bf16[32,4,32,256]{3,2,1,0:T(8,128)(2,1)}, u32[]{:S(2)}, u32[]{:S(2)}) %collective-permute-start.8) | collective-permute-done | bytes 2097184 | tf_op jit(solution)/shard_map/ppermute | solution.py:75
  185.6 14.6 %all-to-all-start.3 = ((bf16[128,32,256]{2,1,0:T(8,128)(2,1)}), bf16[128,32,256]{2,1,0:T(8,128)(2,1)S(1)}, u32[]{:S(2)}, u32[]{:S(2)}) async-start(bf16[128,32,256]{2,1,0:T(8,128)(2,1)} %bitcast.42), calls=%async_computation.3 | async-start | bytes 4194304 | tf_op jit(solution)/shard_map/all_to_all | solution.py:280
  216.6 3.2 collective-permute-start.4
  221.0 8.7 %all-to-all-done.3.refs_2_ = bf16[128,32,256]{2,1,0:T(8,128)(2,1)S(1)} async-done(((bf16[128,32,256]{2,1,0:T(8,128)(2,1)}), bf16[128,32,256]{2,1,0:T(8,128)(2,1)S(1)}, u32[]{:S(2)}, u32[]{:S(2)}) %all-to-all-start.3) | async-done | bytes 2097184 | tf_op jit(solution)/shard_map/all_to_all | solution.py:280
  229.7 3.4 shard_map.118.refs_4_.refs_5_.refs_10_.refs_1_
  234.1 2.4 collective-permute-start.11
  236.5 3.5 shard_map.120.refs_6_.refs_5_.refs_10_.refs_9_.refs_2_
  243.2 3.2 collective-permute-start.13
  246.5 3.5 shard_map.122.refs_6_.refs_5_.refs_7_.refs_9_.refs_3_
  250.1 2.5 collective-permute-done.14.refs_3_
  253.4 3.2 collective-permute-start.16
  256.7 3.5 shard_map.124.refs_6_.refs_4_
  260.2 3.0 collective-permute-done.17.refs_3_
  264.1 3.2 collective-permute-start.19
  267.4 3.8 %collective-permute-done.18.refs_1_ = bf16[128,640]{1,0:T(8,128)(2,1)S(1)} collective-permute-done((bf16[128,640]{1,0:T(8,128)(2,1)S(1)}, bf16[128,640]{1,0:T(8,128)(2,1)S(1)}, u32[]{:S(2)}, u32[]{:S(2)}) %collective-permute-start.18) | collective-permute-done | bytes 163872 | tf_op jit(solution)/shard_map/ppermute | solution.py:79
  275.7 3.2 collective-permute-start.24
  281.7 3.0 collective-permute-done.25.refs_4_
  285.7 3.2 collective-permute-start.29
  292.0 2.7 collective-permute-done.30.refs_4_
  296.1 3.2 collective-permute-start.43
  302.1 3.0 collective-permute-done.44.refs_4_
  311.6 4.2 %collective-permute-done.36.refs_6_ = bf16[4,256,128]{2,1,0:T(8,128)(2,1)S(1)} collective-permute-done((bf16[4,256,128]{2,1,0:T(8,128)(2,1)S(1)}, bf16[4,256,128]{2,1,0:T(8,128)(2,1)S(1)}, u32[]{:S(2)}, u32[]{:S(2)}) %collective-permute-start.36) | collective-permute-done | bytes 262176 | tf_op jit(solution)/shard_map/ppermute | solution.py:75
  315.7 5.6 %collective-permute-done.37.refs_7_ = bf16[4,256,128]{2,1,0:T(8,128)(2,1)S(1)} collective-permute-done((bf16[4,256,128]{2,1,0:T(8,128)(2,1)S(1)}, bf16[4,256,128]{2,1,0:T(8,128)(2,1)S(1)}, u32[]{:S(2)}, u32[]{:S(2)}) %collective-permute-start.37) | collective-permute-done | bytes 262176 | tf_op jit(solution)/shard_map/ppermute | solution.py:75
  332.1 7.1 %collective-permute-start.48 = (bf16[4,256,128]{2,1,0:T(8,128)(2,1)S(1)}, bf16[4,256,128]{2,1,0:T(8,128)(2,1)S(1)}, u32[]{:S(2)}, u32[]{:S(2)}) collective-permute-start(bf16[4,256,128]{2,1,0:T(8,128)(2,1)S(1)} %get-tuple-element.150), channel_id=1, source_target_pairs={{0,16},{4,20},{8,24},{12,28},{16,0},{20,4},{24,8},{28,12},{32,48},... | collective-permute-start | bytes 786440 | tf_op jit(solution)/shard_map/ppermute | solution.py:75
  344.4 10.9 %collective-permute-start.41 = (bf16[2,256,128]{2,1,0:T(8,128)(2,1)S(1)}, bf16[2,256,128]{2,1,0:T(8,128)(2,1)S(1)}, u32[]{:S(2)}, u32[]{:S(2)}) collective-permute-start(bf16[2,256,128]{2,1,0:T(8,128)(2,1)S(1)} %get-tuple-element.142), channel_id=1, source_target_pairs={{0,24},{4,28},{8,0},{12,4},{16,8},{20,12},{24,16},{28,20},{32,56},... | collective-permute-start | bytes 393224 | tf_op jit(solution)/shard_map/ppermute | solution.py:75
  357.2 2.3 collective-permute-start.55
  (187 shorter events, 95.1 us)
Async XLA Ops:
  5.2 19.1 %all-to-all-start.1 = ((s32[128,1,16]{2,1,0:T(1,128)}), s32[128,1,16]{2,1,0:T(1,128)S(1)}, u32[]{:S(2)}, u32[]{:S(2)}) async-start(s32[128,1,16]{2,1,0:T(1,128)} %bitcast.16), calls=%async_computation.1 | async-start | bytes 131072 | tf_op jit(solution)/shard_map/all_to_all | solution.py:250
  25.7 159.9 %all-to-all-start.2 = ((bf16[128,128,256]{2,1,0:T(8,128)(2,1)}), bf16[128,128,256]{2,1,0:T(8,128)(2,1)}, u32[]{:S(2)}, u32[]{:S(2)}) async-start(bf16[128,128,256]{2,1,0:T(8,128)(2,1)} %bitcast.40), calls=%async_computation.2 | async-start | bytes 16777216 | tf_op jit(solution)/shard_map/all_to_all | solution.py:255
  39.8 11.9 %collective-permute-start.6 = (bf16[32,4,32,256]{3,2,1,0:T(8,128)(2,1)}, bf16[32,4,32,256]{3,2,1,0:T(8,128)(2,1)}, u32[]{:S(2)}, u32[]{:S(2)}) collective-permute-start(bf16[32,4,32,256]{3,2,1,0:T(8,128)(2,1)} %get-tuple-element.103), channel_id=1, source_target_pairs={{0,4},{4,0},{8,12},{12,8},{16,20},{20,16},{24,28},{28,24},{32,36},... | collective-permute-start | bytes 6291464 | tf_op jit(solution)/shard_map/ppermute | solution.py:83
  40.0 139.1 %collective-permute-start.7 = (bf16[32,4,32,256]{3,2,1,0:T(8,128)(2,1)}, bf16[32,4,32,256]{3,2,1,0:T(8,128)(2,1)}, u32[]{:S(2)}, u32[]{:S(2)}) collective-permute-start(bf16[32,4,32,256]{3,2,1,0:T(8,128)(2,1)} %get-tuple-element.104), channel_id=1, source_target_pairs={{0,32},{4,36},{8,40},{12,44},{16,48},{20,52},{24,56},{28,60},{32,6... | collective-permute-start | bytes 6291464 | tf_op jit(solution)/shard_map/ppermute | solution.py:75
  41.5 142.5 %collective-permute-start.8 = (bf16[32,4,32,256]{3,2,1,0:T(8,128)(2,1)}, bf16[32,4,32,256]{3,2,1,0:T(8,128)(2,1)}, u32[]{:S(2)}, u32[]{:S(2)}) collective-permute-start(bf16[32,4,32,256]{3,2,1,0:T(8,128)(2,1)} %get-tuple-element.105), channel_id=1, source_target_pairs={{0,8},{4,12},{8,16},{12,20},{16,24},{20,28},{24,0},{28,4},{32,40},... | collective-permute-start | bytes 6291464 | tf_op jit(solution)/shard_map/ppermute | solution.py:75
  45.0 167.9 %collective-permute-start = (bf16[2,4,32,256]{3,2,1,0:T(8,128)(2,1)}, bf16[2,4,32,256]{3,2,1,0:T(8,128)(2,1)S(1)}, u32[]{:S(2)}, u32[]{:S(2)}) collective-permute-start(bf16[2,4,32,256]{3,2,1,0:T(8,128)(2,1)} %get-tuple-element.94), channel_id=1, source_target_pairs={{0,1},{1,2},{2,3},{3,0},{4,5},{5,6},{6,7},{7,4},{8,9},{9,10},{10,1... | collective-permute-start | bytes 393224 | tf_op jit(solution)/shard_map/ppermute | solution.py:79
  46.7 166.2 %collective-permute-start.1 = (bf16[2,4,32,256]{3,2,1,0:T(8,128)(2,1)}, bf16[2,4,32,256]{3,2,1,0:T(8,128)(2,1)S(1)}, u32[]{:S(2)}, u32[]{:S(2)}) collective-permute-start(bf16[2,4,32,256]{3,2,1,0:T(8,128)(2,1)} %get-tuple-element.95), channel_id=1, source_target_pairs={{0,2},{1,3},{2,0},{3,1},{4,6},{5,7},{6,4},{7,5},{8,10},{9,11},{10,... | collective-permute-start | bytes 393224 | tf_op jit(solution)/shard_map/ppermute | solution.py:79
  51.7 161.3 %collective-permute-start.2 = (bf16[2,4,32,256]{3,2,1,0:T(8,128)(2,1)}, bf16[2,4,32,256]{3,2,1,0:T(8,128)(2,1)S(1)}, u32[]{:S(2)}, u32[]{:S(2)}) collective-permute-start(bf16[2,4,32,256]{3,2,1,0:T(8,128)(2,1)} %copy-done.8), channel_id=1, source_target_pairs={{0,3},{1,0},{2,1},{3,2},{4,7},{5,4},{6,5},{7,6},{8,11},{9,8},{10,9... | collective-permute-start | bytes 393224 | tf_op jit(solution)/shard_map/ppermute | solution.py:79
  185.6 44.1 %all-to-all-start.3 = ((bf16[128,32,256]{2,1,0:T(8,128)(2,1)}), bf16[128,32,256]{2,1,0:T(8,128)(2,1)S(1)}, u32[]{:S(2)}, u32[]{:S(2)}) async-start(bf16[128,32,256]{2,1,0:T(8,128)(2,1)} %bitcast.42), calls=%async_computation.3 | async-start | bytes 4194304 | tf_op jit(solution)/shard_map/all_to_all | solution.py:280
  215.0 18.1 %collective-permute-start.3 = (bf16[2,4,32,256]{3,2,1,0:T(8,128)(2,1)}, bf16[2,4,32,256]{3,2,1,0:T(8,128)(2,1)S(1)}, u32[]{:S(2)}, u32[]{:S(2)}) collective-permute-start(bf16[2,4,32,256]{3,2,1,0:T(8,128)(2,1)} %get-tuple-element.97), channel_id=1, source_target_pairs={{0,1},{1,2},{2,3},{3,0},{4,5},{5,6},{6,7},{7,4},{8,9},{9,10},{10,1... | collective-permute-start | bytes 393224 | tf_op jit(solution)/shard_map/ppermute | solution.py:79
  216.6 16.5 %collective-permute-start.4 = (bf16[2,4,32,256]{3,2,1,0:T(8,128)(2,1)}, bf16[2,4,32,256]{3,2,1,0:T(8,128)(2,1)S(1)}, u32[]{:S(2)}, u32[]{:S(2)}) collective-permute-start(bf16[2,4,32,256]{3,2,1,0:T(8,128)(2,1)} %get-tuple-element.98), channel_id=1, source_target_pairs={{0,2},{1,3},{2,0},{3,1},{4,6},{5,7},{6,4},{7,5},{8,10},{9,11},{10,... | collective-permute-start | bytes 393224 | tf_op jit(solution)/shard_map/ppermute | solution.py:79
  219.8 13.3 %collective-permute-start.5 = (bf16[2,4,32,256]{3,2,1,0:T(8,128)(2,1)}, bf16[2,4,32,256]{3,2,1,0:T(8,128)(2,1)S(1)}, u32[]{:S(2)}, u32[]{:S(2)}) collective-permute-start(bf16[2,4,32,256]{3,2,1,0:T(8,128)(2,1)} %get-tuple-element.99), channel_id=1, source_target_pairs={{0,3},{1,0},{2,1},{3,2},{4,7},{5,4},{6,5},{7,6},{8,11},{9,8},{10,9... | collective-permute-start | bytes 393224 | tf_op jit(solution)/shard_map/ppermute | solution.py:79
  278.9 10.0 %collective-permute-start.26 = (bf16[128,2048]{1,0:T(8,128)(2,1)S(1)}, bf16[128,2048]{1,0:T(8,128)(2,1)S(1)}, u32[]{:S(2)}, u32[]{:S(2)}) collective-permute-start(bf16[128,2048]{1,0:T(8,128)(2,1)S(1)} %get-tuple-element.115.refs_1_), channel_id=1, source_target_pairs={{0,4},{4,0},{8,12},{12,8},{16,20},{20,16},{24,28},{28,24},{32,36},... | collective-permute-start | bytes 1572872 | tf_op jit(solution)/shard_map/ppermute | solution.py:83
  288.9 10.4 %collective-permute-start.31 = (bf16[128,2048]{1,0:T(8,128)(2,1)S(1)}, bf16[128,2048]{1,0:T(8,128)(2,1)S(1)}, u32[]{:S(2)}, u32[]{:S(2)}) collective-permute-start(bf16[128,2048]{1,0:T(8,128)(2,1)S(1)} %get-tuple-element.111.refs_1_), channel_id=1, source_target_pairs={{0,4},{4,0},{8,12},{12,8},{16,20},{20,16},{24,28},{28,24},{32,36},... | collective-permute-start | bytes 1572872 | tf_op jit(solution)/shard_map/ppermute | solution.py:83
  295.6 14.4 %collective-permute-start.45 = (bf16[128,2048]{1,0:T(8,128)(2,1)S(1)}, bf16[128,2048]{1,0:T(8,128)(2,1)S(1)}, u32[]{:S(2)}, u32[]{:S(2)}) collective-permute-start(bf16[128,2048]{1,0:T(8,128)(2,1)S(1)} %get-tuple-element.143.refs_1_), channel_id=1, source_target_pairs={{0,4},{4,0},{8,12},{12,8},{16,20},{20,16},{24,28},{28,24},{32,36},... | collective-permute-start | bytes 1572872 | tf_op jit(solution)/shard_map/ppermute | solution.py:83
  305.2 21.1 %collective-permute-start.46 = (bf16[128,2048]{1,0:T(8,128)(2,1)S(1)}, bf16[128,2048]{1,0:T(8,128)(2,1)S(1)}, u32[]{:S(2)}, u32[]{:S(2)}) collective-permute-start(bf16[128,2048]{1,0:T(8,128)(2,1)S(1)} %shard_map.133.refs_2_), channel_id=1, source_target_pairs={{0,4},{4,0},{8,12},{12,8},{16,20},{20,16},{24,28},{28,24},{32,36},... | collective-permute-start | bytes 1572872 | tf_op jit(solution)/shard_map/ppermute | solution.py:83
  305.3 10.4 %collective-permute-start.36 = (bf16[4,256,128]{2,1,0:T(8,128)(2,1)S(1)}, bf16[4,256,128]{2,1,0:T(8,128)(2,1)S(1)}, u32[]{:S(2)}, u32[]{:S(2)}) collective-permute-start(bf16[4,256,128]{2,1,0:T(8,128)(2,1)S(1)} %get-tuple-element.136), channel_id=1, source_target_pairs={{0,32},{4,36},{8,40},{12,44},{16,48},{20,52},{24,56},{28,60},{32,6... | collective-permute-start | bytes 786440 | tf_op jit(solution)/shard_map/ppermute | solution.py:75
  306.4 15.0 %collective-permute-start.37 = (bf16[4,256,128]{2,1,0:T(8,128)(2,1)S(1)}, bf16[4,256,128]{2,1,0:T(8,128)(2,1)S(1)}, u32[]{:S(2)}, u32[]{:S(2)}) collective-permute-start(bf16[4,256,128]{2,1,0:T(8,128)(2,1)S(1)} %get-tuple-element.137), channel_id=1, source_target_pairs={{0,64},{4,68},{8,72},{12,76},{16,80},{20,84},{24,88},{28,92},{32,9... | collective-permute-start | bytes 786440 | tf_op jit(solution)/shard_map/ppermute | solution.py:75
  308.6 14.0 %collective-permute-start.38 = (bf16[4,256,128]{2,1,0:T(8,128)(2,1)S(1)}, bf16[4,256,128]{2,1,0:T(8,128)(2,1)S(1)}, u32[]{:S(2)}, u32[]{:S(2)}) collective-permute-start(bf16[4,256,128]{2,1,0:T(8,128)(2,1)S(1)} %get-tuple-element.138), channel_id=1, source_target_pairs={{0,96},{4,100},{8,104},{12,108},{16,112},{20,116},{24,120},{28,124... | collective-permute-start | bytes 786440 | tf_op jit(solution)/shard_map/ppermute | solution.py:75
  310.0 14.9 %collective-permute-start.50 = (bf16[4,256,128]{2,1,0:T(8,128)(2,1)S(1)}, bf16[4,256,128]{2,1,0:T(8,128)(2,1)S(1)}, u32[]{:S(2)}, u32[]{:S(2)}) collective-permute-start(bf16[4,256,128]{2,1,0:T(8,128)(2,1)S(1)} %get-tuple-element.152), channel_id=1, source_target_pairs={{0,8},{4,12},{8,16},{12,20},{16,24},{20,28},{24,0},{28,4},{32,40},... | collective-permute-start | bytes 786440 | tf_op jit(solution)/shard_map/ppermute | solution.py:75
  315.7 13.5 %collective-permute-start.33 = (bf16[4,256,128]{2,1,0:T(8,128)(2,1)S(1)}, bf16[4,256,128]{2,1,0:T(8,128)(2,1)S(1)}, u32[]{:S(2)}, u32[]{:S(2)}) collective-permute-start(bf16[4,256,128]{2,1,0:T(8,128)(2,1)S(1)} %get-tuple-element.133), channel_id=1, source_target_pairs={{0,32},{4,36},{8,40},{12,44},{16,48},{20,52},{24,56},{28,60},{32,6... | collective-permute-start | bytes 786440 | tf_op jit(solution)/shard_map/ppermute | solution.py:75
  321.4 10.8 %collective-permute-start.34 = (bf16[4,256,128]{2,1,0:T(8,128)(2,1)S(1)}, bf16[4,256,128]{2,1,0:T(8,128)(2,1)S(1)}, u32[]{:S(2)}, u32[]{:S(2)}) collective-permute-start(bf16[4,256,128]{2,1,0:T(8,128)(2,1)S(1)} %get-tuple-element.134), channel_id=1, source_target_pairs={{0,64},{4,68},{8,72},{12,76},{16,80},{20,84},{24,88},{28,92},{32,9... | collective-permute-start | bytes 786440 | tf_op jit(solution)/shard_map/ppermute | solution.py:75
  322.7 16.6 %collective-permute-start.35 = (bf16[4,256,128]{2,1,0:T(8,128)(2,1)S(1)}, bf16[4,256,128]{2,1,0:T(8,128)(2,1)S(1)}, u32[]{:S(2)}, u32[]{:S(2)}) collective-permute-start(bf16[4,256,128]{2,1,0:T(8,128)(2,1)S(1)} %get-tuple-element.135), channel_id=1, source_target_pairs={{0,96},{4,100},{8,104},{12,108},{16,112},{20,116},{24,120},{28,124... | collective-permute-start | bytes 786440 | tf_op jit(solution)/shard_map/ppermute | solution.py:75
  324.9 15.2 %collective-permute-start.51 = (bf16[4,256,128]{2,1,0:T(8,128)(2,1)S(1)}, bf16[4,256,128]{2,1,0:T(8,128)(2,1)S(1)}, u32[]{:S(2)}, u32[]{:S(2)}) collective-permute-start(bf16[4,256,128]{2,1,0:T(8,128)(2,1)S(1)} %get-tuple-element.153), channel_id=1, source_target_pairs={{0,16},{4,20},{8,24},{12,28},{16,0},{20,4},{24,8},{28,12},{32,48},... | collective-permute-start | bytes 786440 | tf_op jit(solution)/shard_map/ppermute | solution.py:75
  326.3 15.9 %collective-permute-start.52 = (bf16[4,256,128]{2,1,0:T(8,128)(2,1)S(1)}, bf16[4,256,128]{2,1,0:T(8,128)(2,1)S(1)}, u32[]{:S(2)}, u32[]{:S(2)}) collective-permute-start(bf16[4,256,128]{2,1,0:T(8,128)(2,1)S(1)} %get-tuple-element.154), channel_id=1, source_target_pairs={{0,24},{4,28},{8,0},{12,4},{16,8},{20,12},{24,16},{28,20},{32,56},... | collective-permute-start | bytes 786440 | tf_op jit(solution)/shard_map/ppermute | solution.py:75
  329.2 15.2 %collective-permute-start.47 = (bf16[4,256,128]{2,1,0:T(8,128)(2,1)S(1)}, bf16[4,256,128]{2,1,0:T(8,128)(2,1)S(1)}, u32[]{:S(2)}, u32[]{:S(2)}) collective-permute-start(bf16[4,256,128]{2,1,0:T(8,128)(2,1)S(1)} %get-tuple-element.149), channel_id=1, source_target_pairs={{0,8},{4,12},{8,16},{12,20},{16,24},{20,28},{24,0},{28,4},{32,40},... | collective-permute-start | bytes 786440 | tf_op jit(solution)/shard_map/ppermute | solution.py:75
  332.1 23.2 %collective-permute-start.48 = (bf16[4,256,128]{2,1,0:T(8,128)(2,1)S(1)}, bf16[4,256,128]{2,1,0:T(8,128)(2,1)S(1)}, u32[]{:S(2)}, u32[]{:S(2)}) collective-permute-start(bf16[4,256,128]{2,1,0:T(8,128)(2,1)S(1)} %get-tuple-element.150), channel_id=1, source_target_pairs={{0,16},{4,20},{8,24},{12,28},{16,0},{20,4},{24,8},{28,12},{32,48},... | collective-permute-start | bytes 786440 | tf_op jit(solution)/shard_map/ppermute | solution.py:75
  339.3 16.0 %collective-permute-start.49 = (bf16[4,256,128]{2,1,0:T(8,128)(2,1)S(1)}, bf16[4,256,128]{2,1,0:T(8,128)(2,1)S(1)}, u32[]{:S(2)}, u32[]{:S(2)}) collective-permute-start(bf16[4,256,128]{2,1,0:T(8,128)(2,1)S(1)} %get-tuple-element.151), channel_id=1, source_target_pairs={{0,24},{4,28},{8,0},{12,4},{16,8},{20,12},{24,16},{28,20},{32,56},... | collective-permute-start | bytes 786440 | tf_op jit(solution)/shard_map/ppermute | solution.py:75
  340.1 17.1 %collective-permute-start.39 = (bf16[2,256,128]{2,1,0:T(8,128)(2,1)S(1)}, bf16[2,256,128]{2,1,0:T(8,128)(2,1)S(1)}, u32[]{:S(2)}, u32[]{:S(2)}) collective-permute-start(bf16[2,256,128]{2,1,0:T(8,128)(2,1)S(1)} %get-tuple-element.140), channel_id=1, source_target_pairs={{0,8},{4,12},{8,16},{12,20},{16,24},{20,28},{24,0},{28,4},{32,40},... | collective-permute-start | bytes 393224 | tf_op jit(solution)/shard_map/ppermute | solution.py:75
  342.2 18.0 %collective-permute-start.40 = (bf16[2,256,128]{2,1,0:T(8,128)(2,1)S(1)}, bf16[2,256,128]{2,1,0:T(8,128)(2,1)S(1)}, u32[]{:S(2)}, u32[]{:S(2)}) collective-permute-start(bf16[2,256,128]{2,1,0:T(8,128)(2,1)S(1)} %get-tuple-element.141), channel_id=1, source_target_pairs={{0,16},{4,20},{8,24},{12,28},{16,0},{20,4},{24,8},{28,12},{32,48},... | collective-permute-start | bytes 393224 | tf_op jit(solution)/shard_map/ppermute | solution.py:75
  344.4 15.8 %collective-permute-start.41 = (bf16[2,256,128]{2,1,0:T(8,128)(2,1)S(1)}, bf16[2,256,128]{2,1,0:T(8,128)(2,1)S(1)}, u32[]{:S(2)}, u32[]{:S(2)}) collective-permute-start(bf16[2,256,128]{2,1,0:T(8,128)(2,1)S(1)} %get-tuple-element.142), channel_id=1, source_target_pairs={{0,24},{4,28},{8,0},{12,4},{16,8},{20,12},{24,16},{28,20},{32,56},... | collective-permute-start | bytes 393224 | tf_op jit(solution)/shard_map/ppermute | solution.py:75
  360.3 9.6 %collective-permute-start.60 = (bf16[4,32,256]{2,1,0:T(8,128)(2,1)S(1)}, bf16[4,32,256]{2,1,0:T(8,128)(2,1)S(1)}, u32[]{:S(2)}, u32[]{:S(2)}) collective-permute-start(bf16[4,32,256]{2,1,0:T(8,128)(2,1)S(1)} %get-tuple-element.166), channel_id=1, source_target_pairs={{0,2},{1,3},{2,0},{3,1},{4,6},{5,7},{6,4},{7,5},{8,10},{9,11},{10,... | collective-permute-start | bytes 196616 | tf_op jit(solution)/shard_map/ppermute | solution.py:79
  (45 other events, 272.8 us)

commit v2 on v1

v2 whole, which is shorter than its diff:
```python
import functools

import jax
import jax.numpy as jnp
from jax import lax
from jax.experimental import pallas as pl
from jax.experimental.pallas import tpu as pltpu
from jax.sharding import PartitionSpec as P


D = 7168
HID = 256
TOK = 128
NBLK = 112
HALF = 56
PIECE = 32
LOCAL = HALF * PIECE
GROUPS = LOCAL // 128
SECTIONS = 4
REPLICAS = 32
DEVICES = 128
OWN = 4
REAL_OWNERS = NBLK // OWN
BIG = 1 << 20
CHUNK = SECTIONS * PIECE + 16
EVERY = ("replica", "section")

rms_eps = 1e-05
beta_first = 0.9
beta_second = 0.95
step_size = 0.1
adam_eps = 1e-08
SCALE_IN = D ** (-0.5)
SCALE_OUT = HID ** (-0.5)

f32 = jnp.float32
bf16 = jnp.bfloat16
ANY = pl.BlockSpec(memory_space=pl.ANY)
HBM = pl.BlockSpec(memory_space=pltpu.HBM)
SMEM = pl.BlockSpec(memory_space=pltpu.SMEM)
VMEM = pl.BlockSpec(memory_space=pltpu.VMEM)
LIMIT = 12 * 1024 * 1024
BULK = 62 * 1024 * 1024


def struct(shape, dtype):
    return jax.ShapeDtypeStruct(shape, dtype)


def call(kernel, out_shape, in_specs, out_specs, scratch=(), after=(), aliases=None, limit=LIMIT):
    waits = len(after)

    def body(*refs):
        kernel(*refs[waits:])

    run = pl.pallas_call(
        body,
        out_shape=out_shape,
        in_specs=[ANY] * waits + in_specs,
        out_specs=out_specs,
        scratch_shapes=list(scratch),
        input_output_aliases={waits + i: o for i, o in (aliases or {}).items()},
        compiler_params=pltpu.CompilerParams(vmem_limit_bytes=limit),
    )
    return lambda *arrays: run(*after, *arrays)


def replica_at(x, y, core):
    return ((x % 4) * 4 + (y % 4)) * 2 + core


def shift_xy(block, step_x, step_y):
    route = [
        (replica_at(x, y, c), replica_at(x + step_x, y + step_y, c))
        for x in range(4)
        for y in range(4)
        for c in range(2)
    ]
    return lax.ppermute(block, "replica", route)


def shift_z(block, step):
    return lax.ppermute(block, "section", [(i, (i + step) % 4) for i in range(4)])


def spread(block, axis):
    if axis == "z":
        names = ("replica", "section")
        route = []
        for r in range(REPLICAS):
            step = 1 - 2 * (r % 2)
            route += [(r * 4 + i, r * 4 + (i + step) % 4) for i in range(4)]
        return lax.ppermute(block, names, route)
    route = []
    for x in range(4):
        for y in range(4):
            for c in range(2):
                step = 1 - 2 * c
                to = (x + step, y) if axis == "x" else (x, y + step)
                route.append((replica_at(x, y, c), replica_at(*to, c)))
    return lax.ppermute(block, "replica", route)


def from_sibling(block):
    return lax.ppermute(block, "replica", [(i, i ^ 1) for i in range(REPLICAS)])


def pack_kernel(slots, blocks, out, room, came, went):
    for part in range(8):
        for s in range(SECTIONS):

            def start(i, carry):
                r = part * 4 + i
                pltpu.make_async_copy(
                    blocks.at[slots[r * 4 + s]],
                    room.at[r, :, pl.ds(s * PIECE, PIECE)],
                    came.at[part],
                ).start()
                return carry

            lax.fori_loop(0, 4, start, 0)

    def go(part):
        rows = pl.ds(part * 4, 4)
        into = out.at[rows, :, pl.ds(0, SECTIONS * PIECE)]
        return pltpu.make_async_copy(room.at[rows], into, went.at[part])

    for part in range(8):
        rows = pl.ds(part * 4, 4)
        pltpu.make_async_copy(room.at[rows], room.at[rows], came.at[part]).wait()
        go(part).start()
    for part in range(8):
        go(part).wait()


def pack(slots, blocks, tall, after=()):
    return call(
        pack_kernel,
        struct((REPLICAS, 4, tall, HID), bf16),
        [SMEM, ANY],
        HBM,
        [
            pltpu.VMEM((REPLICAS, 4, SECTIONS * PIECE, HID), bf16),
            pltpu.SemaphoreType.DMA((8,)),
            pltpu.SemaphoreType.DMA((8,)),
        ],
        after=after,
        limit=BULK,
    )(slots, blocks)


def pack_second_kernel(flag, slots, blocks, *refs):
    outs, (room, came, went) = refs[:5], refs[5:]

    @pl.when(flag[0] == 1)
    def _():
        for s in range(SECTIONS):

            def start(r, carry):
                pltpu.make_async_copy(
                    blocks.at[slots[r * 4 + s]], room.at[s, r], came.at[s]
                ).start()
                return carry

            lax.fori_loop(0, REPLICAS, start, 0)

        def go(s, h):
            rows = room.at[s, :, :, pl.ds(h * 16, 16)]
            return pltpu.make_async_copy(
                rows, outs[4].at[s] if h else outs[s], went.at[s + 4 * h]
            )

        for s in range(SECTIONS):
            pltpu.make_async_copy(room.at[s], room.at[s], came.at[s]).wait()
            go(s, 1).start()
            go(s, 0).start()
        for s in range(SECTIONS):
            go(s, 1).wait()
            go(s, 0).wait()


def pack_second(flag, slots, blocks):
    return call(
        pack_second_kernel,
        [struct((REPLICAS, 4, 16, HID), bf16)] * 4
        + [struct((SECTIONS, REPLICAS, 4, 16, HID), bf16)],
        [SMEM, SMEM, ANY],
        [HBM] * 5,
        [
            pltpu.VMEM((SECTIONS, REPLICAS, 4, PIECE, HID), bf16),
            pltpu.SemaphoreType.DMA((4,)),
            pltpu.SemaphoreType.DMA((8,)),
        ],
        limit=BULK,
    )(flag, slots, blocks)


def take_over_kernel(flag, got, in_0, in_1, in_2, in_3, out_0, out_1, out_2, out_3, room, came, went):
    outs = (out_0, out_1, out_2, out_3)

    @pl.when(flag[0] == 1)
    def _():
        def come(s):
            return pltpu.make_async_copy(got.at[s], room.at[s], came.at[s])

        def go(s):
            return pltpu.make_async_copy(room.at[s], outs[s], went.at[s])

        for s in range(SECTIONS):
            come(s).start()
        for s in range(SECTIONS):
            come(s).wait()
            go(s).start()
        for s in range(SECTIONS):
            go(s).wait()


def take_over(flag, got, own, after):
    return call(
        take_over_kernel,
        [struct((REPLICAS, 4, 16, HID), bf16)] * 4,
        [SMEM] + [HBM] * 5,
        [HBM] * 4,
        [
            pltpu.VMEM((SECTIONS, REPLICAS, 4, 16, HID), bf16),
            pltpu.SemaphoreType.DMA((4,)),
            pltpu.SemaphoreType.DMA((4,)),
        ],
        after=after,
        aliases={2: 0, 3: 1, 4: 2, 5: 3},
        limit=BULK,
    )(flag, got, *own)


def add_relayed_kernel(which, in_0, in_1, in_2, in_3, buffer, out, room, sem):
    for k, ref in enumerate((in_0, in_1, in_2, in_3)):

        @pl.when(which[0] == k)
        def _():
            come = pltpu.make_async_copy(ref, room, sem.at[0])
            come.start()
            come.wait()
            go = pltpu.make_async_copy(room, out.at[:, :, pl.ds(SECTIONS * PIECE, 16)], sem.at[1])
            go.start()
            go.wait()


def add_relayed(which, relays, buffer):
    return call(
        add_relayed_kernel,
        struct((REPLICAS, 4, CHUNK, HID), bf16),
        [SMEM] + [HBM] * 5,
        HBM,
        [pltpu.VMEM((REPLICAS, 4, 16, HID), bf16), pltpu.SemaphoreType.DMA((2,))],
        aliases={5: 0},
        limit=BULK,
    )(which, *relays, buffer)


def blank_kernel(flag, out):
    pass


def blank(flag):
    return call(blank_kernel, struct((DEVICES, SECTIONS * PIECE, HID), bf16), [SMEM], HBM)(flag)


def fetch(section, place, relays, first, second, out, sem):
    rows = section * PIECE
    if not isinstance(section, int):
        rows = pl.multiple_of(rows, PIECE)
    rows = pl.ds(rows, PIECE)
    extra = pl.ds(SECTIONS * PIECE, 16)

    @pl.when(place < DEVICES)
    def _():
        pltpu.make_async_copy(first.at[place, rows], out, sem).start()

    @pl.when(place >= DEVICES)
    def _():
        @pl.when(place < 2 * DEVICES)
        def _():
            pltpu.make_async_copy(second.at[place - DEVICES, rows], out, sem).start()

        @pl.when(place == 2 * DEVICES)
        def _():
            low, high = relays[section], relays[section + 4]
            pltpu.make_async_copy(first.at[low, extra], out.at[pl.ds(0, 16)], sem).start()
            pltpu.make_async_copy(first.at[high, extra], out.at[pl.ds(16, 16)], sem).start()


def gather_kernel(section, begin, places, relays, first, second, out, sem):
    def start(b, carry):
        fetch(section, places[begin + b], relays, first, second, out.at[b], sem)
        return carry

    lax.fori_loop(0, HALF, start, 0, unroll=8)
    pltpu.make_async_copy(out, out, sem).wait()


def gather(section, begin, places, relays, first, second):
    return call(
        functools.partial(gather_kernel, section, begin),
        struct((HALF, PIECE, HID), bf16),
        [SMEM, SMEM, ANY, ANY],
        ANY,
        [pltpu.SemaphoreType.DMA],
    )(places, relays, first, second)


def send_tables(send_slot, send_dest, send_block):
    code = send_slot.reshape(1, -1) * 128 + send_block.reshape(1, -1)
    match = send_dest.reshape(1, -1) == jnp.arange(DEVICES, dtype=jnp.int32)[:, None]
    low = jnp.min(jnp.where(match, code, BIG), axis=1)
    high = jnp.max(jnp.where(match, code, -1), axis=1)
    first = jnp.where(low < BIG, low, -1)
    second = jnp.where(high > low, high, -1)
    return first, second


def route_blocks(old_blocks, send_slot, send_dest, send_block, moment_dest):
    me_r = lax.axis_index("replica")
    me_z = lax.axis_index("section")
    blocks = old_blocks.reshape(NBLK, 4, PIECE, HID)
    first, second = send_tables(send_slot, send_dest, send_block)
    has_second = jnp.any(second >= 0).astype(jnp.int32)
    spread_out = jnp.arange(DEVICES, dtype=jnp.int32) % NBLK
    first_slots = jnp.where(first >= 0, first // 128, spread_out)
    second_slots = jnp.where(second >= 0, second // 128, spread_out)

    def labels_of(codes):
        return jnp.where(codes >= 0, codes % 128 + 1, 0).reshape(REPLICAS, 1, SECTIONS)

    note = jnp.concatenate([has_second.reshape(1), moment_dest.reshape(-1), jnp.zeros((3,), jnp.int32)])
    labels = jnp.concatenate(
        [
            labels_of(first),
            labels_of(second),
            jnp.broadcast_to(note, (REPLICAS, 1, 8)),
        ],
        axis=2,
    )
    labels = jnp.broadcast_to(labels, (REPLICAS, 4, 16)).reshape(DEVICES, 16)

    flag = has_second.reshape(1)
    *own, other = pack_second(flag, second_slots, blocks)
    flag_other = from_sibling(jnp.broadcast_to(flag, (128,)))[:1]
    came = from_sibling(other)
    other, labels = lax.optimization_barrier((other, labels))
    got = lax.all_to_all(labels, EVERY, 0, 0, tiled=True)
    mine = take_over(flag_other, came, own, after=[got])
    relays = [mine[0], spread(mine[1], "x"), spread(mine[2], "y"), spread(mine[3], "z")]
    buffer = pack(first_slots, blocks, CHUNK)

    holders = got[:, 8]
    alone = jnp.sum(holders) == 1
    numbers = jnp.arange(DEVICES, dtype=jnp.int32)
    busy = jnp.sum(jnp.where(holders > 0, numbers, 0))
    busy = jnp.where(alone, busy, 0)
    x, y, core, z = busy // 32, (busy // 8) % 4, (busy // 4) % 2, busy % 4
    found = []
    for c in (core, 1 - core):
        step = 1 + 2 * c
        for dx, dy, dz in ((0, 0, 0), (1, 0, 0), (0, 1, 0), (0, 0, 1)):
            chip = (x + dx * step) % 4 * 4 + (y + dy * step) % 4
            found.append((chip * 2 + c) * 4 + (z + dz * step) % 4)
    relay_places = jnp.stack(found).astype(jnp.int32)
    is_me = relay_places == me_r * 4 + me_z
    which = jnp.sum(jnp.where(is_me, jnp.arange(8, dtype=jnp.int32) % 4 + 1, 0)) - 1
    buffer = add_relayed(which.reshape(1).astype(jnp.int32), relays, buffer)
    arrived = lax.all_to_all(buffer.reshape(DEVICES, CHUNK, HID), EVERY, 0, 0, tiled=True)

    def second_round():
        again = pack(second_slots, blocks, SECTIONS * PIECE)
        return lax.all_to_all(
            again.reshape(DEVICES, SECTIONS * PIECE, HID), EVERY, 0, 0, tiled=True
        )

    spare = lax.cond(alone, lambda: blank(flag), second_round)

    wanted = jnp.arange(1, NBLK + 1, dtype=jnp.int32)[None, None, :]
    in_first = got[:, 0:4, None] == wanted
    in_second = got[:, 4:8, None] == wanted
    senders = numbers[:, None, None]
    later = jnp.where(alone, 2 * DEVICES, senders + DEVICES)
    places = jnp.sum(jnp.where(in_first, senders, 0) + jnp.where(in_second, later, 0), axis=0)
    places = jnp.clip(places, 0, 2 * DEVICES)
    weights = [
        [gather(s, begin, places[s], relay_places, arrived, spare) for begin in (0, HALF)]
        for s in range(SECTIONS)
    ]
    return weights, got, (places.reshape(-1), relay_places, arrived, spare)


def quarter_kernel(pick, acts, cots, acts_out, cots_out):
    chosen = pick[...]
    for j in range(GROUPS):
        wide = slice(j * 512, (j + 1) * 512)
        narrow = slice(j * 128, (j + 1) * 128)
        acts_out[:, narrow] = jnp.dot(
            acts[:, wide], chosen, preferred_element_type=f32
        ).astype(bf16)
        cots_out[:, narrow] = jnp.dot(
            cots[:, wide], chosen, preferred_element_type=f32
        ).astype(bf16)


def quarter(acts, cots, q):
    rows = jnp.arange(512, dtype=jnp.int32)[:, None]
    columns = jnp.arange(128, dtype=jnp.int32)[None, :]
    pick = (rows == (columns // 32) * 128 + q * 32 + columns % 32).astype(bf16)
    return call(
        quarter_kernel,
        [struct((TOK, LOCAL), bf16)] * 2,
        [VMEM] * 3,
        [VMEM] * 2,
    )(pick, acts, cots)


def flat(weight):
    return weight[...].reshape(LOCAL, HID)


def put_forward(message, layer_in, up_matrix):
    wide = layer_in.astype(f32)
    squares = jnp.sum(wide * wide, axis=1, keepdims=True)
    high = squares.astype(bf16)
    low = (squares - high.astype(f32)).astype(bf16)
    lane = lax.broadcasted_iota(jnp.int32, (TOK, 128), 1)
    message[:, 0:HID] = jnp.dot(layer_in, up_matrix, preferred_element_type=f32).astype(bf16)
    message[:, HID : HID + 128] = jnp.where(
        lane == 0, high.astype(f32), jnp.where(lane == 1, low.astype(f32), 0.0)
    ).astype(bf16)


def take_forward(total):
    squares = total[:, HID : HID + 1] + total[:, HID + 1 : HID + 2]
    inverse = lax.rsqrt(squares * (1.0 / D) + rms_eps)
    pre = total[:, 0:HID] * inverse * SCALE_IN
    return pre, jax.nn.gelu(pre, approximate=True).astype(bf16), inverse


def gelu_slope(v):
    root = 0.7978845608028654
    t = jnp.tanh(root * (v + 0.044715 * v * v * v))
    return 0.5 * (1.0 + t) + 0.5 * v * (1.0 - t * t) * root * (1.0 + 0.134145 * v * v)


def times_t(a, b):
    return lax.dot_general(a, b, (((1,), (1,)), ((), ())), preferred_element_type=f32)


def summed(refs):
    return sum([ref[...].astype(f32) for ref in refs[1:]], refs[0][...].astype(f32))


def open_kernel(layer_in, weight, message):
    put_forward(message, layer_in[...], flat(weight))


def forward_kernel(layer_in, out_matrix, up_next, *refs):
    messages, (pair, pre, inverse, layer_out, message) = refs[:4], refs[4:]
    result = forward_step(messages, layer_in, out_matrix, pair, pre, inverse, layer_out)
    put_forward(message, result, flat(up_next))


def forward_step(messages, layer_in, out_matrix, pair, pre, inverse, layer_out):
    pre_value, act_value, inverse_value = take_forward(summed(messages))
    pair[:, 0:LOCAL] = layer_in[...]
    pair[:, LOCAL:] = act_value
    pre[...] = pre_value
    inverse[...] = jnp.broadcast_to(inverse_value, (TOK, 128))
    branch = times_t(act_value, flat(out_matrix))
    result = (layer_in[...].astype(f32) + branch * SCALE_OUT).astype(bf16)
    layer_out[...] = result
    return result


def turn_kernel(layer_in, out_matrix, up_next, out_next, cots, *refs):
    messages, (pair, pre, inverse, layer_out, message) = refs[:4], refs[4:]
    result = forward_step(messages, layer_in, out_matrix, pair, pre, inverse, layer_out)
    put_forward(message, result, flat(up_next))
    message[:, HID + 128 :] = jnp.dot(
        cots[...], flat(out_next), preferred_element_type=f32
    ).astype(bf16)


def backward_kernel(from_forward, *refs):
    messages, refs = refs[:4], refs[4:]
    total = summed(messages)
    if from_forward:
        grad_out, layer_in, up_matrix, out_next, pair, back, grad_in, message = refs
        pre_value, act_value, inverse_value = take_forward(total)
        pair[:, 0:LOCAL] = layer_in[...]
        pair[:, LOCAL:] = act_value
        grad_act = total[:, HID + 128 :] * SCALE_OUT
    else:
        pre, inverse, grad_out, layer_in, up_matrix, out_next, back, grad_in, message = refs
        pre_value = pre[...]
        inverse_value = inverse[:, 0:1]
        grad_act = total * SCALE_OUT
    pulled = (grad_act * gelu_slope(pre_value)).astype(bf16)
    back[:, 0:LOCAL] = grad_out[...]
    back[:, LOCAL:] = (pulled.astype(f32) * inverse_value).astype(bf16)
    correction = jnp.sum(pulled.astype(f32) * pre_value, axis=1, keepdims=True) * (1.0 / D)
    grad_norm = times_t(pulled, flat(up_matrix)) * SCALE_IN
    normed = layer_in[...].astype(f32) * inverse_value
    result = grad_out[...].astype(f32) + (grad_norm - normed * correction) * inverse_value
    result = result.astype(bf16)
    grad_in[...] = result
    message[...] = jnp.dot(result, flat(out_next), preferred_element_type=f32).astype(bf16)


def close_kernel(*refs):
    messages, (pre, inverse, grad_out, back) = refs[:4], refs[4:]
    grad_act = summed(messages) * SCALE_OUT
    pulled = (grad_act * gelu_slope(pre[...])).astype(bf16)
    back[:, 0:LOCAL] = grad_out[...]
    back[:, LOCAL:] = (pulled.astype(f32) * inverse[:, 0:1]).astype(bf16)


def all_of(message):
    return [message] + [shift_z(message, k) for k in (1, 3, 2)]


def products(core, pair, back, pair_sib, back_sib, chosen, store):
    small = slice(LOCAL, LOCAL + HID)
    half = GROUPS // 2

    def product(left, left_sib, right, right_sib, scale, start):
        both = jnp.concatenate([left[:, small], left_sib[:, small]], axis=0)
        turned = both.astype(f32).T.astype(bf16)
        for g in range(half):
            columns = pl.ds(pl.multiple_of((2 * g + core) * 128, 128), 128)
            chosen[0:TOK, g * 128 : (g + 1) * 128] = right[:, columns]
            chosen[TOK:, g * 128 : (g + 1) * 128] = right_sib[:, columns]
        result = jnp.dot(turned, chosen[...], preferred_element_type=f32) * scale
        for g in range(half):
            store(start + g, result[:, g * 128 : (g + 1) * 128].astype(bf16))

    product(back, back_sib, pair, pair_sib, SCALE_IN, 0)
    product(pair, pair_sib, back, back_sib, SCALE_OUT, half)
    for owner in range(2 * half, 16):
        store(owner, jnp.zeros((HID, 128), bf16))


def gradient_kernel(x_first, count, place, *refs):
    ins, outs, (chosen, table) = refs[: 4 * count], refs[4 * count : 4 * count + 4], refs[-2:]
    for n in range(count):

        def store(owner, value):
            table[owner, n] = value

        products(place[2], *ins[4 * n : 4 * n + 4], chosen, store)
    for k in range(4):
        for j in range(4):
            if x_first:
                owner = lax.rem(place[0] + k, 4) * 4 + j
            else:
                owner = j * 4 + lax.rem(place[1] + k, 4)
            outs[k][j] = table[owner]


def halve_kernel(x_first, counts, place, *refs):
    mine = place[1] if x_first else place[0]
    outs = refs[4 * len(counts) :]
    for k in range(4):
        chunk = lax.rem(mine + k, 4)
        start = 0
        for n, count in enumerate(counts):
            four = refs[4 * n : 4 * n + 4]
            total = sum([ref[chunk].astype(f32) for ref in four[1:]], four[0][chunk].astype(f32))
            outs[k][start : start + count] = total.astype(outs[k].dtype)
            start += count


def first_half(x_first, place, sections, after=()):
    count = len(sections)
    chunks = call(
        functools.partial(gradient_kernel, x_first, count),
        [struct((4, count, HID, 128), bf16)] * 4,
        [SMEM] + [VMEM] * (4 * count),
        [VMEM] * 4,
        [pltpu.VMEM((2 * TOK, LOCAL // 2), bf16), pltpu.VMEM((16, count, HID, 128), bf16)],
        after=after,
    )(place, *[v for section in sections for v in section])
    step = (1, 0) if x_first else (0, 1)
    return [chunks[0]] + [shift_xy(chunks[k], k * step[0], k * step[1]) for k in (1, 2, 3)]


def second_half(x_first, place, parts, after):
    counts = [part[0].shape[1] for part in parts]
    count = sum(counts)
    kept, *sends = call(
        functools.partial(halve_kernel, x_first, counts),
        [struct((count, HID, 128), f32)] + [struct((count, HID, 128), bf16)] * 3,
        [SMEM] + [VMEM] * (4 * len(parts)),
        [VMEM] * 4,
        after=after,
    )(place, *[v for part in parts for v in part])
    step = (0, 1) if x_first else (1, 0)
    return [kept] + [shift_xy(sends[k - 1], k * step[0], k * step[1]) for k in (1, 2, 3)]


def finish_kernel(places_in, place, *refs):
    groups, refs = refs[: 4 * len(places_in)], refs[4 * len(places_in) :]
    kept, sends, table = refs[0], refs[1:4], refs[4]
    for m, sections in enumerate(places_in):
        four = groups[4 * m : 4 * m + 4]
        for n, section in enumerate(sections):
            table[section] = sum([ref[n].astype(f32) for ref in four[1:]], four[0][n])
    for k in range(4):
        value = table[lax.rem(place[3] + k, 4)]
        if k == 0:
            kept[...] = value
        else:
            sends[k - 1][...] = value.astype(bf16)


def split_moments_kernel(place, first, second, *outs):
    for k in range(4):
        rows = pl.ds(pl.multiple_of(lax.rem(place[3] + k, 4) * PIECE, PIECE), PIECE)
        for a in range(OWN):
            outs[k][0, a] = first[a, rows, :].astype(bf16)
            outs[k][1, a] = second[a, rows, :].astype(bf16)


def order_kernel(place, source, places, relays, first, second, *refs):
    moments, outs, (table, came, sem) = refs[:4], refs[4:8], refs[8:]
    start = jnp.minimum(place[4], REAL_OWNERS - 1) * OWN
    for k in range(4):
        section = lax.rem(place[3] + k, 4)
        for i in range(OWN):
            held = places[section * NBLK + start + i]
            fetch(section, held, relays, first, second, came.at[k, i], sem)
    for k in range(4):
        table[k] = moments[k][...]
    for k in range(4):
        section = lax.rem(place[3] + k, 4)
        for i in range(OWN):
            held = source[section * OWN + i]
            outs[k][1, i] = table[held // OWN, 0, lax.rem(held, OWN)]
            outs[k][2, i] = table[held // OWN, 1, lax.rem(held, OWN)]
    pltpu.make_async_copy(came, came, sem).wait()
    for k in range(4):
        outs[k][0] = came[k]


def adam_kernel(place, *refs):
    gradients, held = refs[:4], refs[4:8]
    weight_out, first_out, second_out = refs[8:]
    real = place[4] < REAL_OWNERS
    for k in range(4):
        q = lax.rem(place[3] + 4 - k, 4)
        rows = pl.ds(pl.multiple_of(q * PIECE, PIECE), PIECE)
        turned = jnp.where(real, gradients[k][...].astype(f32).T, 0.0)
        for i in range(OWN):
            gradient = turned[i * PIECE : (i + 1) * PIECE, :]
            weight = jnp.where(real, held[k][0, i].astype(f32), 0.0)
            first = beta_first * held[k][1, i].astype(f32) + (1.0 - beta_first) * gradient
            second = beta_second * held[k][2, i].astype(f32) + (
                (1.0 - beta_second) * gradient * gradient
            )
            first_out[i, rows, :] = first
            second_out[i, rows, :] = second
            weight_out[i, rows, :] = (
                weight - step_size * first / (jnp.sqrt(second) + adam_eps)
            ).astype(bf16)


def on_device(
    acts_in,
    cotangent,
    old_blocks,
    send_slot,
    send_dest,
    send_block,
    old_first,
    old_second,
    moment_dest,
):
    me_r = lax.axis_index("replica")
    me_z = lax.axis_index("section")
    place = jnp.stack([me_r // 8, (me_r // 2) % 4, me_r % 2, me_z, me_r]).astype(jnp.int32)

    split = call(
        split_moments_kernel,
        [struct((2, OWN, PIECE, HID), bf16)] * 4,
        [SMEM, VMEM, VMEM],
        [VMEM] * 4,
    )(place, old_first[0], old_second[0])
    pieces = [split[0]] + [shift_z(split[k], k) for k in (1, 2, 3)]

    weights, labels, arrivals = route_blocks(
        old_blocks, send_slot, send_dest, send_block, moment_dest
    )
    table = lax.dynamic_slice_in_dim(labels, me_r * 4, 4, 0)[:, 9:13]
    distance = (me_z - jnp.arange(SECTIONS, dtype=jnp.int32)) % 4
    held = (distance[:, None] * OWN + jnp.arange(OWN, dtype=jnp.int32)[None, :]).reshape(-1)
    slots = jnp.arange(SECTIONS * OWN, dtype=jnp.int32)
    source = jnp.sum(jnp.where(table.reshape(1, -1) == slots[:, None], held[None, :], 0), axis=1)
    layer_0, cots = quarter(acts_in, cotangent, me_z)
    message = call(
        open_kernel, struct((TOK, HID + 128), bf16), [VMEM] * 2, VMEM
    )(layer_0, weights[0][0])
    layers = [layer_0]
    pairs, pairs_sib, pres, inverses = [], [], [], []
    wide = struct((TOK, LOCAL + HID), bf16)
    narrow = struct((TOK, LOCAL), bf16)
    for s in range(SECTIONS - 1):
        messages = all_of(message)
        turn = s == SECTIONS - 2
        extra = (weights[s + 1][1], cots) if turn else ()
        pair, pre, inverse, layer, message = call(
            turn_kernel if turn else forward_kernel,
            [
                wide,
                struct((TOK, HID), f32),
                struct((TOK, 128), f32),
                narrow,
                struct((TOK, 2 * HID + 128 if turn else HID + 128), bf16),
            ],
            [VMEM] * (7 + len(extra)),
            [VMEM] * 5,
            after=pairs_sib[-1:] if s else pieces[1:],
        )(layers[s], weights[s][1], weights[s + 1][0], *extra, *messages)
        layers.append(layer)
        pairs.append(pair)
        pairs_sib.append(from_sibling(pair))
        pres.append(pre)
        inverses.append(inverse)

    ordered = call(
        order_kernel,
        [struct((3, OWN, PIECE, HID), bf16)] * 4,
        [SMEM] * 4 + [ANY] * 2 + [VMEM] * 4,
        [VMEM] * 4,
        [
            pltpu.VMEM((4, 2, OWN, PIECE, HID), bf16),
            pltpu.VMEM((4, OWN, PIECE, HID), bf16),
            pltpu.SemaphoreType.DMA,
        ],
    )(place, source, *arrivals, *pieces)
    owned = [ordered[0]] + [shift_z(ordered[k], k) for k in (1, 2, 3)]

    grad = cots
    ready, parts = [None] * SECTIONS, [None] * SECTIONS
    after = pairs_sib[-1:]
    for s in reversed(range(SECTIONS)):
        messages = all_of(message)
        if s == SECTIONS - 1:
            pair, back, grad, message = call(
                functools.partial(backward_kernel, True),
                [wide, wide, narrow, struct((TOK, HID), bf16)],
                [VMEM] * 8,
                [VMEM] * 4,
                after=after,
            )(*messages, grad, layers[s], weights[s][0], weights[s - 1][1])
            pairs.append(pair)
            pairs_sib.append(from_sibling(pair))
        elif s > 0:
            back, grad, message = call(
                functools.partial(backward_kernel, False),
                [wide, narrow, struct((TOK, HID), bf16)],
                [VMEM] * 10,
                [VMEM] * 3,
                after=after,
            )(*messages, pres[s], inverses[s], grad, layers[s], weights[s][0], weights[s - 1][1])
        else:
            back = call(close_kernel, wide, [VMEM] * 7, VMEM, after=after)(
                *messages, pres[0], inverses[0], grad
            )
        ready[s] = (pairs[s], back, pairs_sib[s], from_sibling(back))
        if s == 3:
            after = []
        elif s == 2:
            after = [ready[2][3], ready[3][3]]
        elif s == 1:
            odd = first_half(True, place, [ready[3], ready[1]])
            after = odd[:1]
        else:
            even = first_half(False, place, [ready[2], ready[0]])
            after = even[:1]
    across = second_half(True, place, [odd], after)
    along = second_half(False, place, [even], after)
    kept, *sends = call(
        functools.partial(finish_kernel, ((3, 1), (2, 0))),
        [struct((HID, 128), f32)] + [struct((HID, 128), bf16)] * 3,
        [SMEM] + [VMEM] * 8,
        [VMEM] * 4,
        [pltpu.VMEM((SECTIONS, HID, 128), f32)],
    )(place, *across, *along)
    gradients = [kept] + [shift_z(sends[k - 1], k) for k in (1, 2, 3)]
    new_weight, new_first, new_second = call(
        adam_kernel,
        [
            struct((OWN, 128, HID), bf16),
            struct((OWN, 128, HID), f32),
            struct((OWN, 128, HID), f32),
        ],
        [SMEM] + [VMEM] * 8,
        [VMEM] * 3,
    )(place, *gradients, *owned)
    return (new_weight[None], new_first[None], new_second[None])


def solution(mesh):
    in_specs = (
        P("replica", None),
        P("replica", None),
        P(("replica", "section"), None, None, None),
        P(("replica", "section"), None),
        P(("replica", "section"), None),
        P(("replica", "section"), None),
        P(("replica", "section"), None, None, None),
        P(("replica", "section"), None, None, None),
        P(("replica", "section"), None),
    )
    out_specs = (
        P("section", "replica", None, None),
        P("section", "replica", None, None),
        P("section", "replica", None, None),
    )
    return jax.shard_map(
        on_device, mesh=mesh, in_specs=in_specs, out_specs=out_specs, check_vma=False
    )
```

time: 375 us -> 317 us (0.85)
  waiting for transfers between devices: 185 us -> 157 us
  starting transfers between devices: 123 us -> 97.7 us
  local copies, waits for them, and re-layouts: 14.8 us -> 3.8 us
  Pallas kernels: 39.3 us -> 46 us
    ppermute x20 -> x12, waiting for transfers between devices: 146 us -> 15 us  [shift_xy(): return lax.ppermute(block, 'replica', route)]
    all_to_all x2 -> x1, waiting for transfers between devices: 8.66 us -> 104 us  [route_blocks(): lax.all_to_all(buffer.reshape(DEVICES, CHUNK, HID), EVERY, 0, 0, tiled=True)]
    all_to_all x2 -> x1, starting transfers between devices: 28 us -> 6.35 us  [route_blocks(): lax.all_to_all(buffer.reshape(DEVICES, CHUNK, HID), EVERY, 0, 0, tiled=True)]
    ppermute x20 -> x12, starting transfers between devices: 40.9 us -> 29.6 us  [shift_xy(): return lax.ppermute(block, 'replica', route)]
    unnamed x24 -> x20, local copies, waits for them, and re-layouts: 8.92 us -> 2.16 us
    pallas_call x28 -> x30, Pallas kernels: 39.3 us -> 46 us  [call(): return lambda *arrays: run(*after, *arrays)]
    all_to_all x1, waiting for transfers between devices: 0.8 us -> 7.43 us  [route_blocks(): got = lax.all_to_all(labels, EVERY, 0, 0, tiled=True)]
    ppermute x33 -> x30, waiting for transfers between devices: 30.3 us -> 25.4 us  [shift_z(): lax.ppermute(block, 'section', [(i, (i + step) % 4) for i in range(4)])]
  transfers between devices with their start and end apart: 65 -> 57, of which waited for: 29 -> 24; matrix products, arithmetic and copies ran while one was open for 3% -> 2% of each run, Pallas kernels for 9% -> 12%
where the time goes in v2:
time: 317 us; the launch traced here: 315 us
  waiting for transfers between devices  157 us (50%)
  starting transfers between devices  97.7 us (31%)
  Pallas kernels  46 us (15%)
  other arithmetic  6.18 us (2%)
  between operations  4.16 us (1%)
  local copies, waits for them, and re-layouts  3.8 us (1%)
    all_to_all x1, waiting for transfers between devices, route_blocks(): lax.all_to_all(buffer.reshape(DEVICES, CHUNK, HID), EVERY, 0, 0, tiled=True)  104 us
    pallas_call x30, Pallas kernels, call(): return lambda *arrays: run(*after, *arrays)  46 us
    ppermute x30, starting transfers between devices, shift_z(): lax.ppermute(block, 'section', [(i, (i + step) % 4) for i in range(4)])  45.6 us
    ppermute x12, starting transfers between devices, shift_xy(): return lax.ppermute(block, 'replica', route)  29.6 us
    ppermute x30, waiting for transfers between devices, shift_z(): lax.ppermute(block, 'section', [(i, (i + step) % 4) for i in range(4)])  25.4 us
    ppermute x12, waiting for transfers between devices, shift_xy(): return lax.ppermute(block, 'replica', route)  15 us
    all_to_all x1, starting transfers between devices, route_blocks(): got = lax.all_to_all(labels, EVERY, 0, 0, tiled=True)  11 us
    all_to_all x1, waiting for transfers between devices, route_blocks(): got = lax.all_to_all(labels, EVERY, 0, 0, tiled=True)  7.43 us
  transfers between devices with their start and end apart: 57, of which 24 were waited for; matrix products, arithmetic and copies ran while one was open for 2% of the time, Pallas kernels for 12%

profile of v2, /device:TPU:8, one launch (start us, length us, event | category | flops | bytes accessed | tf_op | source)
XLA Modules:
  0.0 314.9 jit_solution(16585452148641605788)
XLA Ops:
  6.5 11.0 %all-to-all-start.1 = ((s32[128,1,16]{2,1,0:T(1,128)}), s32[128,1,16]{2,1,0:T(1,128)S(1)}, u32[]{:S(2)}, u32[]{:S(2)}) async-start(s32[128,1,16]{2,1,0:T(1,128)} %bitcast.15), calls=%async_computation.1 | async-start | bytes 131072 | tf_op jit(solution)/shard_map/all_to_all | solution.py:350
  18.7 7.4 %all-to-all-done.1 = s32[128,1,16]{2,1,0:T(1,128)S(1)} async-done(((s32[128,1,16]{2,1,0:T(1,128)}), s32[128,1,16]{2,1,0:T(1,128)S(1)}, u32[]{:S(2)}, u32[]{:S(2)}) %all-to-all-start.1) | async-done | bytes 8224 | tf_op jit(solution)/shard_map/all_to_all | solution.py:350
  28.1 3.7 %collective-permute-start.6 = (bf16[32,4,16,256]{3,2,1,0:T(8,128)(2,1)}, bf16[32,4,16,256]{3,2,1,0:T(8,128)(2,1)}, u32[]{:S(2)}, u32[]{:S(2)}) collective-permute-start(bf16[32,4,16,256]{3,2,1,0:T(8,128)(2,1)} %get-tuple-element.93), channel_id=1, source_target_pairs={{0,8},{4,28},{8,16},{12,4},{16,24},{20,12},{24,0},{28,20},{32,40},... | collective-permute-start | bytes 3145736 | tf_op jit(solution)/shard_map/ppermute | solution.py:101
  31.8 7.5 %shard_map.116.refs_5_ = bf16[32,4,144,256]{3,2,1,0:T(8,128)(2,1)} custom-call(s32[128]{0:T(128)} %get-tuple-element.159.refs_0_, bf16[112,4,32,256]{3,2,1,0:T(8,128)(2,1)} %bitcast.47), custom_call_target="tpu_custom_call" | custom-call | tf_op jit(solution)/shard_map/pallas_call | solution.py:65
  44.5 3.7 %collective-permute-done.7.refs_4_ = bf16[32,4,16,256]{3,2,1,0:T(8,128)(2,1)} collective-permute-done((bf16[32,4,16,256]{3,2,1,0:T(8,128)(2,1)}, bf16[32,4,16,256]{3,2,1,0:T(8,128)(2,1)}, u32[]{:S(2)}, u32[]{:S(2)}) %collective-permute-start.7) | collective-permute-done | bytes 1048608 | tf_op jit(solution)/shard_map/ppermute | solution.py:93
  48.2 6.4 %all-to-all-start.2 = ((bf16[128,144,256]{2,1,0:T(8,128)(2,1)}), bf16[128,144,256]{2,1,0:T(8,128)(2,1)}, u32[]{:S(2)}, u32[]{:S(2)}) async-start(bf16[128,144,256]{2,1,0:T(8,128)(2,1)} %bitcast.45), calls=%async_computation.2 | async-start | bytes 18874368 | tf_op jit(solution)/shard_map/all_to_all | solution.py:371
  57.7 3.2 %collective-permute-start.1 = (bf16[2,4,32,256]{3,2,1,0:T(8,128)(2,1)}, bf16[2,4,32,256]{3,2,1,0:T(8,128)(2,1)S(1)}, u32[]{:S(2)}, u32[]{:S(2)}) collective-permute-start(bf16[2,4,32,256]{3,2,1,0:T(8,128)(2,1)} %get-tuple-element.82), channel_id=1, source_target_pairs={{0,2},{1,3},{2,0},{3,1},{4,6},{5,7},{6,4},{7,5},{8,10},{9,11},{10,... | collective-permute-start | bytes 393224 | tf_op jit(solution)/shard_map/ppermute | solution.py:83
  65.3 104.0 %all-to-all-done.2.refs_2_.refs_4_ = bf16[128,144,256]{2,1,0:T(8,128)(2,1)} async-done(((bf16[128,144,256]{2,1,0:T(8,128)(2,1)}), bf16[128,144,256]{2,1,0:T(8,128)(2,1)}, u32[]{:S(2)}, u32[]{:S(2)}) %all-to-all-start.2) | async-done | bytes 9437216 | tf_op jit(solution)/shard_map/all_to_all | solution.py:371
  171.4 4.5 %collective-permute-start.10 = (bf16[128,384]{1,0:T(8,128)(2,1)S(1)}, bf16[128,384]{1,0:T(8,128)(2,1)S(1)}, u32[]{:S(2)}, u32[]{:S(2)}) collective-permute-start(bf16[128,384]{1,0:T(8,128)(2,1)S(1)} %shard_map.121.refs_6_), channel_id=1, source_target_pairs={{0,2},{1,3},{2,0},{3,1},{4,6},{5,7},{6,4},{7,5},{8,10},{9,11},{10,... | collective-permute-start | bytes 294920 | tf_op jit(solution)/shard_map/ppermute | solution.py:83
  175.9 3.2 %collective-permute-start.9 = (bf16[128,384]{1,0:T(8,128)(2,1)S(1)}, bf16[128,384]{1,0:T(8,128)(2,1)S(1)}, u32[]{:S(2)}, u32[]{:S(2)}) collective-permute-start(bf16[128,384]{1,0:T(8,128)(2,1)S(1)} %shard_map.121.refs_6_), channel_id=1, source_target_pairs={{0,3},{1,0},{2,1},{3,2},{4,7},{5,4},{6,5},{7,6},{8,11},{9,8},{10,9... | collective-permute-start | bytes 294920 | tf_op jit(solution)/shard_map/ppermute | solution.py:83
  184.0 3.2 %collective-permute-start.13 = (bf16[128,384]{1,0:T(8,128)(2,1)S(1)}, bf16[128,384]{1,0:T(8,128)(2,1)S(1)}, u32[]{:S(2)}, u32[]{:S(2)}) collective-permute-start(bf16[128,384]{1,0:T(8,128)(2,1)S(1)} %get-tuple-element.97.refs_4_), channel_id=1, source_target_pairs={{0,3},{1,0},{2,1},{3,2},{4,7},{5,4},{6,5},{7,6},{8,11},{9,8},{10,9... | collective-permute-start | bytes 294920 | tf_op jit(solution)/shard_map/ppermute | solution.py:83
  194.8 2.8 collective-permute-start.17
  210.1 2.5 collective-permute-done.20.refs_2_
  212.7 2.8 collective-permute-done.21.refs_3_
  223.5 2.9 collective-permute-done.25.refs_3_
  227.6 3.0 collective-permute-start.30
  230.7 2.4 collective-permute-done.29.refs_3_
  233.8 2.7 collective-permute-done.31.refs_5_
  237.4 3.2 %collective-permute-start.34 = (bf16[128,256]{1,0:T(8,128)(2,1)S(1)}, bf16[128,256]{1,0:T(8,128)(2,1)S(1)}, u32[]{:S(2)}, u32[]{:S(2)}) collective-permute-start(bf16[128,256]{1,0:T(8,128)(2,1)S(1)} %get-tuple-element.118.refs_1_), channel_id=1, source_target_pairs={{0,3},{1,0},{2,1},{3,2},{4,7},{5,4},{6,5},{7,6},{8,11},{9,8},{10,9... | collective-permute-start | bytes 196616 | tf_op jit(solution)/shard_map/ppermute | solution.py:83
  240.7 3.2 %shard_map.133 = (bf16[4,2,256,128]{3,2,1,0:T(8,128)(2,1)S(1)}, bf16[4,2,256,128]{3,2,1,0:T(8,128)(2,1)S(1)}, bf16[4,2,256,128]{3,2,1,0:T(8,128)(2,1)}, bf16[4,2,256,128]{3,2,1,0:T(8,128)(2,1)}) custom-call(s32[5]{0:T(128)S(1)} %stack.50.refs_0_.refs_1_, bf16[128,2048]{1,0:T(8,128)(2,1)S(1)} %get-tuple-element.110.refs_1_, ...), custom_call_target="tpu_custom_call" | custom-call | tf_op jit(solution)/shard_map/pallas_call | solution.py:65
  243.8 2.6 collective-permute-done.35.refs_4_
  250.1 3.4 %shard_map.135 = (bf16[4,2,256,128]{3,2,1,0:T(8,128)(2,1)S(1)}, bf16[4,2,256,128]{3,2,1,0:T(8,128)(2,1)}, bf16[4,2,256,128]{3,2,1,0:T(8,128)(2,1)}, bf16[4,2,256,128]{3,2,1,0:T(8,128)(2,1)}) custom-call(s32[5]{0:T(128)S(1)} %stack.50.refs_0_.refs_1_, bf16[128,2048]{1,0:T(8,128)(2,1)S(1)} %get-tuple-element.102.refs_1_, ...), custom_call_target="tpu_custom_call" | custom-call | tf_op jit(solution)/shard_map/pallas_call | solution.py:65
  253.4 4.4 %collective-permute-start.43 = (bf16[4,2,256,128]{3,2,1,0:T(8,128)(2,1)}, bf16[4,2,256,128]{3,2,1,0:T(8,128)(2,1)S(1)}, u32[]{:S(2)}, u32[]{:S(2)}) collective-permute-start(bf16[4,2,256,128]{3,2,1,0:T(8,128)(2,1)} %get-tuple-element.130), channel_id=1, source_target_pairs={{0,8},{4,12},{8,16},{12,20},{16,24},{20,28},{24,0},{28,4},{32,40},... | collective-permute-start | bytes 1572872 | tf_op jit(solution)/shard_map/ppermute | solution.py:79
  257.9 4.8 %collective-permute-start.44 = (bf16[4,2,256,128]{3,2,1,0:T(8,128)(2,1)}, bf16[4,2,256,128]{3,2,1,0:T(8,128)(2,1)S(1)}, u32[]{:S(2)}, u32[]{:S(2)}) collective-permute-start(bf16[4,2,256,128]{3,2,1,0:T(8,128)(2,1)} %get-tuple-element.131), channel_id=1, source_target_pairs={{0,16},{4,20},{8,24},{12,28},{16,0},{20,4},{24,8},{28,12},{32,48},... | collective-permute-start | bytes 1572872 | tf_op jit(solution)/shard_map/ppermute | solution.py:79
  262.7 10.8 %collective-permute-done.37.refs_3_ = bf16[4,2,256,128]{3,2,1,0:T(8,128)(2,1)S(1)} collective-permute-done((bf16[4,2,256,128]{3,2,1,0:T(8,128)(2,1)S(1)}, bf16[4,2,256,128]{3,2,1,0:T(8,128)(2,1)S(1)}, u32[]{:S(2)}, u32[]{:S(2)}) %collective-permute-start.37) | collective-permute-done | bytes 524320 | tf_op jit(solution)/shard_map/ppermute | solution.py:79
  275.9 3.6 %collective-permute-start.40 = (bf16[2,256,128]{2,1,0:T(8,128)(2,1)S(1)}, bf16[2,256,128]{2,1,0:T(8,128)(2,1)S(1)}, u32[]{:S(2)}, u32[]{:S(2)}) collective-permute-start(bf16[2,256,128]{2,1,0:T(8,128)(2,1)S(1)} %get-tuple-element.127), channel_id=1, source_target_pairs={{0,8},{4,12},{8,16},{12,20},{16,24},{20,28},{24,0},{28,4},{32,40},... | collective-permute-start | bytes 393224 | tf_op jit(solution)/shard_map/ppermute | solution.py:79
  279.5 4.8 %collective-permute-start.41 = (bf16[2,256,128]{2,1,0:T(8,128)(2,1)S(1)}, bf16[2,256,128]{2,1,0:T(8,128)(2,1)S(1)}, u32[]{:S(2)}, u32[]{:S(2)}) collective-permute-start(bf16[2,256,128]{2,1,0:T(8,128)(2,1)S(1)} %get-tuple-element.128), channel_id=1, source_target_pairs={{0,16},{4,20},{8,24},{12,28},{16,0},{20,4},{24,8},{28,12},{32,48},... | collective-permute-start | bytes 393224 | tf_op jit(solution)/shard_map/ppermute | solution.py:79
  284.3 5.1 %collective-permute-start.42 = (bf16[2,256,128]{2,1,0:T(8,128)(2,1)S(1)}, bf16[2,256,128]{2,1,0:T(8,128)(2,1)S(1)}, u32[]{:S(2)}, u32[]{:S(2)}) collective-permute-start(bf16[2,256,128]{2,1,0:T(8,128)(2,1)S(1)} %get-tuple-element.129), channel_id=1, source_target_pairs={{0,24},{4,28},{8,0},{12,4},{16,8},{20,12},{24,16},{28,20},{32,56},... | collective-permute-start | bytes 393224 | tf_op jit(solution)/shard_map/ppermute | solution.py:79
  294.8 3.3 %collective-permute-start.48 = (bf16[2,256,128]{2,1,0:T(8,128)(2,1)S(1)}, bf16[2,256,128]{2,1,0:T(8,128)(2,1)S(1)}, u32[]{:S(2)}, u32[]{:S(2)}) collective-permute-start(bf16[2,256,128]{2,1,0:T(8,128)(2,1)S(1)} %get-tuple-element.136), channel_id=1, source_target_pairs={{0,96},{4,100},{8,104},{12,108},{16,112},{20,116},{24,120},{28,124... | collective-permute-start | bytes 393224 | tf_op jit(solution)/shard_map/ppermute | solution.py:79
  298.1 2.4 collective-permute-start.53
  304.8 3.8 %collective-permute-start.50 = (bf16[256,128]{1,0:T(8,128)(2,1)S(1)}, bf16[256,128]{1,0:T(8,128)(2,1)S(1)}, u32[]{:S(2)}, u32[]{:S(2)}) collective-permute-start(bf16[256,128]{1,0:T(8,128)(2,1)S(1)} %get-tuple-element.139), channel_id=1, source_target_pairs={{0,2},{1,3},{2,0},{3,1},{4,6},{5,7},{6,4},{7,5},{8,10},{9,11},{10,... | collective-permute-start | bytes 196616 | tf_op jit(solution)/shard_map/ppermute | solution.py:83
  309.5 2.1 collective-permute-done.50.refs_3_
  (171 shorter events, 76.4 us)
Async XLA Ops:
  4.6 21.5 %collective-permute-start.4 = (bf16[4,32,4,16,256]{4,3,2,1,0:T(8,128)(2,1)}, bf16[4,32,4,16,256]{4,3,2,1,0:T(8,128)(2,1)}, u32[]{:S(2)}, u32[]{:S(2)}) collective-permute-start(bf16[4,32,4,16,256]{4,3,2,1,0:T(8,128)(2,1)} %get-tuple-element.85), channel_id=1, source_target_pairs={{0,4},{4,0},{8,12},{12,8},{16,20},{20,16},{24,28},{28,24},{32,36},... | collective-permute-start | bytes 12582920 | tf_op jit(solution)/shard_map/ppermute | solution.py:105
  6.5 19.6 %all-to-all-start.1 = ((s32[128,1,16]{2,1,0:T(1,128)}), s32[128,1,16]{2,1,0:T(1,128)S(1)}, u32[]{:S(2)}, u32[]{:S(2)}) async-start(s32[128,1,16]{2,1,0:T(1,128)} %bitcast.15), calls=%async_computation.1 | async-start | bytes 131072 | tf_op jit(solution)/shard_map/all_to_all | solution.py:350
  27.5 16.4 %collective-permute-start.5 = (bf16[32,4,16,256]{3,2,1,0:T(8,128)(2,1)}, bf16[32,4,16,256]{3,2,1,0:T(8,128)(2,1)S(1)}, u32[]{:S(2)}, u32[]{:S(2)}) collective-permute-start(bf16[32,4,16,256]{3,2,1,0:T(8,128)(2,1)} %get-tuple-element.92), channel_id=1, source_target_pairs={{0,32},{4,100},{8,40},{12,108},{16,48},{20,116},{24,56},{28,124},{... | collective-permute-start | bytes 3145736 | tf_op jit(solution)/shard_map/ppermute | solution.py:101
  28.1 16.4 %collective-permute-start.6 = (bf16[32,4,16,256]{3,2,1,0:T(8,128)(2,1)}, bf16[32,4,16,256]{3,2,1,0:T(8,128)(2,1)}, u32[]{:S(2)}, u32[]{:S(2)}) collective-permute-start(bf16[32,4,16,256]{3,2,1,0:T(8,128)(2,1)} %get-tuple-element.93), channel_id=1, source_target_pairs={{0,8},{4,28},{8,16},{12,4},{16,24},{20,12},{24,0},{28,20},{32,40},... | collective-permute-start | bytes 3145736 | tf_op jit(solution)/shard_map/ppermute | solution.py:101
  31.8 16.3 %collective-permute-start.7 = (bf16[32,4,16,256]{3,2,1,0:T(8,128)(2,1)}, bf16[32,4,16,256]{3,2,1,0:T(8,128)(2,1)}, u32[]{:S(2)}, u32[]{:S(2)}) collective-permute-start(bf16[32,4,16,256]{3,2,1,0:T(8,128)(2,1)} %get-tuple-element.94), channel_id=1, source_target_pairs={{0,1},{1,2},{2,3},{3,0},{4,7},{5,4},{6,5},{7,6},{8,9},{9,10},{10,1... | collective-permute-start | bytes 3145736 | tf_op jit(solution)/shard_map/ppermute | solution.py:93
  48.2 121.0 %all-to-all-start.2 = ((bf16[128,144,256]{2,1,0:T(8,128)(2,1)}), bf16[128,144,256]{2,1,0:T(8,128)(2,1)}, u32[]{:S(2)}, u32[]{:S(2)}) async-start(bf16[128,144,256]{2,1,0:T(8,128)(2,1)} %bitcast.45), calls=%async_computation.2 | async-start | bytes 18874368 | tf_op jit(solution)/shard_map/all_to_all | solution.py:371
  56.0 119.9 %collective-permute-start = (bf16[2,4,32,256]{3,2,1,0:T(8,128)(2,1)}, bf16[2,4,32,256]{3,2,1,0:T(8,128)(2,1)S(1)}, u32[]{:S(2)}, u32[]{:S(2)}) collective-permute-start(bf16[2,4,32,256]{3,2,1,0:T(8,128)(2,1)} %get-tuple-element.81), channel_id=1, source_target_pairs={{0,1},{1,2},{2,3},{3,0},{4,5},{5,6},{6,7},{7,4},{8,9},{9,10},{10,1... | collective-permute-start | bytes 393224 | tf_op jit(solution)/shard_map/ppermute | solution.py:83
  57.7 125.3 %collective-permute-start.1 = (bf16[2,4,32,256]{3,2,1,0:T(8,128)(2,1)}, bf16[2,4,32,256]{3,2,1,0:T(8,128)(2,1)S(1)}, u32[]{:S(2)}, u32[]{:S(2)}) collective-permute-start(bf16[2,4,32,256]{3,2,1,0:T(8,128)(2,1)} %get-tuple-element.82), channel_id=1, source_target_pairs={{0,2},{1,3},{2,0},{3,1},{4,6},{5,7},{6,4},{7,5},{8,10},{9,11},{10,... | collective-permute-start | bytes 393224 | tf_op jit(solution)/shard_map/ppermute | solution.py:83
  60.9 122.1 %collective-permute-start.2 = (bf16[2,4,32,256]{3,2,1,0:T(8,128)(2,1)}, bf16[2,4,32,256]{3,2,1,0:T(8,128)(2,1)S(1)}, u32[]{:S(2)}, u32[]{:S(2)}) collective-permute-start(bf16[2,4,32,256]{3,2,1,0:T(8,128)(2,1)} %get-tuple-element.83), channel_id=1, source_target_pairs={{0,3},{1,0},{2,1},{3,2},{4,7},{5,4},{6,5},{7,6},{8,11},{9,8},{10,9... | collective-permute-start | bytes 393224 | tf_op jit(solution)/shard_map/ppermute | solution.py:83
  171.4 11.6 %collective-permute-start.10 = (bf16[128,384]{1,0:T(8,128)(2,1)S(1)}, bf16[128,384]{1,0:T(8,128)(2,1)S(1)}, u32[]{:S(2)}, u32[]{:S(2)}) collective-permute-start(bf16[128,384]{1,0:T(8,128)(2,1)S(1)} %shard_map.121.refs_6_), channel_id=1, source_target_pairs={{0,2},{1,3},{2,0},{3,1},{4,6},{5,7},{6,4},{7,5},{8,10},{9,11},{10,... | collective-permute-start | bytes 294920 | tf_op jit(solution)/shard_map/ppermute | solution.py:83
  183.9 9.5 %collective-permute-start.11 = (bf16[128,2048]{1,0:T(8,128)(2,1)S(1)}, bf16[128,2048]{1,0:T(8,128)(2,1)S(1)}, u32[]{:S(2)}, u32[]{:S(2)}) collective-permute-start(bf16[128,2048]{1,0:T(8,128)(2,1)S(1)} %get-tuple-element.95.refs_5_), channel_id=1, source_target_pairs={{0,4},{4,0},{8,12},{12,8},{16,20},{20,16},{24,28},{28,24},{32,36},... | collective-permute-start | bytes 1572872 | tf_op jit(solution)/shard_map/ppermute | solution.py:105
  194.2 9.6 %collective-permute-start.15 = (bf16[128,2048]{1,0:T(8,128)(2,1)S(1)}, bf16[128,2048]{1,0:T(8,128)(2,1)S(1)}, u32[]{:S(2)}, u32[]{:S(2)}) collective-permute-start(bf16[128,2048]{1,0:T(8,128)(2,1)S(1)} %get-tuple-element.98.refs_5_), channel_id=1, source_target_pairs={{0,4},{4,0},{8,12},{12,8},{16,20},{20,16},{24,28},{28,24},{32,36},... | collective-permute-start | bytes 1572872 | tf_op jit(solution)/shard_map/ppermute | solution.py:105
  194.3 9.5 %collective-permute-start.16 = (bf16[128,384]{1,0:T(8,128)(2,1)S(1)}, bf16[128,384]{1,0:T(8,128)(2,1)S(1)}, u32[]{:S(2)}, u32[]{:S(2)}) collective-permute-start(bf16[128,384]{1,0:T(8,128)(2,1)S(1)} %get-tuple-element.101.refs_6_), channel_id=1, source_target_pairs={{0,1},{1,2},{2,3},{3,0},{4,5},{5,6},{6,7},{7,4},{8,9},{9,10},{10,1... | collective-permute-start | bytes 294920 | tf_op jit(solution)/shard_map/ppermute | solution.py:83
  194.8 9.1 %collective-permute-start.17 = (bf16[128,384]{1,0:T(8,128)(2,1)S(1)}, bf16[128,384]{1,0:T(8,128)(2,1)S(1)}, u32[]{:S(2)}, u32[]{:S(2)}) collective-permute-start(bf16[128,384]{1,0:T(8,128)(2,1)S(1)} %get-tuple-element.101.refs_6_), channel_id=1, source_target_pairs={{0,3},{1,0},{2,1},{3,2},{4,7},{5,4},{6,5},{7,6},{8,11},{9,8},{10,9... | collective-permute-start | bytes 294920 | tf_op jit(solution)/shard_map/ppermute | solution.py:83
  204.7 11.7 %collective-permute-start.19 = (bf16[128,2048]{1,0:T(8,128)(2,1)S(1)}, bf16[128,2048]{1,0:T(8,128)(2,1)S(1)}, u32[]{:S(2)}, u32[]{:S(2)}) collective-permute-start(bf16[128,2048]{1,0:T(8,128)(2,1)S(1)} %get-tuple-element.102.refs_1_), channel_id=1, source_target_pairs={{0,4},{4,0},{8,12},{12,8},{16,20},{20,16},{24,28},{28,24},{32,36},... | collective-permute-start | bytes 1572872 | tf_op jit(solution)/shard_map/ppermute | solution.py:105
  206.3 9.1 %collective-permute-start.21 = (bf16[128,640]{1,0:T(8,128)(2,1)S(1)}, bf16[128,640]{1,0:T(8,128)(2,1)S(1)}, u32[]{:S(2)}, u32[]{:S(2)}) collective-permute-start(bf16[128,640]{1,0:T(8,128)(2,1)S(1)} %get-tuple-element.103.refs_1_), channel_id=1, source_target_pairs={{0,3},{1,0},{2,1},{3,2},{4,7},{5,4},{6,5},{7,6},{8,11},{9,8},{10,9... | collective-permute-start | bytes 491528 | tf_op jit(solution)/shard_map/ppermute | solution.py:83
  208.1 8.3 %collective-permute-start.22 = (bf16[128,640]{1,0:T(8,128)(2,1)S(1)}, bf16[128,640]{1,0:T(8,128)(2,1)S(1)}, u32[]{:S(2)}, u32[]{:S(2)}) collective-permute-start(bf16[128,640]{1,0:T(8,128)(2,1)S(1)} %get-tuple-element.103.refs_1_), channel_id=1, source_target_pairs={{0,2},{1,3},{2,0},{3,1},{4,6},{5,7},{6,4},{7,5},{8,10},{9,11},{10,... | collective-permute-start | bytes 491528 | tf_op jit(solution)/shard_map/ppermute | solution.py:83
  221.6 14.9 %collective-permute-start.28 = (bf16[128,2048]{1,0:T(8,128)(2,1)S(1)}, bf16[128,2048]{1,0:T(8,128)(2,1)S(1)}, u32[]{:S(2)}, u32[]{:S(2)}) collective-permute-start(bf16[128,2048]{1,0:T(8,128)(2,1)S(1)} %get-tuple-element.111.refs_2_), channel_id=1, source_target_pairs={{0,4},{4,0},{8,12},{12,8},{16,20},{20,16},{24,28},{28,24},{32,36},... | collective-permute-start | bytes 1572872 | tf_op jit(solution)/shard_map/ppermute | solution.py:105
  227.3 9.2 %collective-permute-start.26 = (bf16[128,2048]{1,0:T(8,128)(2,1)S(1)}, bf16[128,2048]{1,0:T(8,128)(2,1)S(1)}, u32[]{:S(2)}, u32[]{:S(2)}) collective-permute-start(bf16[128,2048]{1,0:T(8,128)(2,1)S(1)} %get-tuple-element.109.refs_2_), channel_id=1, source_target_pairs={{0,4},{4,0},{8,12},{12,8},{16,20},{20,16},{24,28},{28,24},{32,36},... | collective-permute-start | bytes 1572872 | tf_op jit(solution)/shard_map/ppermute | solution.py:105
  246.7 26.8 %collective-permute-start.37 = (bf16[4,2,256,128]{3,2,1,0:T(8,128)(2,1)S(1)}, bf16[4,2,256,128]{3,2,1,0:T(8,128)(2,1)S(1)}, u32[]{:S(2)}, u32[]{:S(2)}) collective-permute-start(bf16[4,2,256,128]{3,2,1,0:T(8,128)(2,1)S(1)} %get-tuple-element.123), channel_id=1, source_target_pairs={{0,32},{4,36},{8,40},{12,44},{16,48},{20,52},{24,56},{28,60},{32,6... | collective-permute-start | bytes 1572872 | tf_op jit(solution)/shard_map/ppermute | solution.py:79
  247.3 26.6 %collective-permute-start.38 = (bf16[4,2,256,128]{3,2,1,0:T(8,128)(2,1)}, bf16[4,2,256,128]{3,2,1,0:T(8,128)(2,1)}, u32[]{:S(2)}, u32[]{:S(2)}) collective-permute-start(bf16[4,2,256,128]{3,2,1,0:T(8,128)(2,1)} %get-tuple-element.124), channel_id=1, source_target_pairs={{0,64},{4,68},{8,72},{12,76},{16,80},{20,84},{24,88},{28,92},{32,9... | collective-permute-start | bytes 1572872 | tf_op jit(solution)/shard_map/ppermute | solution.py:79
  248.3 26.1 %collective-permute-start.39 = (bf16[4,2,256,128]{3,2,1,0:T(8,128)(2,1)}, bf16[4,2,256,128]{3,2,1,0:T(8,128)(2,1)}, u32[]{:S(2)}, u32[]{:S(2)}) collective-permute-start(bf16[4,2,256,128]{3,2,1,0:T(8,128)(2,1)} %get-tuple-element.125), channel_id=1, source_target_pairs={{0,96},{4,100},{8,104},{12,108},{16,112},{20,116},{24,120},{28,124... | collective-permute-start | bytes 1572872 | tf_op jit(solution)/shard_map/ppermute | solution.py:79
  253.4 30.9 %collective-permute-start.43 = (bf16[4,2,256,128]{3,2,1,0:T(8,128)(2,1)}, bf16[4,2,256,128]{3,2,1,0:T(8,128)(2,1)S(1)}, u32[]{:S(2)}, u32[]{:S(2)}) collective-permute-start(bf16[4,2,256,128]{3,2,1,0:T(8,128)(2,1)} %get-tuple-element.130), channel_id=1, source_target_pairs={{0,8},{4,12},{8,16},{12,20},{16,24},{20,28},{24,0},{28,4},{32,40},... | collective-permute-start | bytes 1572872 | tf_op jit(solution)/shard_map/ppermute | solution.py:79
  257.9 31.5 %collective-permute-start.44 = (bf16[4,2,256,128]{3,2,1,0:T(8,128)(2,1)}, bf16[4,2,256,128]{3,2,1,0:T(8,128)(2,1)S(1)}, u32[]{:S(2)}, u32[]{:S(2)}) collective-permute-start(bf16[4,2,256,128]{3,2,1,0:T(8,128)(2,1)} %get-tuple-element.131), channel_id=1, source_target_pairs={{0,16},{4,20},{8,24},{12,28},{16,0},{20,4},{24,8},{28,12},{32,48},... | collective-permute-start | bytes 1572872 | tf_op jit(solution)/shard_map/ppermute | solution.py:79
  273.5 18.0 %collective-permute-start.45 = (bf16[4,2,256,128]{3,2,1,0:T(8,128)(2,1)}, bf16[4,2,256,128]{3,2,1,0:T(8,128)(2,1)}, u32[]{:S(2)}, u32[]{:S(2)}) collective-permute-start(bf16[4,2,256,128]{3,2,1,0:T(8,128)(2,1)} %get-tuple-element.132), channel_id=1, source_target_pairs={{0,24},{4,28},{8,0},{12,4},{16,8},{20,12},{24,16},{28,20},{32,56},... | collective-permute-start | bytes 1572872 | tf_op jit(solution)/shard_map/ppermute | solution.py:79
  275.9 18.8 %collective-permute-start.40 = (bf16[2,256,128]{2,1,0:T(8,128)(2,1)S(1)}, bf16[2,256,128]{2,1,0:T(8,128)(2,1)S(1)}, u32[]{:S(2)}, u32[]{:S(2)}) collective-permute-start(bf16[2,256,128]{2,1,0:T(8,128)(2,1)S(1)} %get-tuple-element.127), channel_id=1, source_target_pairs={{0,8},{4,12},{8,16},{12,20},{16,24},{20,28},{24,0},{28,4},{32,40},... | collective-permute-start | bytes 393224 | tf_op jit(solution)/shard_map/ppermute | solution.py:79
  279.5 15.2 %collective-permute-start.41 = (bf16[2,256,128]{2,1,0:T(8,128)(2,1)S(1)}, bf16[2,256,128]{2,1,0:T(8,128)(2,1)S(1)}, u32[]{:S(2)}, u32[]{:S(2)}) collective-permute-start(bf16[2,256,128]{2,1,0:T(8,128)(2,1)S(1)} %get-tuple-element.128), channel_id=1, source_target_pairs={{0,16},{4,20},{8,24},{12,28},{16,0},{20,4},{24,8},{28,12},{32,48},... | collective-permute-start | bytes 393224 | tf_op jit(solution)/shard_map/ppermute | solution.py:79
  284.3 13.7 %collective-permute-start.42 = (bf16[2,256,128]{2,1,0:T(8,128)(2,1)S(1)}, bf16[2,256,128]{2,1,0:T(8,128)(2,1)S(1)}, u32[]{:S(2)}, u32[]{:S(2)}) collective-permute-start(bf16[2,256,128]{2,1,0:T(8,128)(2,1)S(1)} %get-tuple-element.129), channel_id=1, source_target_pairs={{0,24},{4,28},{8,0},{12,4},{16,8},{20,12},{24,16},{28,20},{32,56},... | collective-permute-start | bytes 393224 | tf_op jit(solution)/shard_map/ppermute | solution.py:79
  294.6 14.0 %collective-permute-start.52 = (bf16[3,4,32,256]{3,2,1,0:T(8,128)(2,1)S(1)}, bf16[3,4,32,256]{3,2,1,0:T(8,128)(2,1)S(1)}, u32[]{:S(2)}, u32[]{:S(2)}) collective-permute-start(bf16[3,4,32,256]{3,2,1,0:T(8,128)(2,1)S(1)} %get-tuple-element.143), channel_id=1, source_target_pairs={{0,1},{1,2},{2,3},{3,0},{4,5},{5,6},{6,7},{7,4},{8,9},{9,10},{10,1... | collective-permute-start | bytes 589832 | tf_op jit(solution)/shard_map/ppermute | solution.py:83
  294.8 8.5 %collective-permute-start.48 = (bf16[2,256,128]{2,1,0:T(8,128)(2,1)S(1)}, bf16[2,256,128]{2,1,0:T(8,128)(2,1)S(1)}, u32[]{:S(2)}, u32[]{:S(2)}) collective-permute-start(bf16[2,256,128]{2,1,0:T(8,128)(2,1)S(1)} %get-tuple-element.136), channel_id=1, source_target_pairs={{0,96},{4,100},{8,104},{12,108},{16,112},{20,116},{24,120},{28,124... | collective-permute-start | bytes 393224 | tf_op jit(solution)/shard_map/ppermute | solution.py:79
  298.1 10.9 %collective-permute-start.53 = (bf16[3,4,32,256]{3,2,1,0:T(8,128)(2,1)S(1)}, bf16[3,4,32,256]{3,2,1,0:T(8,128)(2,1)S(1)}, u32[]{:S(2)}, u32[]{:S(2)}) collective-permute-start(bf16[3,4,32,256]{3,2,1,0:T(8,128)(2,1)S(1)} %get-tuple-element.144), channel_id=1, source_target_pairs={{0,2},{1,3},{2,0},{3,1},{4,6},{5,7},{6,4},{7,5},{8,10},{9,11},{10,... | collective-permute-start | bytes 589832 | tf_op jit(solution)/shard_map/ppermute | solution.py:83
  300.4 8.6 %collective-permute-start.54 = (bf16[3,4,32,256]{3,2,1,0:T(8,128)(2,1)S(1)}, bf16[3,4,32,256]{3,2,1,0:T(8,128)(2,1)S(1)}, u32[]{:S(2)}, u32[]{:S(2)}) collective-permute-start(bf16[3,4,32,256]{3,2,1,0:T(8,128)(2,1)S(1)} %get-tuple-element.145), channel_id=1, source_target_pairs={{0,3},{1,0},{2,1},{3,2},{4,7},{5,4},{6,5},{7,6},{8,11},{9,8},{10,9... | collective-permute-start | bytes 589832 | tf_op jit(solution)/shard_map/ppermute | solution.py:83
  (35 other events, 216.5 us)

commit v3 on v2

--- a/solution.py
+++ b/solution.py
@@ -16,12 +16,13 @@
 PIECE = 32
 LOCAL = HALF * PIECE
 GROUPS = LOCAL // 128
+LEFT = 2 * LOCAL + HID
 SECTIONS = 4
 REPLICAS = 32
 DEVICES = 128
 OWN = 4
 REAL_OWNERS = NBLK // OWN
-BIG = 1 << 20
+BIG = 1e6
 CHUNK = SECTIONS * PIECE + 16
 EVERY = ("replica", "section")
 
@@ -41,13 +42,14 @@
 VMEM = pl.BlockSpec(memory_space=pltpu.VMEM)
 LIMIT = 12 * 1024 * 1024
 BULK = 62 * 1024 * 1024
+BYTES_PER_US = 3.4e6
 
 
 def struct(shape, dtype):
     return jax.ShapeDtypeStruct(shape, dtype)
 
 
-def call(kernel, out_shape, in_specs, out_specs, scratch=(), after=(), aliases=None, limit=LIMIT):
+def call(kernel, out_shape, in_specs, out_specs, scratch=(), after=(), aliases=None, limit=LIMIT, us=1.0):
     waits = len(after)
 
     def body(*refs):
@@ -61,6 +63,9 @@
         scratch_shapes=list(scratch),
         input_output_aliases={waits + i: o for i, o in (aliases or {}).items()},
         compiler_params=pltpu.CompilerParams(vmem_limit_bytes=limit),
+        cost_estimate=pl.CostEstimate(
+            flops=0, bytes_accessed=int(us * BYTES_PER_US), transcendentals=0
+        ),
     )
     return lambda *arrays: run(*after, *arrays)
 
@@ -105,14 +110,14 @@
     return lax.ppermute(block, "replica", [(i, i ^ 1) for i in range(REPLICAS)])
 
 
-def pack_kernel(slots, blocks, out, room, came, went):
+def pack_kernel(which, table, blocks, out, room, came, went):
     for part in range(8):
         for s in range(SECTIONS):
 
             def start(i, carry):
                 r = part * 4 + i
                 pltpu.make_async_copy(
-                    blocks.at[slots[r * 4 + s]],
+                    blocks.at[table[which, r * 4 + s]],
                     room.at[r, :, pl.ds(s * PIECE, PIECE)],
                     came.at[part],
                 ).start()
@@ -133,9 +138,9 @@
         go(part).wait()
 
 
-def pack(slots, blocks, tall, after=()):
+def pack(which, table, blocks, tall, after=()):
     return call(
-        pack_kernel,
+        functools.partial(pack_kernel, which),
         struct((REPLICAS, 4, tall, HID), bf16),
         [SMEM, ANY],
         HBM,
@@ -145,60 +150,57 @@
             pltpu.SemaphoreType.DMA((8,)),
         ],
         after=after,
-        limit=BULK,
-    )(slots, blocks)
-
-
-def pack_second_kernel(flag, slots, blocks, *refs):
-    outs, (room, came, went) = refs[:5], refs[5:]
-
-    @pl.when(flag[0] == 1)
+        limit=BULK, us=7.4)(table, blocks)
+
+
+def pack_second_kernel(half, table, blocks, *refs):
+    outs, (room, came, went) = refs[:-3], refs[-3:]
+
+    @pl.when(table[2, 0] == 1)
     def _():
         for s in range(SECTIONS):
 
             def start(r, carry):
-                pltpu.make_async_copy(
-                    blocks.at[slots[r * 4 + s]], room.at[s, r], came.at[s]
-                ).start()
+                rows = blocks.at[table[1, r * 4 + s], :, pl.ds(half * 16, 16)]
+                pltpu.make_async_copy(rows, room.at[s, r], came.at[s]).start()
                 return carry
 
-            lax.fori_loop(0, REPLICAS, start, 0)
-
-        def go(s, h):
-            rows = room.at[s, :, :, pl.ds(h * 16, 16)]
-            return pltpu.make_async_copy(
-                rows, outs[4].at[s] if h else outs[s], went.at[s + 4 * h]
-            )
+            lax.fori_loop(0, REPLICAS, start, 0, unroll=4)
+
+        def go(s):
+            out = outs[0].at[s] if len(outs) == 1 else outs[s]
+            return pltpu.make_async_copy(room.at[s], out, went.at[s])
 
         for s in range(SECTIONS):
             pltpu.make_async_copy(room.at[s], room.at[s], came.at[s]).wait()
-            go(s, 1).start()
-            go(s, 0).start()
+            go(s).start()
         for s in range(SECTIONS):
-            go(s, 1).wait()
-            go(s, 0).wait()
-
-
-def pack_second(flag, slots, blocks):
+            go(s).wait()
+
+
+def pack_second(half, table, blocks, after=()):
+    shape = (REPLICAS, 4, 16, HID)
+    split = [struct(shape, bf16)] * SECTIONS
+    whole = [struct((SECTIONS, *shape), bf16)]
+    outs = whole if half else split
     return call(
-        pack_second_kernel,
-        [struct((REPLICAS, 4, 16, HID), bf16)] * 4
-        + [struct((SECTIONS, REPLICAS, 4, 16, HID), bf16)],
-        [SMEM, SMEM, ANY],
-        [HBM] * 5,
+        functools.partial(pack_second_kernel, half),
+        outs,
+        [SMEM, ANY],
+        [HBM] * len(outs),
         [
-            pltpu.VMEM((SECTIONS, REPLICAS, 4, PIECE, HID), bf16),
+            pltpu.VMEM((SECTIONS, *shape), bf16),
             pltpu.SemaphoreType.DMA((4,)),
-            pltpu.SemaphoreType.DMA((8,)),
+            pltpu.SemaphoreType.DMA((4,)),
         ],
-        limit=BULK,
-    )(flag, slots, blocks)
-
-
-def take_over_kernel(flag, got, in_0, in_1, in_2, in_3, out_0, out_1, out_2, out_3, room, came, went):
+        after=after,
+        limit=BULK, us=4.0)(table, blocks)
+
+
+def take_over_kernel(table, got, in_0, in_1, in_2, in_3, out_0, out_1, out_2, out_3, room, came, went):
     outs = (out_0, out_1, out_2, out_3)
 
-    @pl.when(flag[0] == 1)
+    @pl.when(table[2, 0] == 1)
     def _():
         def come(s):
             return pltpu.make_async_copy(got.at[s], room.at[s], came.at[s])
@@ -215,7 +217,7 @@
             go(s).wait()
 
 
-def take_over(flag, got, own, after):
+def take_over(flag, got, own):
     return call(
         take_over_kernel,
         [struct((REPLICAS, 4, 16, HID), bf16)] * 4,
@@ -226,16 +228,31 @@
             pltpu.SemaphoreType.DMA((4,)),
             pltpu.SemaphoreType.DMA((4,)),
         ],
-        after=after,
         aliases={2: 0, 3: 1, 4: 2, 5: 3},
-        limit=BULK,
-    )(flag, got, *own)
-
-
-def add_relayed_kernel(which, in_0, in_1, in_2, in_3, buffer, out, room, sem):
+        limit=BULK, us=4.0)(flag, got, *own)
+
+
+def relay_places(busy):
+    x, y, core, z = busy // 32, (busy // 8) % 4, (busy // 4) % 2, busy % 4
+    found = []
+    for c in (core, 1 - core):
+        step = 1 + 2 * c
+        for dx, dy, dz in ((0, 0, 0), (1, 0, 0), (0, 1, 0), (0, 0, 1)):
+            chip = (x + dx * step) % 4 * 4 + (y + dy * step) % 4
+            found.append((chip * 2 + c) * 4 + (z + dz * step) % 4)
+    return found
+
+
+def add_relayed_kernel(got, place, in_0, in_1, in_2, in_3, buffer, out, room, sem):
+    numbers = lax.broadcasted_iota(jnp.int32, (DEVICES, 16), 0)
+    lanes = lax.broadcasted_iota(jnp.int32, (DEVICES, 16), 1)
+    holds = (lanes == 8) & (got[...] == 1)
+    busy = jnp.max(jnp.where(holds, numbers.astype(f32), 0.0)).astype(jnp.int32)
+    places = relay_places(busy)
+    me = place[4] * 4 + place[3]
     for k, ref in enumerate((in_0, in_1, in_2, in_3)):
 
-        @pl.when(which[0] == k)
+        @pl.when((places[k] == me) | (places[4 + k] == me))
         def _():
             come = pltpu.make_async_copy(ref, room, sem.at[0])
             come.start()
@@ -245,16 +262,15 @@
             go.wait()
 
 
-def add_relayed(which, relays, buffer):
+def add_relayed(got, place, relays, buffer):
     return call(
         add_relayed_kernel,
         struct((REPLICAS, 4, CHUNK, HID), bf16),
-        [SMEM] + [HBM] * 5,
+        [VMEM, SMEM] + [HBM] * 5,
         HBM,
         [pltpu.VMEM((REPLICAS, 4, 16, HID), bf16), pltpu.SemaphoreType.DMA((2,))],
-        aliases={5: 0},
-        limit=BULK,
-    )(which, *relays, buffer)
+        aliases={6: 0},
+        limit=BULK, us=2.2)(got, place, *relays, buffer)
 
 
 def blank_kernel(flag, out):
@@ -304,79 +320,93 @@
         struct((HALF, PIECE, HID), bf16),
         [SMEM, SMEM, ANY, ANY],
         ANY,
-        [pltpu.SemaphoreType.DMA],
-    )(places, relays, first, second)
-
-
-def send_tables(send_slot, send_dest, send_block):
-    code = send_slot.reshape(1, -1) * 128 + send_block.reshape(1, -1)
-    match = send_dest.reshape(1, -1) == jnp.arange(DEVICES, dtype=jnp.int32)[:, None]
-    low = jnp.min(jnp.where(match, code, BIG), axis=1)
-    high = jnp.max(jnp.where(match, code, -1), axis=1)
-    first = jnp.where(low < BIG, low, -1)
-    second = jnp.where(high > low, high, -1)
-    return first, second
-
-
-def route_blocks(old_blocks, send_slot, send_dest, send_block, moment_dest):
-    me_r = lax.axis_index("replica")
-    me_z = lax.axis_index("section")
+        [pltpu.SemaphoreType.DMA], us=1.9)(places, relays, first, second)
+
+
+def tables_kernel(lists, table, labels):
+    send_slot, send_dest, send_block = lists[0:1], lists[1:2], lists[2:3]
+    code = (send_slot * 128 + send_block).astype(f32)
+    lanes = lax.broadcasted_iota(jnp.int32, (DEVICES, 128), 1)
+    rows = lax.broadcasted_iota(jnp.int32, (DEVICES, 128), 0)
+    entries = (DEVICES, lists.shape[1])
+    match = send_dest == lax.broadcasted_iota(jnp.int32, entries, 0)
+    low = jnp.min(jnp.where(match, code, BIG), axis=1, keepdims=True)
+    high = jnp.max(jnp.where(match, code, -1.0), axis=1, keepdims=True)
+    first = jnp.where(low < BIG, low, -1.0)
+    second = jnp.where(high > low, high, -1.0)
+    any_second = jnp.max(second, axis=0, keepdims=True) >= 0.0
+    flag = jnp.broadcast_to(jnp.where(any_second, 1.0, 0.0), (8, 128))
+    spare_slot = jnp.where(lanes >= NBLK, lanes - NBLK, lanes).astype(f32)
+    slots, named = [], []
+    for codes in (first, second):
+        along = jnp.broadcast_to(codes, (DEVICES, 128)).T
+        slot = jnp.floor(along * (1.0 / 128))
+        slots.append(jnp.where(along >= 0.0, slot, spare_slot)[0:8])
+        block = jnp.where(along >= 0.0, along - 128.0 * slot + 1.0, 0.0)
+        named.append(jnp.where(rows // 4 == lanes // 4, block, 0.0).astype(bf16))
+    short = lax.broadcasted_iota(jnp.int32, (8, 128), 0)
+    table[...] = jnp.where(
+        short == 0, slots[0], jnp.where(short == 1, slots[1], flag)
+    ).astype(jnp.int32)
+    d = lax.broadcasted_iota(jnp.int32, (DEVICES, 16), 0)
+    j = lax.broadcasted_iota(jnp.int32, (DEVICES, 16), 1)
+    total = jnp.where(j == 8, jnp.broadcast_to(flag[0:1, 0:16], (DEVICES, 16)), 0.0)
+    for n, names in enumerate(named):
+        pick = jnp.where(d % 4 == j - 4 * n, 1.0, 0.0).astype(bf16)
+        total = total + jnp.dot(names, pick, preferred_element_type=f32)
+    result = total.astype(jnp.int32)
+    for k in range(OWN):
+        own = jnp.broadcast_to(lists[3:4, k : k + 1], (DEVICES, 16))
+        result = jnp.where(j == 9 + k, own, result)
+    labels[...] = result
+
+
+def send_tables(moment_dest, send_slot, send_dest, send_block):
+    moments = jnp.pad(moment_dest, ((0, 0), (0, send_dest.shape[1] - moment_dest.shape[1])))
+    return call(
+        tables_kernel,
+        [struct((8, 128), jnp.int32), struct((DEVICES, 16), jnp.int32)],
+        [VMEM],
+        [VMEM] * 2,
+        us=1.0,
+    )(jnp.concatenate([send_slot, send_dest, send_block, moments], axis=0))
+
+
+def route_blocks(
+    place, acts_in, cotangent, old_blocks, send_slot, send_dest, send_block, moment_dest
+):
     blocks = old_blocks.reshape(NBLK, 4, PIECE, HID)
-    first, second = send_tables(send_slot, send_dest, send_block)
-    has_second = jnp.any(second >= 0).astype(jnp.int32)
-    spread_out = jnp.arange(DEVICES, dtype=jnp.int32) % NBLK
-    first_slots = jnp.where(first >= 0, first // 128, spread_out)
-    second_slots = jnp.where(second >= 0, second // 128, spread_out)
-
-    def labels_of(codes):
-        return jnp.where(codes >= 0, codes % 128 + 1, 0).reshape(REPLICAS, 1, SECTIONS)
-
-    note = jnp.concatenate([has_second.reshape(1), moment_dest.reshape(-1), jnp.zeros((3,), jnp.int32)])
-    labels = jnp.concatenate(
-        [
-            labels_of(first),
-            labels_of(second),
-            jnp.broadcast_to(note, (REPLICAS, 1, 8)),
-        ],
-        axis=2,
-    )
-    labels = jnp.broadcast_to(labels, (REPLICAS, 4, 16)).reshape(DEVICES, 16)
-
-    flag = has_second.reshape(1)
-    *own, other = pack_second(flag, second_slots, blocks)
-    flag_other = from_sibling(jnp.broadcast_to(flag, (128,)))[:1]
+    table, labels = send_tables(moment_dest, send_slot, send_dest, send_block)
+
+    (other,) = pack_second(1, table, blocks)
+    table_other = from_sibling(table)
     came = from_sibling(other)
     other, labels = lax.optimization_barrier((other, labels))
     got = lax.all_to_all(labels, EVERY, 0, 0, tiled=True)
-    mine = take_over(flag_other, came, own, after=[got])
+    own = pack_second(0, table, blocks, after=[other])
+    mine = take_over(table_other, came, own)
     relays = [mine[0], spread(mine[1], "x"), spread(mine[2], "y"), spread(mine[3], "z")]
-    buffer = pack(first_slots, blocks, CHUNK)
-
+    buffer = pack(0, table, blocks, CHUNK)
+
+    buffer = add_relayed(got, place, relays, buffer)
+    layer_0, cots = quarter(acts_in, cotangent, place[3])
+    buffer, got = lax.optimization_barrier((buffer, got))
     holders = got[:, 8]
     alone = jnp.sum(holders) == 1
     numbers = jnp.arange(DEVICES, dtype=jnp.int32)
     busy = jnp.sum(jnp.where(holders > 0, numbers, 0))
     busy = jnp.where(alone, busy, 0)
-    x, y, core, z = busy // 32, (busy // 8) % 4, (busy // 4) % 2, busy % 4
-    found = []
-    for c in (core, 1 - core):
-        step = 1 + 2 * c
-        for dx, dy, dz in ((0, 0, 0), (1, 0, 0), (0, 1, 0), (0, 0, 1)):
-            chip = (x + dx * step) % 4 * 4 + (y + dy * step) % 4
-            found.append((chip * 2 + c) * 4 + (z + dz * step) % 4)
-    relay_places = jnp.stack(found).astype(jnp.int32)
-    is_me = relay_places == me_r * 4 + me_z
-    which = jnp.sum(jnp.where(is_me, jnp.arange(8, dtype=jnp.int32) % 4 + 1, 0)) - 1
-    buffer = add_relayed(which.reshape(1).astype(jnp.int32), relays, buffer)
+    relayed_by = jnp.stack(relay_places(busy)).astype(jnp.int32)
     arrived = lax.all_to_all(buffer.reshape(DEVICES, CHUNK, HID), EVERY, 0, 0, tiled=True)
 
     def second_round():
-        again = pack(second_slots, blocks, SECTIONS * PIECE)
+        again = pack(1, table, blocks, SECTIONS * PIECE)
         return lax.all_to_all(
             again.reshape(DEVICES, SECTIONS * PIECE, HID), EVERY, 0, 0, tiled=True
         )
 
-    spare = lax.cond(alone, lambda: blank(flag), second_round)
+    arrived, table, alone_now = lax.optimization_barrier((arrived, table, alone))
+    spare = lax.cond(alone_now, lambda: blank(table), second_round)
 
     wanted = jnp.arange(1, NBLK + 1, dtype=jnp.int32)[None, None, :]
     in_first = got[:, 0:4, None] == wanted
@@ -386,10 +416,10 @@
     places = jnp.sum(jnp.where(in_first, senders, 0) + jnp.where(in_second, later, 0), axis=0)
     places = jnp.clip(places, 0, 2 * DEVICES)
     weights = [
-        [gather(s, begin, places[s], relay_places, arrived, spare) for begin in (0, HALF)]
+        [gather(s, begin, places[s], relayed_by, arrived, spare) for begin in (0, HALF)]
         for s in range(SECTIONS)
     ]
-    return weights, got, (places.reshape(-1), relay_places, arrived, spare)
+    return weights, got, (places.reshape(-1), relayed_by, arrived, spare), layer_0, cots
 
 
 def quarter_kernel(pick, acts, cots, acts_out, cots_out):
@@ -413,8 +443,7 @@
         quarter_kernel,
         [struct((TOK, LOCAL), bf16)] * 2,
         [VMEM] * 3,
-        [VMEM] * 2,
-    )(pick, acts, cots)
+        [VMEM] * 2, us=1.1)(pick, acts, cots)
 
 
 def flat(weight):
@@ -459,15 +488,14 @@
 
 
 def forward_kernel(layer_in, out_matrix, up_next, *refs):
-    messages, (pair, pre, inverse, layer_out, message) = refs[:4], refs[4:]
-    result = forward_step(messages, layer_in, out_matrix, pair, pre, inverse, layer_out)
+    messages, (act, pre, inverse, layer_out, message) = refs[:4], refs[4:]
+    result = forward_step(messages, layer_in, out_matrix, act, pre, inverse, layer_out)
     put_forward(message, result, flat(up_next))
 
 
-def forward_step(messages, layer_in, out_matrix, pair, pre, inverse, layer_out):
+def forward_step(messages, layer_in, out_matrix, act, pre, inverse, layer_out):
     pre_value, act_value, inverse_value = take_forward(summed(messages))
-    pair[:, 0:LOCAL] = layer_in[...]
-    pair[:, LOCAL:] = act_value
+    act[...] = act_value
     pre[...] = pre_value
     inverse[...] = jnp.broadcast_to(inverse_value, (TOK, 128))
     branch = times_t(act_value, flat(out_matrix))
@@ -477,8 +505,8 @@
 
 
 def turn_kernel(layer_in, out_matrix, up_next, out_next, cots, *refs):
-    messages, (pair, pre, inverse, layer_out, message) = refs[:4], refs[4:]
-    result = forward_step(messages, layer_in, out_matrix, pair, pre, inverse, layer_out)
+    messages, (act, pre, inverse, layer_out, message) = refs[:4], refs[4:]
+    result = forward_step(messages, layer_in, out_matrix, act, pre, inverse, layer_out)
     put_forward(message, result, flat(up_next))
     message[:, HID + 128 :] = jnp.dot(
         cots[...], flat(out_next), preferred_element_type=f32
@@ -489,19 +517,20 @@
     messages, refs = refs[:4], refs[4:]
     total = summed(messages)
     if from_forward:
-        grad_out, layer_in, up_matrix, out_next, pair, back, grad_in, message = refs
+        grad_out, layer_in, up_matrix, out_next, back, grad_in, message = refs
         pre_value, act_value, inverse_value = take_forward(total)
-        pair[:, 0:LOCAL] = layer_in[...]
-        pair[:, LOCAL:] = act_value
+        back[:, LEFT:] = act_value
         grad_act = total[:, HID + 128 :] * SCALE_OUT
     else:
-        pre, inverse, grad_out, layer_in, up_matrix, out_next, back, grad_in, message = refs
+        act, pre, inverse, grad_out, layer_in, up_matrix, out_next, back, grad_in, message = refs
+        back[:, LEFT:] = act[...]
         pre_value = pre[...]
         inverse_value = inverse[:, 0:1]
         grad_act = total * SCALE_OUT
     pulled = (grad_act * gelu_slope(pre_value)).astype(bf16)
-    back[:, 0:LOCAL] = grad_out[...]
-    back[:, LOCAL:] = (pulled.astype(f32) * inverse_value).astype(bf16)
+    back[:, 0:LOCAL] = layer_in[...]
+    back[:, LOCAL : 2 * LOCAL] = grad_out[...]
+    back[:, 2 * LOCAL : LEFT] = (pulled.astype(f32) * inverse_value).astype(bf16)
     correction = jnp.sum(pulled.astype(f32) * pre_value, axis=1, keepdims=True) * (1.0 / D)
     grad_norm = times_t(pulled, flat(up_matrix)) * SCALE_IN
     normed = layer_in[...].astype(f32) * inverse_value
@@ -512,46 +541,47 @@
 
 
 def close_kernel(*refs):
-    messages, (pre, inverse, grad_out, back) = refs[:4], refs[4:]
+    messages, (act, pre, inverse, grad_out, layer_in, back) = refs[:4], refs[4:]
     grad_act = summed(messages) * SCALE_OUT
     pulled = (grad_act * gelu_slope(pre[...])).astype(bf16)
-    back[:, 0:LOCAL] = grad_out[...]
-    back[:, LOCAL:] = (pulled.astype(f32) * inverse[:, 0:1]).astype(bf16)
+    back[:, 0:LOCAL] = layer_in[...]
+    back[:, LOCAL : 2 * LOCAL] = grad_out[...]
+    back[:, 2 * LOCAL : LEFT] = (pulled.astype(f32) * inverse[:, 0:1]).astype(bf16)
+    back[:, LEFT:] = act[...]
 
 
 def all_of(message):
     return [message] + [shift_z(message, k) for k in (1, 3, 2)]
 
 
-def products(core, pair, back, pair_sib, back_sib, chosen, store):
-    small = slice(LOCAL, LOCAL + HID)
+def products(core, mine, other, chosen, store):
     half = GROUPS // 2
 
-    def product(left, left_sib, right, right_sib, scale, start):
-        both = jnp.concatenate([left[:, small], left_sib[:, small]], axis=0)
+    def product(left, right, scale, start):
+        both = jnp.concatenate([mine[:, left], other[:, left]], axis=0)
         turned = both.astype(f32).T.astype(bf16)
         for g in range(half):
-            columns = pl.ds(pl.multiple_of((2 * g + core) * 128, 128), 128)
-            chosen[0:TOK, g * 128 : (g + 1) * 128] = right[:, columns]
-            chosen[TOK:, g * 128 : (g + 1) * 128] = right_sib[:, columns]
+            columns = pl.ds(pl.multiple_of(right + (2 * g + core) * 128, 128), 128)
+            chosen[0:TOK, g * 128 : (g + 1) * 128] = mine[:, columns]
+            chosen[TOK:, g * 128 : (g + 1) * 128] = other[:, columns]
         result = jnp.dot(turned, chosen[...], preferred_element_type=f32) * scale
         for g in range(half):
             store(start + g, result[:, g * 128 : (g + 1) * 128].astype(bf16))
 
-    product(back, back_sib, pair, pair_sib, SCALE_IN, 0)
-    product(pair, pair_sib, back, back_sib, SCALE_OUT, half)
+    product(slice(2 * LOCAL, LEFT), 0, SCALE_IN, 0)
+    product(slice(LEFT, LEFT + HID), LOCAL, SCALE_OUT, half)
     for owner in range(2 * half, 16):
         store(owner, jnp.zeros((HID, 128), bf16))
 
 
 def gradient_kernel(x_first, count, place, *refs):
-    ins, outs, (chosen, table) = refs[: 4 * count], refs[4 * count : 4 * count + 4], refs[-2:]
+    ins, outs, (chosen, table) = refs[: 2 * count], refs[2 * count : 2 * count + 4], refs[-2:]
     for n in range(count):
 
         def store(owner, value):
             table[owner, n] = value
 
-        products(place[2], *ins[4 * n : 4 * n + 4], chosen, store)
+        products(place[2], *ins[2 * n : 2 * n + 2], chosen, store)
     for k in range(4):
         for j in range(4):
             if x_first:
@@ -579,11 +609,10 @@
     chunks = call(
         functools.partial(gradient_kernel, x_first, count),
         [struct((4, count, HID, 128), bf16)] * 4,
-        [SMEM] + [VMEM] * (4 * count),
+        [SMEM] + [VMEM] * (2 * count),
         [VMEM] * 4,
         [pltpu.VMEM((2 * TOK, LOCAL // 2), bf16), pltpu.VMEM((16, count, HID, 128), bf16)],
-        after=after,
-    )(place, *[v for section in sections for v in section])
+        after=after, us=3.3)(place, *[v for section in sections for v in section])
     step = (1, 0) if x_first else (0, 1)
     return [chunks[0]] + [shift_xy(chunks[k], k * step[0], k * step[1]) for k in (1, 2, 3)]
 
@@ -596,8 +625,7 @@
         [struct((count, HID, 128), f32)] + [struct((count, HID, 128), bf16)] * 3,
         [SMEM] + [VMEM] * (4 * len(parts)),
         [VMEM] * 4,
-        after=after,
-    )(place, *[v for part in parts for v in part])
+        after=after, us=1.4)(place, *[v for part in parts for v in part])
     step = (0, 1) if x_first else (1, 0)
     return [kept] + [shift_xy(sends[k - 1], k * step[0], k * step[1]) for k in (1, 2, 3)]
 
@@ -687,34 +715,32 @@
         split_moments_kernel,
         [struct((2, OWN, PIECE, HID), bf16)] * 4,
         [SMEM, VMEM, VMEM],
-        [VMEM] * 4,
-    )(place, old_first[0], old_second[0])
+        [VMEM] * 4, us=1.3)(place, old_first[0], old_second[0])
     pieces = [split[0]] + [shift_z(split[k], k) for k in (1, 2, 3)]
 
-    weights, labels, arrivals = route_blocks(
-        old_blocks, send_slot, send_dest, send_block, moment_dest
+    weights, labels, arrivals, layer_0, cots = route_blocks(
+        place, acts_in, cotangent, old_blocks, send_slot, send_dest, send_block, moment_dest
     )
     table = lax.dynamic_slice_in_dim(labels, me_r * 4, 4, 0)[:, 9:13]
     distance = (me_z - jnp.arange(SECTIONS, dtype=jnp.int32)) % 4
     held = (distance[:, None] * OWN + jnp.arange(OWN, dtype=jnp.int32)[None, :]).reshape(-1)
     slots = jnp.arange(SECTIONS * OWN, dtype=jnp.int32)
     source = jnp.sum(jnp.where(table.reshape(1, -1) == slots[:, None], held[None, :], 0), axis=1)
-    layer_0, cots = quarter(acts_in, cotangent, me_z)
     message = call(
-        open_kernel, struct((TOK, HID + 128), bf16), [VMEM] * 2, VMEM
-    )(layer_0, weights[0][0])
+        open_kernel, struct((TOK, HID + 128), bf16), [VMEM] * 2, VMEM, us=0.3)(layer_0, weights[0][0])
     layers = [layer_0]
-    pairs, pairs_sib, pres, inverses = [], [], [], []
-    wide = struct((TOK, LOCAL + HID), bf16)
+    acts, pres, inverses = [], [], []
+    wide = struct((TOK, LEFT + HID), bf16)
+    short = struct((TOK, HID), bf16)
     narrow = struct((TOK, LOCAL), bf16)
     for s in range(SECTIONS - 1):
         messages = all_of(message)
         turn = s == SECTIONS - 2
         extra = (weights[s + 1][1], cots) if turn else ()
-        pair, pre, inverse, layer, message = call(
+        act, pre, inverse, layer, message = call(
             turn_kernel if turn else forward_kernel,
             [
-                wide,
+                short,
                 struct((TOK, HID), f32),
                 struct((TOK, 128), f32),
                 narrow,
@@ -722,11 +748,10 @@
             ],
             [VMEM] * (7 + len(extra)),
             [VMEM] * 5,
-            after=pairs_sib[-1:] if s else pieces[1:],
+            after=() if s else pieces[1:],
         )(layers[s], weights[s][1], weights[s + 1][0], *extra, *messages)
         layers.append(layer)
-        pairs.append(pair)
-        pairs_sib.append(from_sibling(pair))
+        acts.append(act)
         pres.append(pre)
         inverses.append(inverse)
 
@@ -739,42 +764,42 @@
             pltpu.VMEM((4, 2, OWN, PIECE, HID), bf16),
             pltpu.VMEM((4, OWN, PIECE, HID), bf16),
             pltpu.SemaphoreType.DMA,
-        ],
-    )(place, source, *arrivals, *pieces)
+        ], us=1.6)(place, source, *arrivals, *pieces)
     owned = [ordered[0]] + [shift_z(ordered[k], k) for k in (1, 2, 3)]
 
     grad = cots
-    ready, parts = [None] * SECTIONS, [None] * SECTIONS
-    after = pairs_sib[-1:]
+    ready = [None] * SECTIONS
+    after = []
     for s in reversed(range(SECTIONS)):
         messages = all_of(message)
         if s == SECTIONS - 1:
-            pair, back, grad, message = call(
+            back, grad, message = call(
                 functools.partial(backward_kernel, True),
-                [wide, wide, narrow, struct((TOK, HID), bf16)],
+                [wide, narrow, short],
                 [VMEM] * 8,
-                [VMEM] * 4,
+                [VMEM] * 3,
                 after=after,
             )(*messages, grad, layers[s], weights[s][0], weights[s - 1][1])
-            pairs.append(pair)
-            pairs_sib.append(from_sibling(pair))
         elif s > 0:
             back, grad, message = call(
                 functools.partial(backward_kernel, False),
-                [wide, narrow, struct((TOK, HID), bf16)],
-                [VMEM] * 10,
+                [wide, narrow, short],
+                [VMEM] * 11,
                 [VMEM] * 3,
                 after=after,
-            )(*messages, pres[s], inverses[s], grad, layers[s], weights[s][0], weights[s - 1][1])
+            )(
+                *messages, acts[s], pres[s], inverses[s], grad, layers[s], weights[s][0],
+                weights[s - 1][1]
+            )
         else:
-            back = call(close_kernel, wide, [VMEM] * 7, VMEM, after=after)(
-                *messages, pres[0], inverses[0], grad
+            back = call(close_kernel, wide, [VMEM] * 9, VMEM, after=after)(
+                *messages, acts[0], pres[0], inverses[0], grad, layers[0]
             )
-        ready[s] = (pairs[s], back, pairs_sib[s], from_sibling(back))
+        ready[s] = (back, from_sibling(back))
         if s == 3:
             after = []
         elif s == 2:
-            after = [ready[2][3], ready[3][3]]
+            after = [ready[2][1], ready[3][1]]
         elif s == 1:
             odd = first_half(True, place, [ready[3], ready[1]])
             after = odd[:1]
@@ -788,8 +813,7 @@
         [struct((HID, 128), f32)] + [struct((HID, 128), bf16)] * 3,
         [SMEM] + [VMEM] * 8,
         [VMEM] * 4,
-        [pltpu.VMEM((SECTIONS, HID, 128), f32)],
-    )(place, *across, *along)
+        [pltpu.VMEM((SECTIONS, HID, 128), f32)], us=0.7)(place, *across, *along)
     gradients = [kept] + [shift_z(sends[k - 1], k) for k in (1, 2, 3)]
     new_weight, new_first, new_second = call(
         adam_kernel,
@@ -799,8 +823,7 @@
             struct((OWN, 128, HID), f32),
         ],
         [SMEM] + [VMEM] * 8,
-        [VMEM] * 3,
-    )(place, *gradients, *owned)
+        [VMEM] * 3, us=2.1)(place, *gradients, *owned)
     return (new_weight[None], new_first[None], new_second[None])
 
 

time: 317 us -> 310 us (0.978)
  waiting for transfers between devices: 157 us -> 148 us
  starting transfers between devices: 97.7 us -> 102 us
  other arithmetic: 6.18 us -> 2.78 us
    all_to_all x1, waiting for transfers between devices: 7.43 us -> 0.73 us  [route_blocks(): got = lax.all_to_all(labels, EVERY, 0, 0, tiled=True)]
    all_to_all x1, starting transfers between devices: 6.35 us -> 11.7 us  [route_blocks(): lax.all_to_all(buffer.reshape(DEVICES, CHUNK, HID), EVERY, 0, 0, tiled=True)]
    ppermute x10 -> x6, waiting for transfers between devices: 1 us -> 6.32 us  [from_sibling(): return lax.ppermute(block, 'replica', [(i, i ^ 1) for i in range(REPLICAS)])]
    all_to_all x1, waiting for transfers between devices: 104 us -> 100 us  [route_blocks(): lax.all_to_all(buffer.reshape(DEVICES, CHUNK, HID), EVERY, 0, 0, tiled=True)]
    ppermute x1, waiting for transfers between devices: 3.69 us -> 0.01 us  [spread(): return lax.ppermute(block, names, route)]
    ppermute x12, starting transfers between devices: 29.6 us -> 26 us  [shift_xy(): return lax.ppermute(block, 'replica', route)]
    pallas_call x30 -> x32, Pallas kernels: 46 us -> 48.6 us  [call(): return lambda *arrays: run(*after, *arrays)]
  transfers between devices with their start and end apart: 57 -> 53, of which waited for: 24 -> 20; matrix products, arithmetic and copies ran while one was open for 2% -> 1% of each run, Pallas kernels for 12% -> 12%
where the time goes in v3:
time: 310 us
  waiting for transfers between devices  148 us (48%)
  starting transfers between devices  102 us (33%)
  Pallas kernels  48.6 us (16%)
  local copies, waits for them, and re-layouts  5.91 us (2%)
    all_to_all x1, waiting for transfers between devices, route_blocks(): lax.all_to_all(buffer.reshape(DEVICES, CHUNK, HID), EVERY, 0, 0, tiled=True)  100 us
    pallas_call x32, Pallas kernels, call(): return lambda *arrays: run(*after, *arrays)  48.6 us
    ppermute x30, starting transfers between devices, shift_z(): lax.ppermute(block, 'section', [(i, (i + step) % 4) for i in range(4)])  46.5 us
    ppermute x12, starting transfers between devices, shift_xy(): return lax.ppermute(block, 'replica', route)  26 us
    ppermute x30, waiting for transfers between devices, shift_z(): lax.ppermute(block, 'section', [(i, (i + step) % 4) for i in range(4)])  23 us
    ppermute x12, waiting for transfers between devices, shift_xy(): return lax.ppermute(block, 'replica', route)  17.9 us
    all_to_all x1, starting transfers between devices, route_blocks(): got = lax.all_to_all(labels, EVERY, 0, 0, tiled=True)  12 us
    all_to_all x1, starting transfers between devices, route_blocks(): lax.all_to_all(buffer.reshape(DEVICES, CHUNK, HID), EVERY, 0, 0, tiled=True)  11.7 us
  transfers between devices with their start and end apart: 53, of which 20 were waited for; matrix products, arithmetic and copies ran while one was open for 1% of the time, Pallas kernels for 12%

profile of v3, /device:TPU:8, one launch (start us, length us, event | category | flops | bytes accessed | tf_op | source)
XLA Modules:
  0.0 310.1 jit_solution(16258464684610174881)
XLA Ops:
  4.3 4.6 %collective-permute-done.3.refs_0_ = s32[8,128]{1,0:T(8,128)S(1)} collective-permute-done((s32[8,128]{1,0:T(8,128)S(1)}, s32[8,128]{1,0:T(8,128)S(1)}, u32[]{:S(2)}, u32[]{:S(2)}) %collective-permute-start.3) | collective-permute-done | bytes 4128 | tf_op jit(solution)/shard_map/ppermute | solution.py:110
  16.5 12.0 %all-to-all-start.1 = ((s32[128,1,16]{2,1,0:T(1,128)}), s32[128,1,16]{2,1,0:T(1,128)S(1)}, u32[]{:S(2)}, u32[]{:S(2)}) async-start(s32[128,1,16]{2,1,0:T(1,128)} %bitcast.10), calls=%async_computation.1 | async-start | bytes 131072 | tf_op jit(solution)/shard_map/all_to_all | solution.py:385
  28.5 7.3 %shard_map.118.refs_6_ = bf16[32,4,144,256]{3,2,1,0:T(8,128)(2,1)} custom-call(s32[8,128]{1,0:T(8,128)S(1)} %get-tuple-element.107.refs_0_.refs_1_, bf16[112,4,32,256]{3,2,1,0:T(8,128)(2,1)} %bitcast.37), custom_call_target="tpu_custom_call" | custom-call | bytes 25160000 | tf_op jit(solution)/shard_map/pallas_call | solution.py:70
  39.3 11.7 %all-to-all-start.2 = ((bf16[128,144,256]{2,1,0:T(8,128)(2,1)}), bf16[128,144,256]{2,1,0:T(8,128)(2,1)}, u32[]{:S(2)}, u32[]{:S(2)}) async-start(bf16[128,144,256]{2,1,0:T(8,128)(2,1)} %bitcast.39), calls=%async_computation.2 | async-start | bytes 18874368 | tf_op jit(solution)/shard_map/all_to_all | solution.py:400
  53.3 3.2 %collective-permute-start.1 = (bf16[2,4,32,256]{3,2,1,0:T(8,128)(2,1)S(1)}, bf16[2,4,32,256]{3,2,1,0:T(8,128)(2,1)S(1)}, u32[]{:S(2)}, u32[]{:S(2)}) collective-permute-start(bf16[2,4,32,256]{3,2,1,0:T(8,128)(2,1)S(1)} %get-tuple-element.88), channel_id=1, source_target_pairs={{0,2},{1,3},{2,0},{3,1},{4,6},{5,7},{6,4},{7,5},{8,10},{9,11},{10,... | collective-permute-start | bytes 393224 | tf_op jit(solution)/shard_map/ppermute | solution.py:88
  65.6 100.0 %all-to-all-done.2.refs_2_.refs_4_ = bf16[128,144,256]{2,1,0:T(8,128)(2,1)} async-done(((bf16[128,144,256]{2,1,0:T(8,128)(2,1)}), bf16[128,144,256]{2,1,0:T(8,128)(2,1)}, u32[]{:S(2)}, u32[]{:S(2)}) %all-to-all-start.2) | async-done | bytes 9437216 | tf_op jit(solution)/shard_map/all_to_all | solution.py:400
  168.5 4.5 %collective-permute-start.10 = (bf16[128,384]{1,0:T(8,128)(2,1)S(1)}, bf16[128,384]{1,0:T(8,128)(2,1)S(1)}, u32[]{:S(2)}, u32[]{:S(2)}) collective-permute-start(bf16[128,384]{1,0:T(8,128)(2,1)S(1)} %shard_map.123.refs_6_), channel_id=1, source_target_pairs={{0,2},{1,3},{2,0},{3,1},{4,6},{5,7},{6,4},{7,5},{8,10},{9,11},{10,... | collective-permute-start | bytes 294920 | tf_op jit(solution)/shard_map/ppermute | solution.py:88
  173.0 3.2 %collective-permute-start.9 = (bf16[128,384]{1,0:T(8,128)(2,1)S(1)}, bf16[128,384]{1,0:T(8,128)(2,1)S(1)}, u32[]{:S(2)}, u32[]{:S(2)}) collective-permute-start(bf16[128,384]{1,0:T(8,128)(2,1)S(1)} %shard_map.123.refs_6_), channel_id=1, source_target_pairs={{0,3},{1,0},{2,1},{3,2},{4,7},{5,4},{6,5},{7,6},{8,11},{9,8},{10,9... | collective-permute-start | bytes 294920 | tf_op jit(solution)/shard_map/ppermute | solution.py:88
  181.1 3.2 %collective-permute-start.12 = (bf16[128,384]{1,0:T(8,128)(2,1)S(1)}, bf16[128,384]{1,0:T(8,128)(2,1)S(1)}, u32[]{:S(2)}, u32[]{:S(2)}) collective-permute-start(bf16[128,384]{1,0:T(8,128)(2,1)S(1)} %get-tuple-element.109.refs_3_), channel_id=1, source_target_pairs={{0,3},{1,0},{2,1},{3,2},{4,7},{5,4},{6,5},{7,6},{8,11},{9,8},{10,9... | collective-permute-start | bytes 294920 | tf_op jit(solution)/shard_map/ppermute | solution.py:88
  188.3 2.1 collective-permute-done.13.refs_6_
  191.3 3.2 %collective-permute-start.15 = (bf16[128,384]{1,0:T(8,128)(2,1)S(1)}, bf16[128,384]{1,0:T(8,128)(2,1)S(1)}, u32[]{:S(2)}, u32[]{:S(2)}) collective-permute-start(bf16[128,384]{1,0:T(8,128)(2,1)S(1)} %get-tuple-element.112.refs_5_), channel_id=1, source_target_pairs={{0,3},{1,0},{2,1},{3,2},{4,7},{5,4},{6,5},{7,6},{8,11},{9,8},{10,9... | collective-permute-start | bytes 294920 | tf_op jit(solution)/shard_map/ppermute | solution.py:88
  202.3 2.5 collective-permute-start.18
  204.8 2.2 collective-permute-start.19
  209.4 2.2 collective-permute-done.19.refs_3_
  213.0 2.9 collective-permute-start.21
  218.1 3.5 %collective-permute-done.22.refs_3_ = bf16[128,256]{1,0:T(8,128)(2,1)S(1)} collective-permute-done((bf16[128,256]{1,0:T(8,128)(2,1)S(1)}, bf16[128,256]{1,0:T(8,128)(2,1)S(1)}, u32[]{:S(2)}, u32[]{:S(2)}) %collective-permute-start.22) | collective-permute-done | bytes 65568 | tf_op jit(solution)/shard_map/ppermute | solution.py:88
  222.7 3.2 %collective-permute-start.26 = (bf16[128,256]{1,0:T(8,128)(2,1)S(1)}, bf16[128,256]{1,0:T(8,128)(2,1)S(1)}, u32[]{:S(2)}, u32[]{:S(2)}) collective-permute-start(bf16[128,256]{1,0:T(8,128)(2,1)S(1)} %get-tuple-element.122.refs_2_), channel_id=1, source_target_pairs={{0,3},{1,0},{2,1},{3,2},{4,7},{5,4},{6,5},{7,6},{8,11},{9,8},{10,9... | collective-permute-start | bytes 196616 | tf_op jit(solution)/shard_map/ppermute | solution.py:88
  226.2 2.1 collective-permute-done.25.refs_3_
  229.0 2.7 collective-permute-done.27.refs_5_
  232.7 3.2 %collective-permute-start.30 = (bf16[128,256]{1,0:T(8,128)(2,1)S(1)}, bf16[128,256]{1,0:T(8,128)(2,1)S(1)}, u32[]{:S(2)}, u32[]{:S(2)}) collective-permute-start(bf16[128,256]{1,0:T(8,128)(2,1)S(1)} %get-tuple-element.129.refs_1_), channel_id=1, source_target_pairs={{0,3},{1,0},{2,1},{3,2},{4,7},{5,4},{6,5},{7,6},{8,11},{9,8},{10,9... | collective-permute-start | bytes 196616 | tf_op jit(solution)/shard_map/ppermute | solution.py:88
  235.9 3.2 %shard_map.135 = (bf16[4,2,256,128]{3,2,1,0:T(8,128)(2,1)S(1)}, bf16[4,2,256,128]{3,2,1,0:T(8,128)(2,1)S(1)}, bf16[4,2,256,128]{3,2,1,0:T(8,128)(2,1)}, bf16[4,2,256,128]{3,2,1,0:T(8,128)(2,1)}) custom-call(s32[5]{0:T(128)S(1)} %copy-done.4, bf16[128,4096]{1,0:T(8,128)(2,1)S(1)} %get-tuple-element.121.refs_1_, ...), custom_call_target="tpu_custom_call" | custom-call | bytes 11220000 | tf_op jit(solution)/shard_map/pallas_call | solution.py:70
  239.1 2.6 collective-permute-done.31.refs_4_
  245.6 3.4 %shard_map.137 = (bf16[4,2,256,128]{3,2,1,0:T(8,128)(2,1)S(1)}, bf16[4,2,256,128]{3,2,1,0:T(8,128)(2,1)}, bf16[4,2,256,128]{3,2,1,0:T(8,128)(2,1)}, bf16[4,2,256,128]{3,2,1,0:T(8,128)(2,1)}) custom-call(s32[5]{0:T(128)S(1)} %copy-done.4, bf16[128,4096]{1,0:T(8,128)(2,1)S(1)} %get-tuple-element.120.refs_1_, ...), custom_call_target="tpu_custom_call" | custom-call | bytes 11220000 | tf_op jit(solution)/shard_map/pallas_call | solution.py:70
  249.0 4.3 %collective-permute-start.39 = (bf16[4,2,256,128]{3,2,1,0:T(8,128)(2,1)}, bf16[4,2,256,128]{3,2,1,0:T(8,128)(2,1)S(1)}, u32[]{:S(2)}, u32[]{:S(2)}) collective-permute-start(bf16[4,2,256,128]{3,2,1,0:T(8,128)(2,1)} %get-tuple-element.142), channel_id=1, source_target_pairs={{0,8},{4,12},{8,16},{12,20},{16,24},{20,28},{24,0},{28,4},{32,40},... | collective-permute-start | bytes 1572872 | tf_op jit(solution)/shard_map/ppermute | solution.py:84
  253.3 5.0 %collective-permute-start.40 = (bf16[4,2,256,128]{3,2,1,0:T(8,128)(2,1)}, bf16[4,2,256,128]{3,2,1,0:T(8,128)(2,1)S(1)}, u32[]{:S(2)}, u32[]{:S(2)}) collective-permute-start(bf16[4,2,256,128]{3,2,1,0:T(8,128)(2,1)} %get-tuple-element.143), channel_id=1, source_target_pairs={{0,16},{4,20},{8,24},{12,28},{16,0},{20,4},{24,8},{28,12},{32,48},... | collective-permute-start | bytes 1572872 | tf_op jit(solution)/shard_map/ppermute | solution.py:84
  258.3 10.5 %collective-permute-done.33.refs_3_ = bf16[4,2,256,128]{3,2,1,0:T(8,128)(2,1)S(1)} collective-permute-done((bf16[4,2,256,128]{3,2,1,0:T(8,128)(2,1)S(1)}, bf16[4,2,256,128]{3,2,1,0:T(8,128)(2,1)S(1)}, u32[]{:S(2)}, u32[]{:S(2)}) %collective-permute-start.33) | collective-permute-done | bytes 524320 | tf_op jit(solution)/shard_map/ppermute | solution.py:84
  271.3 3.4 %collective-permute-start.36 = (bf16[2,256,128]{2,1,0:T(8,128)(2,1)S(1)}, bf16[2,256,128]{2,1,0:T(8,128)(2,1)S(1)}, u32[]{:S(2)}, u32[]{:S(2)}) collective-permute-start(bf16[2,256,128]{2,1,0:T(8,128)(2,1)S(1)} %get-tuple-element.139), channel_id=1, source_target_pairs={{0,8},{4,12},{8,16},{12,20},{16,24},{20,28},{24,0},{28,4},{32,40},... | collective-permute-start | bytes 393224 | tf_op jit(solution)/shard_map/ppermute | solution.py:84
  274.7 4.9 %collective-permute-start.37 = (bf16[2,256,128]{2,1,0:T(8,128)(2,1)S(1)}, bf16[2,256,128]{2,1,0:T(8,128)(2,1)S(1)}, u32[]{:S(2)}, u32[]{:S(2)}) collective-permute-start(bf16[2,256,128]{2,1,0:T(8,128)(2,1)S(1)} %get-tuple-element.140), channel_id=1, source_target_pairs={{0,16},{4,20},{8,24},{12,28},{16,0},{20,4},{24,8},{28,12},{32,48},... | collective-permute-start | bytes 393224 | tf_op jit(solution)/shard_map/ppermute | solution.py:84
  280.9 5.7 %collective-permute-done.41.refs_5_ = bf16[4,2,256,128]{3,2,1,0:T(8,128)(2,1)} collective-permute-done((bf16[4,2,256,128]{3,2,1,0:T(8,128)(2,1)}, bf16[4,2,256,128]{3,2,1,0:T(8,128)(2,1)}, u32[]{:S(2)}, u32[]{:S(2)}) %collective-permute-start.41) | collective-permute-done | bytes 524320 | tf_op jit(solution)/shard_map/ppermute | solution.py:84
  290.0 3.3 %collective-permute-start.44 = (bf16[2,256,128]{2,1,0:T(8,128)(2,1)S(1)}, bf16[2,256,128]{2,1,0:T(8,128)(2,1)S(1)}, u32[]{:S(2)}, u32[]{:S(2)}) collective-permute-start(bf16[2,256,128]{2,1,0:T(8,128)(2,1)S(1)} %get-tuple-element.148), channel_id=1, source_target_pairs={{0,96},{4,100},{8,104},{12,108},{16,112},{20,116},{24,120},{28,124... | collective-permute-start | bytes 393224 | tf_op jit(solution)/shard_map/ppermute | solution.py:84
  293.3 2.4 collective-permute-start.49
  300.0 3.8 %collective-permute-start.46 = (bf16[256,128]{1,0:T(8,128)(2,1)S(1)}, bf16[256,128]{1,0:T(8,128)(2,1)S(1)}, u32[]{:S(2)}, u32[]{:S(2)}) collective-permute-start(bf16[256,128]{1,0:T(8,128)(2,1)S(1)} %get-tuple-element.151), channel_id=1, source_target_pairs={{0,2},{1,3},{2,0},{3,1},{4,6},{5,7},{6,4},{7,5},{8,10},{9,11},{10,... | collective-permute-start | bytes 196616 | tf_op jit(solution)/shard_map/ppermute | solution.py:88
  (151 shorter events, 76.0 us)
Async XLA Ops:
  3.0 7.6 %collective-permute-start.4 = (bf16[4,32,4,16,256]{4,3,2,1,0:T(8,128)(2,1)}, bf16[4,32,4,16,256]{4,3,2,1,0:T(8,128)(2,1)}, u32[]{:S(2)}, u32[]{:S(2)}) collective-permute-start(bf16[4,32,4,16,256]{4,3,2,1,0:T(8,128)(2,1)} %shard_map.115.refs_0_), channel_id=1, source_target_pairs={{0,4},{4,0},{8,12},{12,8},{16,20},{20,16},{24,28},{28,24},{32,36},... | collective-permute-start | bytes 12582920 | tf_op jit(solution)/shard_map/ppermute | solution.py:110
  11.4 25.7 %collective-permute-start.5 = (bf16[32,4,16,256]{3,2,1,0:T(8,128)(2,1)}, bf16[32,4,16,256]{3,2,1,0:T(8,128)(2,1)S(1)}, u32[]{:S(2)}, u32[]{:S(2)}) collective-permute-start(bf16[32,4,16,256]{3,2,1,0:T(8,128)(2,1)} %get-tuple-element.100), channel_id=1, source_target_pairs={{0,32},{4,100},{8,40},{12,108},{16,48},{20,116},{24,56},{28,124},{... | collective-permute-start | bytes 3145736 | tf_op jit(solution)/shard_map/ppermute | solution.py:106
  13.0 24.2 %collective-permute-start.6 = (bf16[32,4,16,256]{3,2,1,0:T(8,128)(2,1)}, bf16[32,4,16,256]{3,2,1,0:T(8,128)(2,1)}, u32[]{:S(2)}, u32[]{:S(2)}) collective-permute-start(bf16[32,4,16,256]{3,2,1,0:T(8,128)(2,1)} %get-tuple-element.101), channel_id=1, source_target_pairs={{0,8},{4,28},{8,16},{12,4},{16,24},{20,12},{24,0},{28,20},{32,40},... | collective-permute-start | bytes 3145736 | tf_op jit(solution)/shard_map/ppermute | solution.py:106
  14.5 22.6 %collective-permute-start.7 = (bf16[32,4,16,256]{3,2,1,0:T(8,128)(2,1)}, bf16[32,4,16,256]{3,2,1,0:T(8,128)(2,1)}, u32[]{:S(2)}, u32[]{:S(2)}) collective-permute-start(bf16[32,4,16,256]{3,2,1,0:T(8,128)(2,1)} %get-tuple-element.102), channel_id=1, source_target_pairs={{0,1},{1,2},{2,3},{3,0},{4,7},{5,4},{6,5},{7,6},{8,9},{9,10},{10,1... | collective-permute-start | bytes 3145736 | tf_op jit(solution)/shard_map/ppermute | solution.py:98
  16.5 20.7 %all-to-all-start.1 = ((s32[128,1,16]{2,1,0:T(1,128)}), s32[128,1,16]{2,1,0:T(1,128)S(1)}, u32[]{:S(2)}, u32[]{:S(2)}) async-start(s32[128,1,16]{2,1,0:T(1,128)} %bitcast.10), calls=%async_computation.1 | async-start | bytes 131072 | tf_op jit(solution)/shard_map/all_to_all | solution.py:385
  39.3 126.3 %all-to-all-start.2 = ((bf16[128,144,256]{2,1,0:T(8,128)(2,1)}), bf16[128,144,256]{2,1,0:T(8,128)(2,1)}, u32[]{:S(2)}, u32[]{:S(2)}) async-start(bf16[128,144,256]{2,1,0:T(8,128)(2,1)} %bitcast.39), calls=%async_computation.2 | async-start | bytes 18874368 | tf_op jit(solution)/shard_map/all_to_all | solution.py:400
  51.6 121.4 %collective-permute-start = (bf16[2,4,32,256]{3,2,1,0:T(8,128)(2,1)S(1)}, bf16[2,4,32,256]{3,2,1,0:T(8,128)(2,1)S(1)}, u32[]{:S(2)}, u32[]{:S(2)}) collective-permute-start(bf16[2,4,32,256]{3,2,1,0:T(8,128)(2,1)S(1)} %get-tuple-element.87), channel_id=1, source_target_pairs={{0,1},{1,2},{2,3},{3,0},{4,5},{5,6},{6,7},{7,4},{8,9},{9,10},{10,1... | collective-permute-start | bytes 393224 | tf_op jit(solution)/shard_map/ppermute | solution.py:88
  53.3 126.8 %collective-permute-start.1 = (bf16[2,4,32,256]{3,2,1,0:T(8,128)(2,1)S(1)}, bf16[2,4,32,256]{3,2,1,0:T(8,128)(2,1)S(1)}, u32[]{:S(2)}, u32[]{:S(2)}) collective-permute-start(bf16[2,4,32,256]{3,2,1,0:T(8,128)(2,1)S(1)} %get-tuple-element.88), channel_id=1, source_target_pairs={{0,2},{1,3},{2,0},{3,1},{4,6},{5,7},{6,4},{7,5},{8,10},{9,11},{10,... | collective-permute-start | bytes 393224 | tf_op jit(solution)/shard_map/ppermute | solution.py:88
  56.5 123.6 %collective-permute-start.2 = (bf16[2,4,32,256]{3,2,1,0:T(8,128)(2,1)S(1)}, bf16[2,4,32,256]{3,2,1,0:T(8,128)(2,1)S(1)}, u32[]{:S(2)}, u32[]{:S(2)}) collective-permute-start(bf16[2,4,32,256]{3,2,1,0:T(8,128)(2,1)S(1)} %get-tuple-element.89), channel_id=1, source_target_pairs={{0,3},{1,0},{2,1},{3,2},{4,7},{5,4},{6,5},{7,6},{8,11},{9,8},{10,9... | collective-permute-start | bytes 393224 | tf_op jit(solution)/shard_map/ppermute | solution.py:88
  168.5 11.7 %collective-permute-start.10 = (bf16[128,384]{1,0:T(8,128)(2,1)S(1)}, bf16[128,384]{1,0:T(8,128)(2,1)S(1)}, u32[]{:S(2)}, u32[]{:S(2)}) collective-permute-start(bf16[128,384]{1,0:T(8,128)(2,1)S(1)} %shard_map.123.refs_6_), channel_id=1, source_target_pairs={{0,2},{1,3},{2,0},{3,1},{4,6},{5,7},{6,4},{7,5},{8,10},{9,11},{10,... | collective-permute-start | bytes 294920 | tf_op jit(solution)/shard_map/ppermute | solution.py:88
  173.0 7.2 %collective-permute-start.9 = (bf16[128,384]{1,0:T(8,128)(2,1)S(1)}, bf16[128,384]{1,0:T(8,128)(2,1)S(1)}, u32[]{:S(2)}, u32[]{:S(2)}) collective-permute-start(bf16[128,384]{1,0:T(8,128)(2,1)S(1)} %shard_map.123.refs_6_), channel_id=1, source_target_pairs={{0,3},{1,0},{2,1},{3,2},{4,7},{5,4},{6,5},{7,6},{8,11},{9,8},{10,9... | collective-permute-start | bytes 294920 | tf_op jit(solution)/shard_map/ppermute | solution.py:88
  181.0 7.3 %collective-permute-start.11 = (bf16[128,384]{1,0:T(8,128)(2,1)S(1)}, bf16[128,384]{1,0:T(8,128)(2,1)S(1)}, u32[]{:S(2)}, u32[]{:S(2)}) collective-permute-start(bf16[128,384]{1,0:T(8,128)(2,1)S(1)} %get-tuple-element.109.refs_3_), channel_id=1, source_target_pairs={{0,1},{1,2},{2,3},{3,0},{4,5},{5,6},{6,7},{7,4},{8,9},{9,10},{10,1... | collective-permute-start | bytes 294920 | tf_op jit(solution)/shard_map/ppermute | solution.py:88
  181.1 7.3 %collective-permute-start.12 = (bf16[128,384]{1,0:T(8,128)(2,1)S(1)}, bf16[128,384]{1,0:T(8,128)(2,1)S(1)}, u32[]{:S(2)}, u32[]{:S(2)}) collective-permute-start(bf16[128,384]{1,0:T(8,128)(2,1)S(1)} %get-tuple-element.109.refs_3_), channel_id=1, source_target_pairs={{0,3},{1,0},{2,1},{3,2},{4,7},{5,4},{6,5},{7,6},{8,11},{9,8},{10,9... | collective-permute-start | bytes 294920 | tf_op jit(solution)/shard_map/ppermute | solution.py:88
  191.2 9.4 %collective-permute-start.14 = (bf16[128,384]{1,0:T(8,128)(2,1)S(1)}, bf16[128,384]{1,0:T(8,128)(2,1)S(1)}, u32[]{:S(2)}, u32[]{:S(2)}) collective-permute-start(bf16[128,384]{1,0:T(8,128)(2,1)S(1)} %get-tuple-element.112.refs_5_), channel_id=1, source_target_pairs={{0,1},{1,2},{2,3},{3,0},{4,5},{5,6},{6,7},{7,4},{8,9},{9,10},{10,1... | collective-permute-start | bytes 294920 | tf_op jit(solution)/shard_map/ppermute | solution.py:88
  191.3 9.3 %collective-permute-start.15 = (bf16[128,384]{1,0:T(8,128)(2,1)S(1)}, bf16[128,384]{1,0:T(8,128)(2,1)S(1)}, u32[]{:S(2)}, u32[]{:S(2)}) collective-permute-start(bf16[128,384]{1,0:T(8,128)(2,1)S(1)} %get-tuple-element.112.refs_5_), channel_id=1, source_target_pairs={{0,3},{1,0},{2,1},{3,2},{4,7},{5,4},{6,5},{7,6},{8,11},{9,8},{10,9... | collective-permute-start | bytes 294920 | tf_op jit(solution)/shard_map/ppermute | solution.py:88
  201.5 7.5 %collective-permute-start.17 = (bf16[128,640]{1,0:T(8,128)(2,1)S(1)}, bf16[128,640]{1,0:T(8,128)(2,1)S(1)}, u32[]{:S(2)}, u32[]{:S(2)}) collective-permute-start(bf16[128,640]{1,0:T(8,128)(2,1)S(1)} %get-tuple-element.113.refs_0_), channel_id=1, source_target_pairs={{0,1},{1,2},{2,3},{3,0},{4,5},{5,6},{6,7},{7,4},{8,9},{9,10},{10,1... | collective-permute-start | bytes 491528 | tf_op jit(solution)/shard_map/ppermute | solution.py:88
  217.4 14.3 %collective-permute-start.24 = (bf16[128,4096]{1,0:T(8,128)(2,1)S(1)}, bf16[128,4096]{1,0:T(8,128)(2,1)S(1)}, u32[]{:S(2)}, u32[]{:S(2)}) collective-permute-start(bf16[128,4096]{1,0:T(8,128)(2,1)S(1)} %get-tuple-element.121.refs_1_), channel_id=1, source_target_pairs={{0,4},{4,0},{8,12},{12,8},{16,20},{20,16},{24,28},{28,24},{32,36},... | collective-permute-start | bytes 3145736 | tf_op jit(solution)/shard_map/ppermute | solution.py:110
  222.5 9.2 %collective-permute-start.23 = (bf16[128,4096]{1,0:T(8,128)(2,1)S(1)}, bf16[128,4096]{1,0:T(8,128)(2,1)S(1)}, u32[]{:S(2)}, u32[]{:S(2)}) collective-permute-start(bf16[128,4096]{1,0:T(8,128)(2,1)S(1)} %get-tuple-element.120.refs_1_), channel_id=1, source_target_pairs={{0,4},{4,0},{8,12},{12,8},{16,20},{20,16},{24,28},{28,24},{32,36},... | collective-permute-start | bytes 3145736 | tf_op jit(solution)/shard_map/ppermute | solution.py:110
  242.0 26.8 %collective-permute-start.33 = (bf16[4,2,256,128]{3,2,1,0:T(8,128)(2,1)S(1)}, bf16[4,2,256,128]{3,2,1,0:T(8,128)(2,1)S(1)}, u32[]{:S(2)}, u32[]{:S(2)}) collective-permute-start(bf16[4,2,256,128]{3,2,1,0:T(8,128)(2,1)S(1)} %get-tuple-element.135), channel_id=1, source_target_pairs={{0,32},{4,36},{8,40},{12,44},{16,48},{20,52},{24,56},{28,60},{32,6... | collective-permute-start | bytes 1572872 | tf_op jit(solution)/shard_map/ppermute | solution.py:84
  242.9 27.0 %collective-permute-start.34 = (bf16[4,2,256,128]{3,2,1,0:T(8,128)(2,1)}, bf16[4,2,256,128]{3,2,1,0:T(8,128)(2,1)}, u32[]{:S(2)}, u32[]{:S(2)}) collective-permute-start(bf16[4,2,256,128]{3,2,1,0:T(8,128)(2,1)} %get-tuple-element.136), channel_id=1, source_target_pairs={{0,64},{4,68},{8,72},{12,76},{16,80},{20,84},{24,88},{28,92},{32,9... | collective-permute-start | bytes 1572872 | tf_op jit(solution)/shard_map/ppermute | solution.py:84
  243.8 26.1 %collective-permute-start.35 = (bf16[4,2,256,128]{3,2,1,0:T(8,128)(2,1)}, bf16[4,2,256,128]{3,2,1,0:T(8,128)(2,1)}, u32[]{:S(2)}, u32[]{:S(2)}) collective-permute-start(bf16[4,2,256,128]{3,2,1,0:T(8,128)(2,1)} %get-tuple-element.137), channel_id=1, source_target_pairs={{0,96},{4,100},{8,104},{12,108},{16,112},{20,116},{24,120},{28,124... | collective-permute-start | bytes 1572872 | tf_op jit(solution)/shard_map/ppermute | solution.py:84
  249.0 30.7 %collective-permute-start.39 = (bf16[4,2,256,128]{3,2,1,0:T(8,128)(2,1)}, bf16[4,2,256,128]{3,2,1,0:T(8,128)(2,1)S(1)}, u32[]{:S(2)}, u32[]{:S(2)}) collective-permute-start(bf16[4,2,256,128]{3,2,1,0:T(8,128)(2,1)} %get-tuple-element.142), channel_id=1, source_target_pairs={{0,8},{4,12},{8,16},{12,20},{16,24},{20,28},{24,0},{28,4},{32,40},... | collective-permute-start | bytes 1572872 | tf_op jit(solution)/shard_map/ppermute | solution.py:84
  253.3 27.7 %collective-permute-start.40 = (bf16[4,2,256,128]{3,2,1,0:T(8,128)(2,1)}, bf16[4,2,256,128]{3,2,1,0:T(8,128)(2,1)S(1)}, u32[]{:S(2)}, u32[]{:S(2)}) collective-permute-start(bf16[4,2,256,128]{3,2,1,0:T(8,128)(2,1)} %get-tuple-element.143), channel_id=1, source_target_pairs={{0,16},{4,20},{8,24},{12,28},{16,0},{20,4},{24,8},{28,12},{32,48},... | collective-permute-start | bytes 1572872 | tf_op jit(solution)/shard_map/ppermute | solution.py:84
  268.7 17.9 %collective-permute-start.41 = (bf16[4,2,256,128]{3,2,1,0:T(8,128)(2,1)}, bf16[4,2,256,128]{3,2,1,0:T(8,128)(2,1)}, u32[]{:S(2)}, u32[]{:S(2)}) collective-permute-start(bf16[4,2,256,128]{3,2,1,0:T(8,128)(2,1)} %get-tuple-element.144), channel_id=1, source_target_pairs={{0,24},{4,28},{8,0},{12,4},{16,8},{20,12},{24,16},{28,20},{32,56},... | collective-permute-start | bytes 1572872 | tf_op jit(solution)/shard_map/ppermute | solution.py:84
  271.3 18.5 %collective-permute-start.36 = (bf16[2,256,128]{2,1,0:T(8,128)(2,1)S(1)}, bf16[2,256,128]{2,1,0:T(8,128)(2,1)S(1)}, u32[]{:S(2)}, u32[]{:S(2)}) collective-permute-start(bf16[2,256,128]{2,1,0:T(8,128)(2,1)S(1)} %get-tuple-element.139), channel_id=1, source_target_pairs={{0,8},{4,12},{8,16},{12,20},{16,24},{20,28},{24,0},{28,4},{32,40},... | collective-permute-start | bytes 393224 | tf_op jit(solution)/shard_map/ppermute | solution.py:84
  274.7 15.3 %collective-permute-start.37 = (bf16[2,256,128]{2,1,0:T(8,128)(2,1)S(1)}, bf16[2,256,128]{2,1,0:T(8,128)(2,1)S(1)}, u32[]{:S(2)}, u32[]{:S(2)}) collective-permute-start(bf16[2,256,128]{2,1,0:T(8,128)(2,1)S(1)} %get-tuple-element.140), channel_id=1, source_target_pairs={{0,16},{4,20},{8,24},{12,28},{16,0},{20,4},{24,8},{28,12},{32,48},... | collective-permute-start | bytes 393224 | tf_op jit(solution)/shard_map/ppermute | solution.py:84
  279.6 13.6 %collective-permute-start.38 = (bf16[2,256,128]{2,1,0:T(8,128)(2,1)S(1)}, bf16[2,256,128]{2,1,0:T(8,128)(2,1)S(1)}, u32[]{:S(2)}, u32[]{:S(2)}) collective-permute-start(bf16[2,256,128]{2,1,0:T(8,128)(2,1)S(1)} %get-tuple-element.141), channel_id=1, source_target_pairs={{0,24},{4,28},{8,0},{12,4},{16,8},{20,12},{24,16},{28,20},{32,56},... | collective-permute-start | bytes 393224 | tf_op jit(solution)/shard_map/ppermute | solution.py:84
  288.0 7.7 %collective-permute-start.42 = (bf16[2,256,128]{2,1,0:T(8,128)(2,1)S(1)}, bf16[2,256,128]{2,1,0:T(8,128)(2,1)S(1)}, u32[]{:S(2)}, u32[]{:S(2)}) collective-permute-start(bf16[2,256,128]{2,1,0:T(8,128)(2,1)S(1)} %get-tuple-element.146), channel_id=1, source_target_pairs={{0,32},{4,36},{8,40},{12,44},{16,48},{20,52},{24,56},{28,60},{32,6... | collective-permute-start | bytes 393224 | tf_op jit(solution)/shard_map/ppermute | solution.py:84
  289.8 14.0 %collective-permute-start.48 = (bf16[3,4,32,256]{3,2,1,0:T(8,128)(2,1)S(1)}, bf16[3,4,32,256]{3,2,1,0:T(8,128)(2,1)S(1)}, u32[]{:S(2)}, u32[]{:S(2)}) collective-permute-start(bf16[3,4,32,256]{3,2,1,0:T(8,128)(2,1)S(1)} %get-tuple-element.155), channel_id=1, source_target_pairs={{0,1},{1,2},{2,3},{3,0},{4,5},{5,6},{6,7},{7,4},{8,9},{9,10},{10,1... | collective-permute-start | bytes 589832 | tf_op jit(solution)/shard_map/ppermute | solution.py:88
  290.0 8.4 %collective-permute-start.44 = (bf16[2,256,128]{2,1,0:T(8,128)(2,1)S(1)}, bf16[2,256,128]{2,1,0:T(8,128)(2,1)S(1)}, u32[]{:S(2)}, u32[]{:S(2)}) collective-permute-start(bf16[2,256,128]{2,1,0:T(8,128)(2,1)S(1)} %get-tuple-element.148), channel_id=1, source_target_pairs={{0,96},{4,100},{8,104},{12,108},{16,112},{20,116},{24,120},{28,124... | collective-permute-start | bytes 393224 | tf_op jit(solution)/shard_map/ppermute | solution.py:84
  293.3 10.9 %collective-permute-start.49 = (bf16[3,4,32,256]{3,2,1,0:T(8,128)(2,1)S(1)}, bf16[3,4,32,256]{3,2,1,0:T(8,128)(2,1)S(1)}, u32[]{:S(2)}, u32[]{:S(2)}) collective-permute-start(bf16[3,4,32,256]{3,2,1,0:T(8,128)(2,1)S(1)} %get-tuple-element.156), channel_id=1, source_target_pairs={{0,2},{1,3},{2,0},{3,1},{4,6},{5,7},{6,4},{7,5},{8,10},{9,11},{10,... | collective-permute-start | bytes 589832 | tf_op jit(solution)/shard_map/ppermute | solution.py:88
  295.6 8.6 %collective-permute-start.50 = (bf16[3,4,32,256]{3,2,1,0:T(8,128)(2,1)S(1)}, bf16[3,4,32,256]{3,2,1,0:T(8,128)(2,1)S(1)}, u32[]{:S(2)}, u32[]{:S(2)}) collective-permute-start(bf16[3,4,32,256]{3,2,1,0:T(8,128)(2,1)S(1)} %get-tuple-element.157), channel_id=1, source_target_pairs={{0,3},{1,0},{2,1},{3,2},{4,7},{5,4},{6,5},{7,6},{8,11},{9,8},{10,9... | collective-permute-start | bytes 589832 | tf_op jit(solution)/shard_map/ppermute | solution.py:88
  (31 other events, 196.9 us)

commit v4 on v3

--- a/solution.py
+++ b/solution.py
@@ -23,7 +23,7 @@
 OWN = 4
 REAL_OWNERS = NBLK // OWN
 BIG = 1e6
-CHUNK = SECTIONS * PIECE + 16
+EXTRA = 2 * PIECE
 EVERY = ("replica", "section")
 
 rms_eps = 1e-05
@@ -110,15 +110,16 @@
     return lax.ppermute(block, "replica", [(i, i ^ 1) for i in range(REPLICAS)])
 
 
-def pack_kernel(which, table, blocks, out, room, came, went):
+def pack_kernel(which, sections, table, blocks, out, room, came, went):
+    tall = len(sections) * PIECE
     for part in range(8):
-        for s in range(SECTIONS):
+        for n, s in enumerate(sections):
 
             def start(i, carry):
                 r = part * 4 + i
                 pltpu.make_async_copy(
                     blocks.at[table[which, r * 4 + s]],
-                    room.at[r, :, pl.ds(s * PIECE, PIECE)],
+                    room.at[r, :, pl.ds(n * PIECE, PIECE)],
                     came.at[part],
                 ).start()
                 return carry
@@ -127,7 +128,7 @@
 
     def go(part):
         rows = pl.ds(part * 4, 4)
-        into = out.at[rows, :, pl.ds(0, SECTIONS * PIECE)]
+        into = out.at[rows, :, pl.ds(0, tall)]
         return pltpu.make_async_copy(room.at[rows], into, went.at[part])
 
     for part in range(8):
@@ -138,19 +139,22 @@
         go(part).wait()
 
 
-def pack(which, table, blocks, tall, after=()):
+def pack(which, sections, table, blocks, extra=0, after=()):
+    tall = len(sections) * PIECE
     return call(
-        functools.partial(pack_kernel, which),
-        struct((REPLICAS, 4, tall, HID), bf16),
+        functools.partial(pack_kernel, which, sections),
+        struct((REPLICAS, 4, tall + extra, HID), bf16),
         [SMEM, ANY],
         HBM,
         [
-            pltpu.VMEM((REPLICAS, 4, SECTIONS * PIECE, HID), bf16),
+            pltpu.VMEM((REPLICAS, 4, tall, HID), bf16),
             pltpu.SemaphoreType.DMA((8,)),
             pltpu.SemaphoreType.DMA((8,)),
         ],
         after=after,
-        limit=BULK, us=7.4)(table, blocks)
+        limit=BULK,
+        us=1.85 * len(sections),
+    )(table, blocks)
 
 
 def pack_second_kernel(half, table, blocks, *refs):
@@ -257,7 +261,7 @@
             come = pltpu.make_async_copy(ref, room, sem.at[0])
             come.start()
             come.wait()
-            go = pltpu.make_async_copy(room, out.at[:, :, pl.ds(SECTIONS * PIECE, 16)], sem.at[1])
+            go = pltpu.make_async_copy(room, out.at[:, :, pl.ds(EXTRA, 16)], sem.at[1])
             go.start()
             go.wait()
 
@@ -265,7 +269,7 @@
 def add_relayed(got, place, relays, buffer):
     return call(
         add_relayed_kernel,
-        struct((REPLICAS, 4, CHUNK, HID), bf16),
+        struct((REPLICAS, 4, EXTRA + 16, HID), bf16),
         [VMEM, SMEM] + [HBM] * 5,
         HBM,
         [pltpu.VMEM((REPLICAS, 4, 16, HID), bf16), pltpu.SemaphoreType.DMA((2,))],
@@ -281,46 +285,57 @@
     return call(blank_kernel, struct((DEVICES, SECTIONS * PIECE, HID), bf16), [SMEM], HBM)(flag)
 
 
-def fetch(section, place, relays, first, second, out, sem):
-    rows = section * PIECE
-    if not isinstance(section, int):
-        rows = pl.multiple_of(rows, PIECE)
-    rows = pl.ds(rows, PIECE)
-    extra = pl.ds(SECTIONS * PIECE, 16)
-
-    @pl.when(place < DEVICES)
-    def _():
-        pltpu.make_async_copy(first.at[place, rows], out, sem).start()
+def fetch(section, place, relays, firsts, second, out, sem):
+    def copy(source, target):
+        pltpu.make_async_copy(source, target, sem).start()
+
+    def rows(start):
+        if not isinstance(start, int):
+            start = pl.multiple_of(start, PIECE)
+        return pl.ds(start, PIECE)
+
+    for half in range(2):
+        here = section // 2 == half
+
+        def direct():
+            @pl.when(place < DEVICES)
+            def _():
+                copy(firsts[half].at[place, rows((section - 2 * half) * PIECE)], out)
+
+        if not isinstance(section, int):
+            pl.when(here)(direct)
+        elif here:
+            direct()
 
     @pl.when(place >= DEVICES)
     def _():
         @pl.when(place < 2 * DEVICES)
         def _():
-            pltpu.make_async_copy(second.at[place - DEVICES, rows], out, sem).start()
+            copy(second.at[place - DEVICES, rows(section * PIECE)], out)
 
         @pl.when(place == 2 * DEVICES)
         def _():
-            low, high = relays[section], relays[section + 4]
-            pltpu.make_async_copy(first.at[low, extra], out.at[pl.ds(0, 16)], sem).start()
-            pltpu.make_async_copy(first.at[high, extra], out.at[pl.ds(16, 16)], sem).start()
-
-
-def gather_kernel(section, begin, places, relays, first, second, out, sem):
+            extra = pl.ds(EXTRA, 16)
+            copy(firsts[1].at[relays[section], extra], out.at[pl.ds(0, 16)])
+            copy(firsts[1].at[relays[section + 4], extra], out.at[pl.ds(16, 16)])
+
+
+def gather_kernel(section, begin, places, relays, early, late, second, out, sem):
     def start(b, carry):
-        fetch(section, places[begin + b], relays, first, second, out.at[b], sem)
+        fetch(section, places[begin + b], relays, (early, late), second, out.at[b], sem)
         return carry
 
     lax.fori_loop(0, HALF, start, 0, unroll=8)
     pltpu.make_async_copy(out, out, sem).wait()
 
 
-def gather(section, begin, places, relays, first, second):
+def gather(section, begin, places, relays, early, late, second):
     return call(
         functools.partial(gather_kernel, section, begin),
         struct((HALF, PIECE, HID), bf16),
-        [SMEM, SMEM, ANY, ANY],
+        [SMEM, SMEM, ANY, ANY, ANY],
         ANY,
-        [pltpu.SemaphoreType.DMA], us=1.9)(places, relays, first, second)
+        [pltpu.SemaphoreType.DMA], us=1.9)(places, relays, early, late, second)
 
 
 def tables_kernel(lists, table, labels):
@@ -378,16 +393,18 @@
     blocks = old_blocks.reshape(NBLK, 4, PIECE, HID)
     table, labels = send_tables(moment_dest, send_slot, send_dest, send_block)
 
+    early = pack(0, (0, 1), table, blocks)
+    early, table = lax.optimization_barrier((early, table))
     (other,) = pack_second(1, table, blocks)
     table_other = from_sibling(table)
     came = from_sibling(other)
-    other, labels = lax.optimization_barrier((other, labels))
-    got = lax.all_to_all(labels, EVERY, 0, 0, tiled=True)
     own = pack_second(0, table, blocks, after=[other])
     mine = take_over(table_other, came, own)
+    buffer = pack(0, (2, 3), table, blocks, 16)
+    early = lax.all_to_all(early.reshape(DEVICES, EXTRA, HID), EVERY, 0, 0, tiled=True)
+    early, labels, buffer = lax.optimization_barrier((early, labels, buffer))
     relays = [mine[0], spread(mine[1], "x"), spread(mine[2], "y"), spread(mine[3], "z")]
-    buffer = pack(0, table, blocks, CHUNK)
-
+    got = lax.all_to_all(labels, EVERY, 0, 0, tiled=True)
     buffer = add_relayed(got, place, relays, buffer)
     layer_0, cots = quarter(acts_in, cotangent, place[3])
     buffer, got = lax.optimization_barrier((buffer, got))
@@ -397,15 +414,15 @@
     busy = jnp.sum(jnp.where(holders > 0, numbers, 0))
     busy = jnp.where(alone, busy, 0)
     relayed_by = jnp.stack(relay_places(busy)).astype(jnp.int32)
-    arrived = lax.all_to_all(buffer.reshape(DEVICES, CHUNK, HID), EVERY, 0, 0, tiled=True)
+    late = lax.all_to_all(buffer.reshape(DEVICES, EXTRA + 16, HID), EVERY, 0, 0, tiled=True)
 
     def second_round():
-        again = pack(1, table, blocks, SECTIONS * PIECE)
+        again = pack(1, tuple(range(SECTIONS)), table, blocks)
         return lax.all_to_all(
             again.reshape(DEVICES, SECTIONS * PIECE, HID), EVERY, 0, 0, tiled=True
         )
 
-    arrived, table, alone_now = lax.optimization_barrier((arrived, table, alone))
+    late, table, alone_now = lax.optimization_barrier((late, table, alone))
     spare = lax.cond(alone_now, lambda: blank(table), second_round)
 
     wanted = jnp.arange(1, NBLK + 1, dtype=jnp.int32)[None, None, :]
@@ -416,10 +433,10 @@
     places = jnp.sum(jnp.where(in_first, senders, 0) + jnp.where(in_second, later, 0), axis=0)
     places = jnp.clip(places, 0, 2 * DEVICES)
     weights = [
-        [gather(s, begin, places[s], relayed_by, arrived, spare) for begin in (0, HALF)]
+        [gather(s, begin, places[s], relayed_by, early, late, spare) for begin in (0, HALF)]
         for s in range(SECTIONS)
     ]
-    return weights, got, (places.reshape(-1), relayed_by, arrived, spare), layer_0, cots
+    return weights, got, (places.reshape(-1), relayed_by, early, late, spare), layer_0, cots
 
 
 def quarter_kernel(pick, acts, cots, acts_out, cots_out):
@@ -653,14 +670,14 @@
             outs[k][1, a] = second[a, rows, :].astype(bf16)
 
 
-def order_kernel(place, source, places, relays, first, second, *refs):
+def order_kernel(place, source, places, relays, early, late, second, *refs):
     moments, outs, (table, came, sem) = refs[:4], refs[4:8], refs[8:]
     start = jnp.minimum(place[4], REAL_OWNERS - 1) * OWN
     for k in range(4):
         section = lax.rem(place[3] + k, 4)
         for i in range(OWN):
             held = places[section * NBLK + start + i]
-            fetch(section, held, relays, first, second, came.at[k, i], sem)
+            fetch(section, held, relays, (early, late), second, came.at[k, i], sem)
     for k in range(4):
         table[k] = moments[k][...]
     for k in range(4):
@@ -758,7 +775,7 @@
     ordered = call(
         order_kernel,
         [struct((3, OWN, PIECE, HID), bf16)] * 4,
-        [SMEM] * 4 + [ANY] * 2 + [VMEM] * 4,
+        [SMEM] * 4 + [ANY] * 3 + [VMEM] * 4,
         [VMEM] * 4,
         [
             pltpu.VMEM((4, 2, OWN, PIECE, HID), bf16),

time: 310 us -> 298 us (0.961); the launches traced: 310 us -> 295 us
  waiting for transfers between devices: 148 us -> 130 us
    all_to_all x1 -> x2, waiting for transfers between devices: 100 us -> 86.9 us  [the longest x1 47.8 us: route_blocks(): lax.all_to_all(buffer.reshape(DEVICES, EXTRA + 16, HID), EVERY, 0, 0, til...]
    all_to_all x1 -> x2, starting transfers between devices: 11.7 us -> 21.1 us  [the longest x1 14 us: route_blocks(): lax.all_to_all(early.reshape(DEVICES, EXTRA, HID), EVERY, 0, 0, tiled=True)]
    all_to_all x1, waiting for transfers between devices: 0.73 us -> 8.08 us  [route_blocks(): got = lax.all_to_all(labels, EVERY, 0, 0, tiled=True)]
    ppermute x12, waiting for transfers between devices: 17.9 us -> 10.8 us  [shift_xy(): return lax.ppermute(block, 'replica', route)]
    all_to_all x1, starting transfers between devices: 12 us -> 5.59 us  [route_blocks(): got = lax.all_to_all(labels, EVERY, 0, 0, tiled=True)]
    ppermute x6, waiting for transfers between devices: 6.32 us -> 0.34 us  [from_sibling(): return lax.ppermute(block, 'replica', [(i, i ^ 1) for i in range(REPLICAS)])]
    ppermute x30, starting transfers between devices: 46.5 us -> 41.9 us  [shift_z(): lax.ppermute(block, 'section', [(i, (i + step) % 4) for i in range(4)])]
    pallas_call x32 -> x33, Pallas kernels: 48.6 us -> 51.1 us  [call(): return lambda *arrays: run(*after, *arrays)]
  transfers between devices with their start and end apart: 53 -> 54, of which waited for: 20 -> 22; matrix products, arithmetic and copies ran while one was open for 1% -> 1% of each run, Pallas kernels for 12% -> 13%
where the time goes in v4:
time: 298 us; the launch traced here: 295 us
  waiting for transfers between devices  130 us (44%)
  starting transfers between devices  102 us (34%)
  Pallas kernels  51.1 us (17%)
  local copies, waits for them, and re-layouts  6.53 us (2%)
    pallas_call x33, Pallas kernels, call(): return lambda *arrays: run(*after, *arrays)  51.1 us
    all_to_all x1, waiting for transfers between devices, route_blocks(): lax.all_to_all(buffer.reshape(DEVICES, EXTRA + 16, HID), EVERY, 0, 0, til...  47.8 us
    ppermute x30, starting transfers between devices, shift_z(): lax.ppermute(block, 'section', [(i, (i + step) % 4) for i in range(4)])  41.9 us
    all_to_all x1, waiting for transfers between devices, route_blocks(): lax.all_to_all(early.reshape(DEVICES, EXTRA, HID), EVERY, 0, 0, tiled=True)  39.1 us
    ppermute x12, starting transfers between devices, shift_xy(): return lax.ppermute(block, 'replica', route)  27.9 us
    ppermute x30, waiting for transfers between devices, shift_z(): lax.ppermute(block, 'section', [(i, (i + step) % 4) for i in range(4)])  23.7 us
    all_to_all x1, starting transfers between devices, route_blocks(): lax.all_to_all(early.reshape(DEVICES, EXTRA, HID), EVERY, 0, 0, tiled=True)  14 us
    ppermute x12, waiting for transfers between devices, shift_xy(): return lax.ppermute(block, 'replica', route)  10.8 us
  transfers between devices with their start and end apart: 54, of which 22 were waited for; matrix products, arithmetic and copies ran while one was open for 1% of the time, Pallas kernels for 13%

profile of v4, /device:TPU:8, one launch (start us, length us, event | category | flops | bytes accessed | tf_op | source)
XLA Modules:
  0.0 294.9 jit_solution(17164273151914200080)
XLA Ops:
  2.3 4.6 %shard_map.115 = bf16[32,4,64,256]{3,2,1,0:T(8,128)(2,1)} custom-call(s32[8,128]{1,0:T(8,128)S(1)} %get-tuple-element.113.refs_0_.refs_1_, bf16[112,4,32,256]{3,2,1,0:T(8,128)(2,1)} %bitcast.38), custom_call_target="tpu_custom_call" | custom-call | bytes 12580000 | tf_op jit(solution)/shard_map/pallas_call | solution.py:70
  7.7 14.0 %all-to-all-start.1 = ((bf16[128,64,256]{2,1,0:T(8,128)(2,1)}), bf16[128,64,256]{2,1,0:T(8,128)(2,1)}, u32[]{:S(2)}, u32[]{:S(2)}) async-start(bf16[128,64,256]{2,1,0:T(8,128)(2,1)} %bitcast.45), calls=%async_computation.1 | async-start | bytes 8388608 | tf_op jit(solution)/shard_map/all_to_all | solution.py:404
  29.2 4.7 %shard_map.116.refs_6_ = bf16[32,4,80,256]{3,2,1,0:T(8,128)(2,1)} custom-call(s32[8,128]{1,0:T(8,128)S(1)} %get-tuple-element.113.refs_0_.refs_1_, bf16[112,4,32,256]{3,2,1,0:T(8,128)(2,1)} %bitcast.41), custom_call_target="tpu_custom_call" | custom-call | bytes 12580000 | tf_op jit(solution)/shard_map/pallas_call | solution.py:70
  33.9 39.1 %all-to-all-done.1.refs_2_.refs_4_ = bf16[128,64,256]{2,1,0:T(8,128)(2,1)} async-done(((bf16[128,64,256]{2,1,0:T(8,128)(2,1)}), bf16[128,64,256]{2,1,0:T(8,128)(2,1)}, u32[]{:S(2)}, u32[]{:S(2)}) %all-to-all-start.1) | async-done | bytes 4194336 | tf_op jit(solution)/shard_map/all_to_all | solution.py:404
  73.1 5.6 %all-to-all-start.2 = ((s32[128,1,16]{2,1,0:T(1,128)}), s32[128,1,16]{2,1,0:T(1,128)S(1)}, u32[]{:S(2)}, u32[]{:S(2)}) async-start(s32[128,1,16]{2,1,0:T(1,128)} %bitcast.11), calls=%async_computation.2 | async-start | bytes 131072 | tf_op jit(solution)/shard_map/all_to_all | solution.py:407
  79.3 8.1 %all-to-all-done.2 = s32[128,1,16]{2,1,0:T(1,128)S(1)} async-done(((s32[128,1,16]{2,1,0:T(1,128)}), s32[128,1,16]{2,1,0:T(1,128)S(1)}, u32[]{:S(2)}, u32[]{:S(2)}) %all-to-all-start.2) | async-done | bytes 8224 | tf_op jit(solution)/shard_map/all_to_all | solution.py:407
  89.5 7.1 %all-to-all-start.3 = ((bf16[128,80,256]{2,1,0:T(8,128)(2,1)}), bf16[128,80,256]{2,1,0:T(8,128)(2,1)}, u32[]{:S(2)}, u32[]{:S(2)}) async-start(bf16[128,80,256]{2,1,0:T(8,128)(2,1)} %bitcast.43), calls=%async_computation.3 | async-start | bytes 10485760 | tf_op jit(solution)/shard_map/all_to_all | solution.py:417
  98.9 3.2 %collective-permute-start.1 = (bf16[2,4,32,256]{3,2,1,0:T(8,128)(2,1)S(1)}, bf16[2,4,32,256]{3,2,1,0:T(8,128)(2,1)S(1)}, u32[]{:S(2)}, u32[]{:S(2)}) collective-permute-start(bf16[2,4,32,256]{3,2,1,0:T(8,128)(2,1)S(1)} %get-tuple-element.91), channel_id=1, source_target_pairs={{0,2},{1,3},{2,0},{3,1},{4,6},{5,7},{6,4},{7,5},{8,10},{9,11},{10,... | collective-permute-start | bytes 393224 | tf_op jit(solution)/shard_map/ppermute | solution.py:88
  111.2 47.8 %all-to-all-done.3.refs_3_.refs_5_ = bf16[128,80,256]{2,1,0:T(8,128)(2,1)} async-done(((bf16[128,80,256]{2,1,0:T(8,128)(2,1)}), bf16[128,80,256]{2,1,0:T(8,128)(2,1)}, u32[]{:S(2)}, u32[]{:S(2)}) %all-to-all-start.3) | async-done | bytes 5242912 | tf_op jit(solution)/shard_map/all_to_all | solution.py:417
  171.7 2.5 collective-permute-start.12
  181.2 3.2 %collective-permute-start.15 = (bf16[128,384]{1,0:T(8,128)(2,1)S(1)}, bf16[128,384]{1,0:T(8,128)(2,1)S(1)}, u32[]{:S(2)}, u32[]{:S(2)}) collective-permute-start(bf16[128,384]{1,0:T(8,128)(2,1)S(1)} %get-tuple-element.118.refs_5_), channel_id=1, source_target_pairs={{0,3},{1,0},{2,1},{3,2},{4,7},{5,4},{6,5},{7,6},{8,11},{9,8},{10,9... | collective-permute-start | bytes 294920 | tf_op jit(solution)/shard_map/ppermute | solution.py:88
  192.2 2.6 collective-permute-start.18
  196.9 2.6 collective-permute-done.17.refs_1_
  202.9 2.9 collective-permute-start.21
  208.4 3.2 %collective-permute-done.22.refs_3_ = bf16[128,256]{1,0:T(8,128)(2,1)S(1)} collective-permute-done((bf16[128,256]{1,0:T(8,128)(2,1)S(1)}, bf16[128,256]{1,0:T(8,128)(2,1)S(1)}, u32[]{:S(2)}, u32[]{:S(2)}) %collective-permute-start.22) | collective-permute-done | bytes 65568 | tf_op jit(solution)/shard_map/ppermute | solution.py:88
  212.6 3.2 %collective-permute-start.26 = (bf16[128,256]{1,0:T(8,128)(2,1)S(1)}, bf16[128,256]{1,0:T(8,128)(2,1)S(1)}, u32[]{:S(2)}, u32[]{:S(2)}) collective-permute-start(bf16[128,256]{1,0:T(8,128)(2,1)S(1)} %get-tuple-element.128.refs_2_), channel_id=1, source_target_pairs={{0,3},{1,0},{2,1},{3,2},{4,7},{5,4},{6,5},{7,6},{8,11},{9,8},{10,9... | collective-permute-start | bytes 196616 | tf_op jit(solution)/shard_map/ppermute | solution.py:88
  215.8 2.4 collective-permute-done.25.refs_3_
  218.9 2.7 collective-permute-done.27.refs_5_
  222.6 3.2 %collective-permute-start.30 = (bf16[128,256]{1,0:T(8,128)(2,1)S(1)}, bf16[128,256]{1,0:T(8,128)(2,1)S(1)}, u32[]{:S(2)}, u32[]{:S(2)}) collective-permute-start(bf16[128,256]{1,0:T(8,128)(2,1)S(1)} %get-tuple-element.135.refs_1_), channel_id=1, source_target_pairs={{0,3},{1,0},{2,1},{3,2},{4,7},{5,4},{6,5},{7,6},{8,11},{9,8},{10,9... | collective-permute-start | bytes 196616 | tf_op jit(solution)/shard_map/ppermute | solution.py:88
  225.8 3.2 %shard_map.136 = (bf16[4,2,256,128]{3,2,1,0:T(8,128)(2,1)S(1)}, bf16[4,2,256,128]{3,2,1,0:T(8,128)(2,1)S(1)}, bf16[4,2,256,128]{3,2,1,0:T(8,128)(2,1)}, bf16[4,2,256,128]{3,2,1,0:T(8,128)(2,1)}) custom-call(s32[5]{0:T(128)S(1)} %copy-done.4, bf16[128,4096]{1,0:T(8,128)(2,1)S(1)} %get-tuple-element.127.refs_1_, ...), custom_call_target="tpu_custom_call" | custom-call | bytes 11220000 | tf_op jit(solution)/shard_map/pallas_call | solution.py:70
  229.0 2.6 collective-permute-done.31.refs_4_
  233.3 2.7 collective-permute-start.34
  236.9 3.4 %shard_map.138 = (bf16[4,2,256,128]{3,2,1,0:T(8,128)(2,1)S(1)}, bf16[4,2,256,128]{3,2,1,0:T(8,128)(2,1)}, bf16[4,2,256,128]{3,2,1,0:T(8,128)(2,1)}, bf16[4,2,256,128]{3,2,1,0:T(8,128)(2,1)}) custom-call(s32[5]{0:T(128)S(1)} %copy-done.4, bf16[128,4096]{1,0:T(8,128)(2,1)S(1)} %get-tuple-element.126.refs_1_, ...), custom_call_target="tpu_custom_call" | custom-call | bytes 11220000 | tf_op jit(solution)/shard_map/pallas_call | solution.py:70
  241.6 4.0 %collective-permute-start.40 = (bf16[4,2,256,128]{3,2,1,0:T(8,128)(2,1)}, bf16[4,2,256,128]{3,2,1,0:T(8,128)(2,1)S(1)}, u32[]{:S(2)}, u32[]{:S(2)}) collective-permute-start(bf16[4,2,256,128]{3,2,1,0:T(8,128)(2,1)} %get-tuple-element.149), channel_id=1, source_target_pairs={{0,16},{4,20},{8,24},{12,28},{16,0},{20,4},{24,8},{28,12},{32,48},... | collective-permute-start | bytes 1572872 | tf_op jit(solution)/shard_map/ppermute | solution.py:84
  247.6 3.5 %collective-permute-start.41 = (bf16[4,2,256,128]{3,2,1,0:T(8,128)(2,1)}, bf16[4,2,256,128]{3,2,1,0:T(8,128)(2,1)}, u32[]{:S(2)}, u32[]{:S(2)}) collective-permute-start(bf16[4,2,256,128]{3,2,1,0:T(8,128)(2,1)} %get-tuple-element.150), channel_id=1, source_target_pairs={{0,24},{4,28},{8,0},{12,4},{16,8},{20,12},{24,16},{28,20},{32,56},... | collective-permute-start | bytes 1572872 | tf_op jit(solution)/shard_map/ppermute | solution.py:84
  252.1 7.2 %collective-permute-done.34.refs_4_ = bf16[4,2,256,128]{3,2,1,0:T(8,128)(2,1)} collective-permute-done((bf16[4,2,256,128]{3,2,1,0:T(8,128)(2,1)}, bf16[4,2,256,128]{3,2,1,0:T(8,128)(2,1)}, u32[]{:S(2)}, u32[]{:S(2)}) %collective-permute-start.34) | collective-permute-done | bytes 524320 | tf_op jit(solution)/shard_map/ppermute | solution.py:84
  262.5 4.7 %collective-permute-start.37 = (bf16[2,256,128]{2,1,0:T(8,128)(2,1)S(1)}, bf16[2,256,128]{2,1,0:T(8,128)(2,1)S(1)}, u32[]{:S(2)}, u32[]{:S(2)}) collective-permute-start(bf16[2,256,128]{2,1,0:T(8,128)(2,1)S(1)} %get-tuple-element.146), channel_id=1, source_target_pairs={{0,16},{4,20},{8,24},{12,28},{16,0},{20,4},{24,8},{28,12},{32,48},... | collective-permute-start | bytes 393224 | tf_op jit(solution)/shard_map/ppermute | solution.py:84
  267.2 2.6 collective-permute-start.38
  271.4 2.7 collective-permute-start.42
  276.1 2.7 collective-permute-start.44
  284.5 3.8 %collective-permute-start.46 = (bf16[256,128]{1,0:T(8,128)(2,1)S(1)}, bf16[256,128]{1,0:T(8,128)(2,1)S(1)}, u32[]{:S(2)}, u32[]{:S(2)}) collective-permute-start(bf16[256,128]{1,0:T(8,128)(2,1)S(1)} %get-tuple-element.157), channel_id=1, source_target_pairs={{0,2},{1,3},{2,0},{3,1},{4,6},{5,7},{6,4},{7,5},{8,10},{9,11},{10,... | collective-permute-start | bytes 196616 | tf_op jit(solution)/shard_map/ppermute | solution.py:88
  288.7 2.7 collective-permute-done.50.refs_8_
  (157 shorter events, 84.2 us)
Async XLA Ops:
  7.6 15.4 %collective-permute-start.4 = (bf16[4,32,4,16,256]{4,3,2,1,0:T(8,128)(2,1)}, bf16[4,32,4,16,256]{4,3,2,1,0:T(8,128)(2,1)}, u32[]{:S(2)}, u32[]{:S(2)}) collective-permute-start(bf16[4,32,4,16,256]{4,3,2,1,0:T(8,128)(2,1)} %shard_map.117.refs_0_), channel_id=1, source_target_pairs={{0,4},{4,0},{8,12},{12,8},{16,20},{20,16},{24,28},{28,24},{32,36},... | collective-permute-start | bytes 12582920 | tf_op jit(solution)/shard_map/ppermute | solution.py:110
  7.7 65.3 %all-to-all-start.1 = ((bf16[128,64,256]{2,1,0:T(8,128)(2,1)}), bf16[128,64,256]{2,1,0:T(8,128)(2,1)}, u32[]{:S(2)}, u32[]{:S(2)}) async-start(bf16[128,64,256]{2,1,0:T(8,128)(2,1)} %bitcast.45), calls=%async_computation.1 | async-start | bytes 8388608 | tf_op jit(solution)/shard_map/all_to_all | solution.py:404
  24.4 63.0 %collective-permute-start.5 = (bf16[32,4,16,256]{3,2,1,0:T(8,128)(2,1)}, bf16[32,4,16,256]{3,2,1,0:T(8,128)(2,1)S(1)}, u32[]{:S(2)}, u32[]{:S(2)}) collective-permute-start(bf16[32,4,16,256]{3,2,1,0:T(8,128)(2,1)} %get-tuple-element.104), channel_id=1, source_target_pairs={{0,32},{4,100},{8,40},{12,108},{16,48},{20,116},{24,56},{28,124},{... | collective-permute-start | bytes 3145736 | tf_op jit(solution)/shard_map/ppermute | solution.py:106
  26.0 61.4 %collective-permute-start.6 = (bf16[32,4,16,256]{3,2,1,0:T(8,128)(2,1)}, bf16[32,4,16,256]{3,2,1,0:T(8,128)(2,1)}, u32[]{:S(2)}, u32[]{:S(2)}) collective-permute-start(bf16[32,4,16,256]{3,2,1,0:T(8,128)(2,1)} %get-tuple-element.105), channel_id=1, source_target_pairs={{0,8},{4,28},{8,16},{12,4},{16,24},{20,12},{24,0},{28,20},{32,40},... | collective-permute-start | bytes 3145736 | tf_op jit(solution)/shard_map/ppermute | solution.py:106
  27.4 60.0 %collective-permute-start.7 = (bf16[32,4,16,256]{3,2,1,0:T(8,128)(2,1)}, bf16[32,4,16,256]{3,2,1,0:T(8,128)(2,1)}, u32[]{:S(2)}, u32[]{:S(2)}) collective-permute-start(bf16[32,4,16,256]{3,2,1,0:T(8,128)(2,1)} %get-tuple-element.106), channel_id=1, source_target_pairs={{0,1},{1,2},{2,3},{3,0},{4,7},{5,4},{6,5},{7,6},{8,9},{9,10},{10,1... | collective-permute-start | bytes 3145736 | tf_op jit(solution)/shard_map/ppermute | solution.py:98
  73.1 14.3 %all-to-all-start.2 = ((s32[128,1,16]{2,1,0:T(1,128)}), s32[128,1,16]{2,1,0:T(1,128)S(1)}, u32[]{:S(2)}, u32[]{:S(2)}) async-start(s32[128,1,16]{2,1,0:T(1,128)} %bitcast.11), calls=%async_computation.2 | async-start | bytes 131072 | tf_op jit(solution)/shard_map/all_to_all | solution.py:407
  89.5 69.5 %all-to-all-start.3 = ((bf16[128,80,256]{2,1,0:T(8,128)(2,1)}), bf16[128,80,256]{2,1,0:T(8,128)(2,1)}, u32[]{:S(2)}, u32[]{:S(2)}) async-start(bf16[128,80,256]{2,1,0:T(8,128)(2,1)} %bitcast.43), calls=%async_computation.3 | async-start | bytes 10485760 | tf_op jit(solution)/shard_map/all_to_all | solution.py:417
  97.2 66.5 %collective-permute-start = (bf16[2,4,32,256]{3,2,1,0:T(8,128)(2,1)S(1)}, bf16[2,4,32,256]{3,2,1,0:T(8,128)(2,1)S(1)}, u32[]{:S(2)}, u32[]{:S(2)}) collective-permute-start(bf16[2,4,32,256]{3,2,1,0:T(8,128)(2,1)S(1)} %get-tuple-element.90), channel_id=1, source_target_pairs={{0,1},{1,2},{2,3},{3,0},{4,5},{5,6},{6,7},{7,4},{8,9},{9,10},{10,1... | collective-permute-start | bytes 393224 | tf_op jit(solution)/shard_map/ppermute | solution.py:88
  98.9 71.1 %collective-permute-start.1 = (bf16[2,4,32,256]{3,2,1,0:T(8,128)(2,1)S(1)}, bf16[2,4,32,256]{3,2,1,0:T(8,128)(2,1)S(1)}, u32[]{:S(2)}, u32[]{:S(2)}) collective-permute-start(bf16[2,4,32,256]{3,2,1,0:T(8,128)(2,1)S(1)} %get-tuple-element.91), channel_id=1, source_target_pairs={{0,2},{1,3},{2,0},{3,1},{4,6},{5,7},{6,4},{7,5},{8,10},{9,11},{10,... | collective-permute-start | bytes 393224 | tf_op jit(solution)/shard_map/ppermute | solution.py:88
  102.1 67.9 %collective-permute-start.2 = (bf16[2,4,32,256]{3,2,1,0:T(8,128)(2,1)S(1)}, bf16[2,4,32,256]{3,2,1,0:T(8,128)(2,1)S(1)}, u32[]{:S(2)}, u32[]{:S(2)}) collective-permute-start(bf16[2,4,32,256]{3,2,1,0:T(8,128)(2,1)S(1)} %get-tuple-element.92), channel_id=1, source_target_pairs={{0,3},{1,0},{2,1},{3,2},{4,7},{5,4},{6,5},{7,6},{8,11},{9,8},{10,9... | collective-permute-start | bytes 393224 | tf_op jit(solution)/shard_map/ppermute | solution.py:88
  162.2 7.9 %collective-permute-start.10 = (bf16[128,384]{1,0:T(8,128)(2,1)S(1)}, bf16[128,384]{1,0:T(8,128)(2,1)S(1)}, u32[]{:S(2)}, u32[]{:S(2)}) collective-permute-start(bf16[128,384]{1,0:T(8,128)(2,1)S(1)} %shard_map.124.refs_6_), channel_id=1, source_target_pairs={{0,2},{1,3},{2,0},{3,1},{4,6},{5,7},{6,4},{7,5},{8,10},{9,11},{10,... | collective-permute-start | bytes 294920 | tf_op jit(solution)/shard_map/ppermute | solution.py:88
  170.9 7.8 %collective-permute-start.11 = (bf16[128,384]{1,0:T(8,128)(2,1)S(1)}, bf16[128,384]{1,0:T(8,128)(2,1)S(1)}, u32[]{:S(2)}, u32[]{:S(2)}) collective-permute-start(bf16[128,384]{1,0:T(8,128)(2,1)S(1)} %get-tuple-element.115.refs_3_), channel_id=1, source_target_pairs={{0,1},{1,2},{2,3},{3,0},{4,5},{5,6},{6,7},{7,4},{8,9},{9,10},{10,1... | collective-permute-start | bytes 294920 | tf_op jit(solution)/shard_map/ppermute | solution.py:88
  181.1 9.4 %collective-permute-start.14 = (bf16[128,384]{1,0:T(8,128)(2,1)S(1)}, bf16[128,384]{1,0:T(8,128)(2,1)S(1)}, u32[]{:S(2)}, u32[]{:S(2)}) collective-permute-start(bf16[128,384]{1,0:T(8,128)(2,1)S(1)} %get-tuple-element.118.refs_5_), channel_id=1, source_target_pairs={{0,1},{1,2},{2,3},{3,0},{4,5},{5,6},{6,7},{7,4},{8,9},{9,10},{10,1... | collective-permute-start | bytes 294920 | tf_op jit(solution)/shard_map/ppermute | solution.py:88
  181.2 9.3 %collective-permute-start.15 = (bf16[128,384]{1,0:T(8,128)(2,1)S(1)}, bf16[128,384]{1,0:T(8,128)(2,1)S(1)}, u32[]{:S(2)}, u32[]{:S(2)}) collective-permute-start(bf16[128,384]{1,0:T(8,128)(2,1)S(1)} %get-tuple-element.118.refs_5_), channel_id=1, source_target_pairs={{0,3},{1,0},{2,1},{3,2},{4,7},{5,4},{6,5},{7,6},{8,11},{9,8},{10,9... | collective-permute-start | bytes 294920 | tf_op jit(solution)/shard_map/ppermute | solution.py:88
  191.4 8.1 %collective-permute-start.17 = (bf16[128,640]{1,0:T(8,128)(2,1)S(1)}, bf16[128,640]{1,0:T(8,128)(2,1)S(1)}, u32[]{:S(2)}, u32[]{:S(2)}) collective-permute-start(bf16[128,640]{1,0:T(8,128)(2,1)S(1)} %get-tuple-element.119.refs_0_), channel_id=1, source_target_pairs={{0,1},{1,2},{2,3},{3,0},{4,5},{5,6},{6,7},{7,4},{8,9},{9,10},{10,1... | collective-permute-start | bytes 491528 | tf_op jit(solution)/shard_map/ppermute | solution.py:88
  192.2 7.3 %collective-permute-start.18 = (bf16[128,640]{1,0:T(8,128)(2,1)S(1)}, bf16[128,640]{1,0:T(8,128)(2,1)S(1)}, u32[]{:S(2)}, u32[]{:S(2)}) collective-permute-start(bf16[128,640]{1,0:T(8,128)(2,1)S(1)} %get-tuple-element.119.refs_0_), channel_id=1, source_target_pairs={{0,3},{1,0},{2,1},{3,2},{4,7},{5,4},{6,5},{7,6},{8,11},{9,8},{10,9... | collective-permute-start | bytes 491528 | tf_op jit(solution)/shard_map/ppermute | solution.py:88
  206.7 14.8 %collective-permute-start.24 = (bf16[128,4096]{1,0:T(8,128)(2,1)S(1)}, bf16[128,4096]{1,0:T(8,128)(2,1)S(1)}, u32[]{:S(2)}, u32[]{:S(2)}) collective-permute-start(bf16[128,4096]{1,0:T(8,128)(2,1)S(1)} %get-tuple-element.127.refs_1_), channel_id=1, source_target_pairs={{0,4},{4,0},{8,12},{12,8},{16,20},{20,16},{24,28},{28,24},{32,36},... | collective-permute-start | bytes 3145736 | tf_op jit(solution)/shard_map/ppermute | solution.py:110
  212.4 9.2 %collective-permute-start.23 = (bf16[128,4096]{1,0:T(8,128)(2,1)S(1)}, bf16[128,4096]{1,0:T(8,128)(2,1)S(1)}, u32[]{:S(2)}, u32[]{:S(2)}) collective-permute-start(bf16[128,4096]{1,0:T(8,128)(2,1)S(1)} %get-tuple-element.126.refs_1_), channel_id=1, source_target_pairs={{0,4},{4,0},{8,12},{12,8},{16,20},{20,16},{24,28},{28,24},{32,36},... | collective-permute-start | bytes 3145736 | tf_op jit(solution)/shard_map/ppermute | solution.py:110
  231.9 15.7 %collective-permute-start.33 = (bf16[4,2,256,128]{3,2,1,0:T(8,128)(2,1)S(1)}, bf16[4,2,256,128]{3,2,1,0:T(8,128)(2,1)S(1)}, u32[]{:S(2)}, u32[]{:S(2)}) collective-permute-start(bf16[4,2,256,128]{3,2,1,0:T(8,128)(2,1)S(1)} %get-tuple-element.141), channel_id=1, source_target_pairs={{0,32},{4,36},{8,40},{12,44},{16,48},{20,52},{24,56},{28,60},{32,6... | collective-permute-start | bytes 1572872 | tf_op jit(solution)/shard_map/ppermute | solution.py:84
  233.3 26.0 %collective-permute-start.34 = (bf16[4,2,256,128]{3,2,1,0:T(8,128)(2,1)}, bf16[4,2,256,128]{3,2,1,0:T(8,128)(2,1)}, u32[]{:S(2)}, u32[]{:S(2)}) collective-permute-start(bf16[4,2,256,128]{3,2,1,0:T(8,128)(2,1)} %get-tuple-element.142), channel_id=1, source_target_pairs={{0,64},{4,68},{8,72},{12,76},{16,80},{20,84},{24,88},{28,92},{32,9... | collective-permute-start | bytes 1572872 | tf_op jit(solution)/shard_map/ppermute | solution.py:84
  236.0 23.6 %collective-permute-start.35 = (bf16[4,2,256,128]{3,2,1,0:T(8,128)(2,1)}, bf16[4,2,256,128]{3,2,1,0:T(8,128)(2,1)}, u32[]{:S(2)}, u32[]{:S(2)}) collective-permute-start(bf16[4,2,256,128]{3,2,1,0:T(8,128)(2,1)} %get-tuple-element.143), channel_id=1, source_target_pairs={{0,96},{4,100},{8,104},{12,108},{16,112},{20,116},{24,120},{28,124... | collective-permute-start | bytes 1572872 | tf_op jit(solution)/shard_map/ppermute | solution.py:84
  240.2 26.9 %collective-permute-start.39 = (bf16[4,2,256,128]{3,2,1,0:T(8,128)(2,1)}, bf16[4,2,256,128]{3,2,1,0:T(8,128)(2,1)S(1)}, u32[]{:S(2)}, u32[]{:S(2)}) collective-permute-start(bf16[4,2,256,128]{3,2,1,0:T(8,128)(2,1)} %get-tuple-element.148), channel_id=1, source_target_pairs={{0,8},{4,12},{8,16},{12,20},{16,24},{20,28},{24,0},{28,4},{32,40},... | collective-permute-start | bytes 1572872 | tf_op jit(solution)/shard_map/ppermute | solution.py:84
  241.6 28.1 %collective-permute-start.40 = (bf16[4,2,256,128]{3,2,1,0:T(8,128)(2,1)}, bf16[4,2,256,128]{3,2,1,0:T(8,128)(2,1)S(1)}, u32[]{:S(2)}, u32[]{:S(2)}) collective-permute-start(bf16[4,2,256,128]{3,2,1,0:T(8,128)(2,1)} %get-tuple-element.149), channel_id=1, source_target_pairs={{0,16},{4,20},{8,24},{12,28},{16,0},{20,4},{24,8},{28,12},{32,48},... | collective-permute-start | bytes 1572872 | tf_op jit(solution)/shard_map/ppermute | solution.py:84
  247.6 22.6 %collective-permute-start.41 = (bf16[4,2,256,128]{3,2,1,0:T(8,128)(2,1)}, bf16[4,2,256,128]{3,2,1,0:T(8,128)(2,1)}, u32[]{:S(2)}, u32[]{:S(2)}) collective-permute-start(bf16[4,2,256,128]{3,2,1,0:T(8,128)(2,1)} %get-tuple-element.150), channel_id=1, source_target_pairs={{0,24},{4,28},{8,0},{12,4},{16,8},{20,12},{24,16},{28,20},{32,56},... | collective-permute-start | bytes 1572872 | tf_op jit(solution)/shard_map/ppermute | solution.py:84
  261.1 14.9 %collective-permute-start.36 = (bf16[2,256,128]{2,1,0:T(8,128)(2,1)S(1)}, bf16[2,256,128]{2,1,0:T(8,128)(2,1)S(1)}, u32[]{:S(2)}, u32[]{:S(2)}) collective-permute-start(bf16[2,256,128]{2,1,0:T(8,128)(2,1)S(1)} %get-tuple-element.145), channel_id=1, source_target_pairs={{0,8},{4,12},{8,16},{12,20},{16,24},{20,28},{24,0},{28,4},{32,40},... | collective-permute-start | bytes 393224 | tf_op jit(solution)/shard_map/ppermute | solution.py:84
  262.5 13.6 %collective-permute-start.37 = (bf16[2,256,128]{2,1,0:T(8,128)(2,1)S(1)}, bf16[2,256,128]{2,1,0:T(8,128)(2,1)S(1)}, u32[]{:S(2)}, u32[]{:S(2)}) collective-permute-start(bf16[2,256,128]{2,1,0:T(8,128)(2,1)S(1)} %get-tuple-element.146), channel_id=1, source_target_pairs={{0,16},{4,20},{8,24},{12,28},{16,0},{20,4},{24,8},{28,12},{32,48},... | collective-permute-start | bytes 393224 | tf_op jit(solution)/shard_map/ppermute | solution.py:84
  267.2 11.6 %collective-permute-start.38 = (bf16[2,256,128]{2,1,0:T(8,128)(2,1)S(1)}, bf16[2,256,128]{2,1,0:T(8,128)(2,1)S(1)}, u32[]{:S(2)}, u32[]{:S(2)}) collective-permute-start(bf16[2,256,128]{2,1,0:T(8,128)(2,1)S(1)} %get-tuple-element.147), channel_id=1, source_target_pairs={{0,24},{4,28},{8,0},{12,4},{16,8},{20,12},{24,16},{28,20},{32,56},... | collective-permute-start | bytes 393224 | tf_op jit(solution)/shard_map/ppermute | solution.py:84
  271.4 9.7 %collective-permute-start.42 = (bf16[2,256,128]{2,1,0:T(8,128)(2,1)S(1)}, bf16[2,256,128]{2,1,0:T(8,128)(2,1)S(1)}, u32[]{:S(2)}, u32[]{:S(2)}) collective-permute-start(bf16[2,256,128]{2,1,0:T(8,128)(2,1)S(1)} %get-tuple-element.152), channel_id=1, source_target_pairs={{0,32},{4,36},{8,40},{12,44},{16,48},{20,52},{24,56},{28,60},{32,6... | collective-permute-start | bytes 393224 | tf_op jit(solution)/shard_map/ppermute | solution.py:84
  275.9 12.4 %collective-permute-start.48 = (bf16[3,4,32,256]{3,2,1,0:T(8,128)(2,1)S(1)}, bf16[3,4,32,256]{3,2,1,0:T(8,128)(2,1)S(1)}, u32[]{:S(2)}, u32[]{:S(2)}) collective-permute-start(bf16[3,4,32,256]{3,2,1,0:T(8,128)(2,1)S(1)} %get-tuple-element.161), channel_id=1, source_target_pairs={{0,1},{1,2},{2,3},{3,0},{4,5},{5,6},{6,7},{7,4},{8,9},{9,10},{10,1... | collective-permute-start | bytes 589832 | tf_op jit(solution)/shard_map/ppermute | solution.py:88
  278.8 10.0 %collective-permute-start.49 = (bf16[3,4,32,256]{3,2,1,0:T(8,128)(2,1)S(1)}, bf16[3,4,32,256]{3,2,1,0:T(8,128)(2,1)S(1)}, u32[]{:S(2)}, u32[]{:S(2)}) collective-permute-start(bf16[3,4,32,256]{3,2,1,0:T(8,128)(2,1)S(1)} %get-tuple-element.162), channel_id=1, source_target_pairs={{0,2},{1,3},{2,0},{3,1},{4,6},{5,7},{6,4},{7,5},{8,10},{9,11},{10,... | collective-permute-start | bytes 589832 | tf_op jit(solution)/shard_map/ppermute | solution.py:88
  281.2 10.2 %collective-permute-start.50 = (bf16[3,4,32,256]{3,2,1,0:T(8,128)(2,1)S(1)}, bf16[3,4,32,256]{3,2,1,0:T(8,128)(2,1)S(1)}, u32[]{:S(2)}, u32[]{:S(2)}) collective-permute-start(bf16[3,4,32,256]{3,2,1,0:T(8,128)(2,1)S(1)} %get-tuple-element.163), channel_id=1, source_target_pairs={{0,3},{1,0},{2,1},{3,2},{4,7},{5,4},{6,5},{7,6},{8,11},{9,8},{10,9... | collective-permute-start | bytes 589832 | tf_op jit(solution)/shard_map/ppermute | solution.py:88
  283.9 7.5 %collective-permute-start.45 = (bf16[256,128]{1,0:T(8,128)(2,1)S(1)}, bf16[256,128]{1,0:T(8,128)(2,1)S(1)}, u32[]{:S(2)}, u32[]{:S(2)}) collective-permute-start(bf16[256,128]{1,0:T(8,128)(2,1)S(1)} %get-tuple-element.156), channel_id=1, source_target_pairs={{0,1},{1,2},{2,3},{3,0},{4,5},{5,6},{6,7},{7,4},{8,9},{9,10},{10,1... | collective-permute-start | bytes 196616 | tf_op jit(solution)/shard_map/ppermute | solution.py:88
  (33 other events, 185.6 us)

commit v5 on v4

--- a/solution.py
+++ b/solution.py
@@ -571,11 +571,11 @@
     return [message] + [shift_z(message, k) for k in (1, 3, 2)]
 
 
-def products(core, mine, other, chosen, store):
+def products(core, mine, other, small, small_sib, chosen, store):
     half = GROUPS // 2
 
-    def product(left, right, scale, start):
-        both = jnp.concatenate([mine[:, left], other[:, left]], axis=0)
+    def product(n, right, scale, start):
+        both = jnp.concatenate([small[n], small_sib[n]], axis=0)
         turned = both.astype(f32).T.astype(bf16)
         for g in range(half):
             columns = pl.ds(pl.multiple_of(right + (2 * g + core) * 128, 128), 128)
@@ -585,20 +585,13 @@
         for g in range(half):
             store(start + g, result[:, g * 128 : (g + 1) * 128].astype(bf16))
 
-    product(slice(2 * LOCAL, LEFT), 0, SCALE_IN, 0)
-    product(slice(LEFT, LEFT + HID), LOCAL, SCALE_OUT, half)
+    product(0, 0, SCALE_IN, 0)
+    product(1, LOCAL, SCALE_OUT, half)
     for owner in range(2 * half, 16):
         store(owner, jnp.zeros((HID, 128), bf16))
 
 
-def gradient_kernel(x_first, count, place, *refs):
-    ins, outs, (chosen, table) = refs[: 2 * count], refs[2 * count : 2 * count + 4], refs[-2:]
-    for n in range(count):
-
-        def store(owner, value):
-            table[owner, n] = value
-
-        products(place[2], *ins[2 * n : 2 * n + 2], chosen, store)
+def deal(x_first, place, table, outs):
     for k in range(4):
         for j in range(4):
             if x_first:
@@ -606,6 +599,54 @@
             else:
                 owner = j * 4 + lax.rem(place[1] + k, 4)
             outs[k][j] = table[owner]
+
+
+def gradient_kernel(x_first, count, place, *refs):
+    ins, outs, (chosen, table) = refs[: 2 * count], refs[2 * count : 2 * count + 4], refs[-2:]
+    for n in range(count):
+
+        def store(owner, value):
+            table[owner, n] = value
+
+        mine, other = ins[2 * n : 2 * n + 2]
+        small, small_sib = [
+            [ref[:, 2 * LOCAL : LEFT], ref[:, LEFT:]] for ref in (mine, other)
+        ]
+        products(place[2], mine, other, small, small_sib, chosen, store)
+    deal(x_first, place, table, outs)
+
+
+def table_kernel(place, mine, other, table, chosen):
+    def store(owner, value):
+        table[owner] = value
+
+    small, small_sib = [[ref[:, 2 * LOCAL : LEFT], ref[:, LEFT:]] for ref in (mine, other)]
+    products(place[2], mine, other, small, small_sib, chosen, store)
+
+
+def last_gradient_kernel(place, earlier, mine, other, *refs):
+    outs, (chosen, table) = refs[:4], refs[4:]
+
+    def store(owner, value):
+        table[owner, 1] = value
+
+    for owner in range(16):
+        table[owner, 0] = earlier[owner]
+    small, small_sib = [[ref[:, 2 * LOCAL : LEFT], ref[:, LEFT:]] for ref in (mine, other)]
+    products(place[2], mine, other, small, small_sib, chosen, store)
+    deal(False, place, table, outs)
+
+
+def last_half(place, arrays):
+    chunks = call(
+        last_gradient_kernel,
+        [struct((4, 2, HID, 128), bf16)] * 4,
+        [SMEM] + [VMEM] * 3,
+        [VMEM] * 4,
+        [pltpu.VMEM((2 * TOK, LOCAL // 2), bf16), pltpu.VMEM((16, 2, HID, 128), bf16)],
+        us=2.0,
+    )(place, *arrays)
+    return [chunks[0]] + [shift_xy(chunks[k], 0, k) for k in (1, 2, 3)]
 
 
 def halve_kernel(x_first, counts, place, *refs):
@@ -819,11 +860,19 @@
             after = [ready[2][1], ready[3][1]]
         elif s == 1:
             odd = first_half(True, place, [ready[3], ready[1]])
-            after = odd[:1]
+            earlier = call(
+                table_kernel,
+                struct((16, HID, 128), bf16),
+                [SMEM] + [VMEM] * 2,
+                VMEM,
+                [pltpu.VMEM((2 * TOK, LOCAL // 2), bf16)],
+                us=1.6,
+            )(place, *ready[2])
+            after = [odd[0], earlier]
         else:
-            even = first_half(False, place, [ready[2], ready[0]])
+            even = last_half(place, (earlier, *ready[0]))
             after = even[:1]
-    across = second_half(True, place, [odd], after)
+    across = second_half(True, place, [odd], [*after, ordered[0]])
     along = second_half(False, place, [even], after)
     kept, *sends = call(
         functools.partial(finish_kernel, ((3, 1), (2, 0))),

time: 298 us -> 292 us (0.980)
  waiting for transfers between devices: 130 us -> 122 us
    ppermute x12, starting transfers between devices: 27.9 us -> 32.4 us  [shift_xy(): return lax.ppermute(block, 'replica', route)]
    ppermute x12, waiting for transfers between devices: 10.8 us -> 6.62 us  [shift_xy(): return lax.ppermute(block, 'replica', route)]
    ppermute x30, waiting for transfers between devices: 23.7 us -> 20.1 us  [shift_z(): lax.ppermute(block, 'section', [(i, (i + step) % 4) for i in range(4)])]
    all_to_all x1, starting transfers between devices: 14 us -> 10.9 us  [route_blocks(): lax.all_to_all(early.reshape(DEVICES, EXTRA, HID), EVERY, 0, 0, tiled=True)]
    unnamed x22 -> x34, local copies, waits for them, and re-layouts: 4.59 us -> 6.18 us
    pallas_call x33 -> x34, Pallas kernels: 51.1 us -> 52.7 us  [call(): return lambda *arrays: run(*after, *arrays)]
  transfers between devices with their start and end apart: 54 -> 54, of which waited for: 22 -> 19; matrix products, arithmetic and copies ran while one was open for 1% -> 1% of each run, Pallas kernels for 13% -> 13%
where the time goes in v5:
time: 292 us; the launch traced here: 289 us
  waiting for transfers between devices  122 us (42%)
  starting transfers between devices  101 us (35%)
  Pallas kernels  52.7 us (18%)
  local copies, waits for them, and re-layouts  7.45 us (3%)
    pallas_call x34, Pallas kernels, call(): return lambda *arrays: run(*after, *arrays)  52.7 us
    all_to_all x1, waiting for transfers between devices, route_blocks(): lax.all_to_all(buffer.reshape(DEVICES, EXTRA + 16, HID), EVERY, 0, 0, til...  48 us
    ppermute x30, starting transfers between devices, shift_z(): lax.ppermute(block, 'section', [(i, (i + step) % 4) for i in range(4)])  39.9 us
    all_to_all x1, waiting for transfers between devices, route_blocks(): lax.all_to_all(early.reshape(DEVICES, EXTRA, HID), EVERY, 0, 0, tiled=True)  39.2 us
    ppermute x12, starting transfers between devices, shift_xy(): return lax.ppermute(block, 'replica', route)  32.4 us
    ppermute x30, waiting for transfers between devices, shift_z(): lax.ppermute(block, 'section', [(i, (i + step) % 4) for i in range(4)])  20.1 us
    all_to_all x1, starting transfers between devices, route_blocks(): lax.all_to_all(early.reshape(DEVICES, EXTRA, HID), EVERY, 0, 0, tiled=True)  10.9 us
    all_to_all x1, waiting for transfers between devices, route_blocks(): got = lax.all_to_all(labels, EVERY, 0, 0, tiled=True)  8.07 us
  transfers between devices with their start and end apart: 54, of which 19 were waited for; matrix products, arithmetic and copies ran while one was open for 1% of the time, Pallas kernels for 13%

profile of v5, /device:TPU:8, one launch (start us, length us, event | category | flops | bytes accessed | tf_op | source)
XLA Modules:
  0.0 288.7 jit_solution(1189927717430282838)
XLA Ops:
  2.3 4.8 %shard_map.115 = bf16[32,4,64,256]{3,2,1,0:T(8,128)(2,1)} custom-call(s32[8,128]{1,0:T(8,128)S(1)} %get-tuple-element.113.refs_0_.refs_1_, bf16[112,4,32,256]{3,2,1,0:T(8,128)(2,1)} %bitcast.38), custom_call_target="tpu_custom_call" | custom-call | bytes 12580000 | tf_op jit(solution)/shard_map/pallas_call | solution.py:70
  7.9 10.9 %all-to-all-start.1 = ((bf16[128,64,256]{2,1,0:T(8,128)(2,1)}), bf16[128,64,256]{2,1,0:T(8,128)(2,1)}, u32[]{:S(2)}, u32[]{:S(2)}) async-start(bf16[128,64,256]{2,1,0:T(8,128)(2,1)} %bitcast.45), calls=%async_computation.1 | async-start | bytes 8388608 | tf_op jit(solution)/shard_map/all_to_all | solution.py:404
  21.4 4.7 %collective-permute-start.5 = (bf16[32,4,16,256]{3,2,1,0:T(8,128)(2,1)}, bf16[32,4,16,256]{3,2,1,0:T(8,128)(2,1)S(1)}, u32[]{:S(2)}, u32[]{:S(2)}) collective-permute-start(bf16[32,4,16,256]{3,2,1,0:T(8,128)(2,1)} %get-tuple-element.104), channel_id=1, source_target_pairs={{0,32},{4,100},{8,40},{12,108},{16,48},{20,116},{24,56},{28,124},{... | collective-permute-start | bytes 3145736 | tf_op jit(solution)/shard_map/ppermute | solution.py:106
  26.1 4.7 %shard_map.116.refs_6_ = bf16[32,4,80,256]{3,2,1,0:T(8,128)(2,1)} custom-call(s32[8,128]{1,0:T(8,128)S(1)} %get-tuple-element.113.refs_0_.refs_1_, bf16[112,4,32,256]{3,2,1,0:T(8,128)(2,1)} %bitcast.41), custom_call_target="tpu_custom_call" | custom-call | bytes 12580000 | tf_op jit(solution)/shard_map/pallas_call | solution.py:70
  30.9 39.2 %all-to-all-done.1.refs_2_.refs_4_ = bf16[128,64,256]{2,1,0:T(8,128)(2,1)} async-done(((bf16[128,64,256]{2,1,0:T(8,128)(2,1)}), bf16[128,64,256]{2,1,0:T(8,128)(2,1)}, u32[]{:S(2)}, u32[]{:S(2)}) %all-to-all-start.1) | async-done | bytes 4194336 | tf_op jit(solution)/shard_map/all_to_all | solution.py:404
  70.0 5.6 %all-to-all-start.2 = ((s32[128,1,16]{2,1,0:T(1,128)}), s32[128,1,16]{2,1,0:T(1,128)S(1)}, u32[]{:S(2)}, u32[]{:S(2)}) async-start(s32[128,1,16]{2,1,0:T(1,128)} %bitcast.11), calls=%async_computation.2 | async-start | bytes 131072 | tf_op jit(solution)/shard_map/all_to_all | solution.py:407
  76.3 8.1 %all-to-all-done.2 = s32[128,1,16]{2,1,0:T(1,128)S(1)} async-done(((s32[128,1,16]{2,1,0:T(1,128)}), s32[128,1,16]{2,1,0:T(1,128)S(1)}, u32[]{:S(2)}, u32[]{:S(2)}) %all-to-all-start.2) | async-done | bytes 8224 | tf_op jit(solution)/shard_map/all_to_all | solution.py:407
  86.5 6.6 %all-to-all-start.3 = ((bf16[128,80,256]{2,1,0:T(8,128)(2,1)}), bf16[128,80,256]{2,1,0:T(8,128)(2,1)}, u32[]{:S(2)}, u32[]{:S(2)}) async-start(bf16[128,80,256]{2,1,0:T(8,128)(2,1)} %bitcast.43), calls=%async_computation.3 | async-start | bytes 10485760 | tf_op jit(solution)/shard_map/all_to_all | solution.py:417
  96.8 3.2 %collective-permute-start.1 = (bf16[2,4,32,256]{3,2,1,0:T(8,128)(2,1)}, bf16[2,4,32,256]{3,2,1,0:T(8,128)(2,1)S(1)}, u32[]{:S(2)}, u32[]{:S(2)}) collective-permute-start(bf16[2,4,32,256]{3,2,1,0:T(8,128)(2,1)} %get-tuple-element.91), channel_id=1, source_target_pairs={{0,2},{1,3},{2,0},{3,1},{4,6},{5,7},{6,4},{7,5},{8,10},{9,11},{10,... | collective-permute-start | bytes 393224 | tf_op jit(solution)/shard_map/ppermute | solution.py:88
  107.5 48.0 %all-to-all-done.3.refs_3_.refs_5_ = bf16[128,80,256]{2,1,0:T(8,128)(2,1)} async-done(((bf16[128,80,256]{2,1,0:T(8,128)(2,1)}), bf16[128,80,256]{2,1,0:T(8,128)(2,1)}, u32[]{:S(2)}, u32[]{:S(2)}) %all-to-all-start.3) | async-done | bytes 5242912 | tf_op jit(solution)/shard_map/all_to_all | solution.py:417
  156.1 2.2 shard_map.123.refs_1_
  159.4 2.9 %collective-permute-start.9 = (bf16[128,384]{1,0:T(8,128)(2,1)S(1)}, bf16[128,384]{1,0:T(8,128)(2,1)S(1)}, u32[]{:S(2)}, u32[]{:S(2)}) collective-permute-start(bf16[128,384]{1,0:T(8,128)(2,1)S(1)} %shard_map.124.refs_6_), channel_id=1, source_target_pairs={{0,3},{1,0},{2,1},{3,2},{4,7},{5,4},{6,5},{7,6},{8,11},{9,8},{10,9... | collective-permute-start | bytes 294920 | tf_op jit(solution)/shard_map/ppermute | solution.py:88
  162.3 2.0 shard_map.121.refs_4_.refs_12_
  177.2 2.2 collective-permute-start.16
  183.4 2.0 shard_map.131.refs_3_
  191.8 3.3 %collective-permute-done.19.refs_3_ = bf16[128,640]{1,0:T(8,128)(2,1)S(1)} collective-permute-done((bf16[128,640]{1,0:T(8,128)(2,1)S(1)}, bf16[128,640]{1,0:T(8,128)(2,1)S(1)}, u32[]{:S(2)}, u32[]{:S(2)}) %collective-permute-start.19) | collective-permute-done | bytes 163872 | tf_op jit(solution)/shard_map/ppermute | solution.py:88
  202.3 2.1 collective-permute-done.22.refs_3_
  210.6 2.7 collective-permute-done.27.refs_5_
  213.3 2.4 collective-permute-done.25.refs_3_
  220.2 3.0 %shard_map.137 = (bf16[4,2,256,128]{3,2,1,0:T(8,128)(2,1)S(1)}, bf16[4,2,256,128]{3,2,1,0:T(8,128)(2,1)}, bf16[4,2,256,128]{3,2,1,0:T(8,128)(2,1)S(1)}, bf16[4,2,256,128]{3,2,1,0:T(8,128)(2,1)S(1)}) custom-call(s32[5]{0:T(128)S(1)} %copy-done.8, bf16[128,4096]{1,0:T(8,128)(2,1)S(1)} %get-tuple-element.127.refs_1_, ...), custom_call_target="tpu_custom_call" | custom-call | bytes 11220000 | tf_op jit(solution)/shard_map/pallas_call | solution.py:70
  226.4 3.0 %collective-permute-start.34 = (bf16[4,2,256,128]{3,2,1,0:T(8,128)(2,1)}, bf16[4,2,256,128]{3,2,1,0:T(8,128)(2,1)}, u32[]{:S(2)}, u32[]{:S(2)}) collective-permute-start(bf16[4,2,256,128]{3,2,1,0:T(8,128)(2,1)} %copy-done.10), channel_id=1, source_target_pairs={{0,64},{4,68},{8,72},{12,76},{16,80},{20,84},{24,88},{28,92},{32,9... | collective-permute-start | bytes 1572872 | tf_op jit(solution)/shard_map/ppermute | solution.py:84
  229.4 3.4 %shard_map.139 = (bf16[4,2,256,128]{3,2,1,0:T(8,128)(2,1)S(1)}, bf16[4,2,256,128]{3,2,1,0:T(8,128)(2,1)}, bf16[4,2,256,128]{3,2,1,0:T(8,128)(2,1)}, bf16[4,2,256,128]{3,2,1,0:T(8,128)(2,1)}) custom-call(s32[5]{0:T(128)S(1)} %copy-done.8, bf16[16,256,128]{2,1,0:T(8,128)(2,1)S(1)} %shard_map.135.refs_1_, bf16[128,4096]{1,0:T(8,128)(2,1)S(1)} %shard_map.138.refs_2_, ...), custom_call_target="tpu_custom_call" | custom-call | bytes 6800000 | tf_op jit(solution)/shard_map/pallas_call | solution.py:70
  234.1 5.1 %collective-permute-start.40 = (bf16[4,2,256,128]{3,2,1,0:T(8,128)(2,1)}, bf16[4,2,256,128]{3,2,1,0:T(8,128)(2,1)S(1)}, u32[]{:S(2)}, u32[]{:S(2)}) collective-permute-start(bf16[4,2,256,128]{3,2,1,0:T(8,128)(2,1)} %get-tuple-element.151), channel_id=1, source_target_pairs={{0,16},{4,20},{8,24},{12,28},{16,0},{20,4},{24,8},{28,12},{32,48},... | collective-permute-start | bytes 1572872 | tf_op jit(solution)/shard_map/ppermute | solution.py:84
  240.7 4.3 %collective-permute-start.41 = (bf16[4,2,256,128]{3,2,1,0:T(8,128)(2,1)}, bf16[4,2,256,128]{3,2,1,0:T(8,128)(2,1)S(1)}, u32[]{:S(2)}, u32[]{:S(2)}) collective-permute-start(bf16[4,2,256,128]{3,2,1,0:T(8,128)(2,1)} %get-tuple-element.152), channel_id=1, source_target_pairs={{0,24},{4,28},{8,0},{12,4},{16,8},{20,12},{24,16},{28,20},{32,56},... | collective-permute-start | bytes 1572872 | tf_op jit(solution)/shard_map/ppermute | solution.py:84
  248.1 5.0 %collective-permute-done.34.refs_5_ = bf16[4,2,256,128]{3,2,1,0:T(8,128)(2,1)} collective-permute-done((bf16[4,2,256,128]{3,2,1,0:T(8,128)(2,1)}, bf16[4,2,256,128]{3,2,1,0:T(8,128)(2,1)}, u32[]{:S(2)}, u32[]{:S(2)}) %collective-permute-start.34) | collective-permute-done | bytes 524320 | tf_op jit(solution)/shard_map/ppermute | solution.py:84
  255.2 5.9 %collective-permute-start.37 = (bf16[2,256,128]{2,1,0:T(8,128)(2,1)S(1)}, bf16[2,256,128]{2,1,0:T(8,128)(2,1)S(1)}, u32[]{:S(2)}, u32[]{:S(2)}) collective-permute-start(bf16[2,256,128]{2,1,0:T(8,128)(2,1)S(1)} %get-tuple-element.148), channel_id=1, source_target_pairs={{0,16},{4,20},{8,24},{12,28},{16,0},{20,4},{24,8},{28,12},{32,48},... | collective-permute-start | bytes 393224 | tf_op jit(solution)/shard_map/ppermute | solution.py:84
  261.2 3.4 %collective-permute-start.38 = (bf16[2,256,128]{2,1,0:T(8,128)(2,1)S(1)}, bf16[2,256,128]{2,1,0:T(8,128)(2,1)S(1)}, u32[]{:S(2)}, u32[]{:S(2)}) collective-permute-start(bf16[2,256,128]{2,1,0:T(8,128)(2,1)S(1)} %get-tuple-element.149), channel_id=1, source_target_pairs={{0,24},{4,28},{8,0},{12,4},{16,8},{20,12},{24,16},{28,20},{32,56},... | collective-permute-start | bytes 393224 | tf_op jit(solution)/shard_map/ppermute | solution.py:84
  265.4 4.8 %collective-permute-start.42 = (bf16[2,256,128]{2,1,0:T(8,128)(2,1)S(1)}, bf16[2,256,128]{2,1,0:T(8,128)(2,1)S(1)}, u32[]{:S(2)}, u32[]{:S(2)}) collective-permute-start(bf16[2,256,128]{2,1,0:T(8,128)(2,1)S(1)} %get-tuple-element.154), channel_id=1, source_target_pairs={{0,32},{4,36},{8,40},{12,44},{16,48},{20,52},{24,56},{28,60},{32,6... | collective-permute-start | bytes 393224 | tf_op jit(solution)/shard_map/ppermute | solution.py:84
  271.3 2.8 collective-permute-start.44
  274.1 3.2 %collective-permute-start.49 = (bf16[3,4,32,256]{3,2,1,0:T(8,128)(2,1)S(1)}, bf16[3,4,32,256]{3,2,1,0:T(8,128)(2,1)S(1)}, u32[]{:S(2)}, u32[]{:S(2)}) collective-permute-start(bf16[3,4,32,256]{3,2,1,0:T(8,128)(2,1)S(1)} %get-tuple-element.162), channel_id=1, source_target_pairs={{0,2},{1,3},{2,0},{3,1},{4,6},{5,7},{6,4},{7,5},{8,10},{9,11},{10,... | collective-permute-start | bytes 589832 | tf_op jit(solution)/shard_map/ppermute | solution.py:88
  282.1 2.2 collective-permute-start.47
  286.6 2.1 shard_map.144
  (170 shorter events, 80.8 us)
Async XLA Ops:
  7.8 12.2 %collective-permute-start.4 = (bf16[4,32,4,16,256]{4,3,2,1,0:T(8,128)(2,1)}, bf16[4,32,4,16,256]{4,3,2,1,0:T(8,128)(2,1)}, u32[]{:S(2)}, u32[]{:S(2)}) collective-permute-start(bf16[4,32,4,16,256]{4,3,2,1,0:T(8,128)(2,1)} %shard_map.117.refs_0_), channel_id=1, source_target_pairs={{0,4},{4,0},{8,12},{12,8},{16,20},{20,16},{24,28},{28,24},{32,36},... | collective-permute-start | bytes 12582920 | tf_op jit(solution)/shard_map/ppermute | solution.py:110
  7.9 62.1 %all-to-all-start.1 = ((bf16[128,64,256]{2,1,0:T(8,128)(2,1)}), bf16[128,64,256]{2,1,0:T(8,128)(2,1)}, u32[]{:S(2)}, u32[]{:S(2)}) async-start(bf16[128,64,256]{2,1,0:T(8,128)(2,1)} %bitcast.45), calls=%async_computation.1 | async-start | bytes 8388608 | tf_op jit(solution)/shard_map/all_to_all | solution.py:404
  21.4 63.0 %collective-permute-start.5 = (bf16[32,4,16,256]{3,2,1,0:T(8,128)(2,1)}, bf16[32,4,16,256]{3,2,1,0:T(8,128)(2,1)S(1)}, u32[]{:S(2)}, u32[]{:S(2)}) collective-permute-start(bf16[32,4,16,256]{3,2,1,0:T(8,128)(2,1)} %get-tuple-element.104), channel_id=1, source_target_pairs={{0,32},{4,100},{8,40},{12,108},{16,48},{20,116},{24,56},{28,124},{... | collective-permute-start | bytes 3145736 | tf_op jit(solution)/shard_map/ppermute | solution.py:106
  26.1 58.2 %collective-permute-start.6 = (bf16[32,4,16,256]{3,2,1,0:T(8,128)(2,1)}, bf16[32,4,16,256]{3,2,1,0:T(8,128)(2,1)}, u32[]{:S(2)}, u32[]{:S(2)}) collective-permute-start(bf16[32,4,16,256]{3,2,1,0:T(8,128)(2,1)} %get-tuple-element.105), channel_id=1, source_target_pairs={{0,8},{4,28},{8,16},{12,4},{16,24},{20,12},{24,0},{28,20},{32,40},... | collective-permute-start | bytes 3145736 | tf_op jit(solution)/shard_map/ppermute | solution.py:106
  26.1 58.2 %collective-permute-start.7 = (bf16[32,4,16,256]{3,2,1,0:T(8,128)(2,1)}, bf16[32,4,16,256]{3,2,1,0:T(8,128)(2,1)}, u32[]{:S(2)}, u32[]{:S(2)}) collective-permute-start(bf16[32,4,16,256]{3,2,1,0:T(8,128)(2,1)} %get-tuple-element.106), channel_id=1, source_target_pairs={{0,1},{1,2},{2,3},{3,0},{4,7},{5,4},{6,5},{7,6},{8,9},{9,10},{10,1... | collective-permute-start | bytes 3145736 | tf_op jit(solution)/shard_map/ppermute | solution.py:98
  70.0 14.3 %all-to-all-start.2 = ((s32[128,1,16]{2,1,0:T(1,128)}), s32[128,1,16]{2,1,0:T(1,128)S(1)}, u32[]{:S(2)}, u32[]{:S(2)}) async-start(s32[128,1,16]{2,1,0:T(1,128)} %bitcast.11), calls=%async_computation.2 | async-start | bytes 131072 | tf_op jit(solution)/shard_map/all_to_all | solution.py:407
  86.5 69.0 %all-to-all-start.3 = ((bf16[128,80,256]{2,1,0:T(8,128)(2,1)}), bf16[128,80,256]{2,1,0:T(8,128)(2,1)}, u32[]{:S(2)}, u32[]{:S(2)}) async-start(bf16[128,80,256]{2,1,0:T(8,128)(2,1)} %bitcast.43), calls=%async_computation.3 | async-start | bytes 10485760 | tf_op jit(solution)/shard_map/all_to_all | solution.py:417
  95.1 67.2 %collective-permute-start = (bf16[2,4,32,256]{3,2,1,0:T(8,128)(2,1)}, bf16[2,4,32,256]{3,2,1,0:T(8,128)(2,1)S(1)}, u32[]{:S(2)}, u32[]{:S(2)}) collective-permute-start(bf16[2,4,32,256]{3,2,1,0:T(8,128)(2,1)} %get-tuple-element.90), channel_id=1, source_target_pairs={{0,1},{1,2},{2,3},{3,0},{4,5},{5,6},{6,7},{7,4},{8,9},{9,10},{10,1... | collective-permute-start | bytes 393224 | tf_op jit(solution)/shard_map/ppermute | solution.py:88
  96.8 69.5 %collective-permute-start.1 = (bf16[2,4,32,256]{3,2,1,0:T(8,128)(2,1)}, bf16[2,4,32,256]{3,2,1,0:T(8,128)(2,1)S(1)}, u32[]{:S(2)}, u32[]{:S(2)}) collective-permute-start(bf16[2,4,32,256]{3,2,1,0:T(8,128)(2,1)} %get-tuple-element.91), channel_id=1, source_target_pairs={{0,2},{1,3},{2,0},{3,1},{4,6},{5,7},{6,4},{7,5},{8,10},{9,11},{10,... | collective-permute-start | bytes 393224 | tf_op jit(solution)/shard_map/ppermute | solution.py:88
  100.0 66.3 %collective-permute-start.2 = (bf16[2,4,32,256]{3,2,1,0:T(8,128)(2,1)}, bf16[2,4,32,256]{3,2,1,0:T(8,128)(2,1)S(1)}, u32[]{:S(2)}, u32[]{:S(2)}) collective-permute-start(bf16[2,4,32,256]{3,2,1,0:T(8,128)(2,1)} %get-tuple-element.92), channel_id=1, source_target_pairs={{0,3},{1,0},{2,1},{3,2},{4,7},{5,4},{6,5},{7,6},{8,11},{9,8},{10,9... | collective-permute-start | bytes 393224 | tf_op jit(solution)/shard_map/ppermute | solution.py:88
  158.7 7.6 %collective-permute-start.10 = (bf16[128,384]{1,0:T(8,128)(2,1)S(1)}, bf16[128,384]{1,0:T(8,128)(2,1)S(1)}, u32[]{:S(2)}, u32[]{:S(2)}) collective-permute-start(bf16[128,384]{1,0:T(8,128)(2,1)S(1)} %shard_map.124.refs_6_), channel_id=1, source_target_pairs={{0,2},{1,3},{2,0},{3,1},{4,6},{5,7},{6,4},{7,5},{8,10},{9,11},{10,... | collective-permute-start | bytes 294920 | tf_op jit(solution)/shard_map/ppermute | solution.py:88
  177.2 10.2 %collective-permute-start.16 = (bf16[128,384]{1,0:T(8,128)(2,1)S(1)}, bf16[128,384]{1,0:T(8,128)(2,1)S(1)}, u32[]{:S(2)}, u32[]{:S(2)}) collective-permute-start(bf16[128,384]{1,0:T(8,128)(2,1)S(1)} %get-tuple-element.118.refs_5_), channel_id=1, source_target_pairs={{0,2},{1,3},{2,0},{3,1},{4,6},{5,7},{6,4},{7,5},{8,10},{9,11},{10,... | collective-permute-start | bytes 294920 | tf_op jit(solution)/shard_map/ppermute | solution.py:88
  179.4 8.0 %collective-permute-start.15 = (bf16[128,384]{1,0:T(8,128)(2,1)S(1)}, bf16[128,384]{1,0:T(8,128)(2,1)S(1)}, u32[]{:S(2)}, u32[]{:S(2)}) collective-permute-start(bf16[128,384]{1,0:T(8,128)(2,1)S(1)} %get-tuple-element.118.refs_5_), channel_id=1, source_target_pairs={{0,3},{1,0},{2,1},{3,2},{4,7},{5,4},{6,5},{7,6},{8,11},{9,8},{10,9... | collective-permute-start | bytes 294920 | tf_op jit(solution)/shard_map/ppermute | solution.py:88
  189.7 7.2 %collective-permute-start.18 = (bf16[128,640]{1,0:T(8,128)(2,1)S(1)}, bf16[128,640]{1,0:T(8,128)(2,1)S(1)}, u32[]{:S(2)}, u32[]{:S(2)}) collective-permute-start(bf16[128,640]{1,0:T(8,128)(2,1)S(1)} %get-tuple-element.119.refs_0_), channel_id=1, source_target_pairs={{0,3},{1,0},{2,1},{3,2},{4,7},{5,4},{6,5},{7,6},{8,11},{9,8},{10,9... | collective-permute-start | bytes 491528 | tf_op jit(solution)/shard_map/ppermute | solution.py:88
  202.3 13.4 %collective-permute-start.24 = (bf16[128,4096]{1,0:T(8,128)(2,1)S(1)}, bf16[128,4096]{1,0:T(8,128)(2,1)S(1)}, u32[]{:S(2)}, u32[]{:S(2)}) collective-permute-start(bf16[128,4096]{1,0:T(8,128)(2,1)S(1)} %get-tuple-element.127.refs_1_), channel_id=1, source_target_pairs={{0,4},{4,0},{8,12},{12,8},{16,20},{20,16},{24,28},{28,24},{32,36},... | collective-permute-start | bytes 3145736 | tf_op jit(solution)/shard_map/ppermute | solution.py:110
  207.2 8.5 %collective-permute-start.23 = (bf16[128,4096]{1,0:T(8,128)(2,1)S(1)}, bf16[128,4096]{1,0:T(8,128)(2,1)S(1)}, u32[]{:S(2)}, u32[]{:S(2)}) collective-permute-start(bf16[128,4096]{1,0:T(8,128)(2,1)S(1)} %get-tuple-element.126.refs_1_), channel_id=1, source_target_pairs={{0,4},{4,0},{8,12},{12,8},{16,20},{20,16},{24,28},{28,24},{32,36},... | collective-permute-start | bytes 3145736 | tf_op jit(solution)/shard_map/ppermute | solution.py:110
  216.6 7.4 %collective-permute-start.31 = (bf16[128,256]{1,0:T(8,128)(2,1)S(1)}, bf16[128,256]{1,0:T(8,128)(2,1)S(1)}, u32[]{:S(2)}, u32[]{:S(2)}) collective-permute-start(bf16[128,256]{1,0:T(8,128)(2,1)S(1)} %get-tuple-element.135.refs_2_), channel_id=1, source_target_pairs={{0,2},{1,3},{2,0},{3,1},{4,6},{5,7},{6,4},{7,5},{8,10},{9,11},{10,... | collective-permute-start | bytes 196616 | tf_op jit(solution)/shard_map/ppermute | solution.py:88
  225.0 15.7 %collective-permute-start.33 = (bf16[4,2,256,128]{3,2,1,0:T(8,128)(2,1)}, bf16[4,2,256,128]{3,2,1,0:T(8,128)(2,1)}, u32[]{:S(2)}, u32[]{:S(2)}) collective-permute-start(bf16[4,2,256,128]{3,2,1,0:T(8,128)(2,1)} %get-tuple-element.143), channel_id=1, source_target_pairs={{0,32},{4,36},{8,40},{12,44},{16,48},{20,52},{24,56},{28,60},{32,6... | collective-permute-start | bytes 1572872 | tf_op jit(solution)/shard_map/ppermute | solution.py:84
  226.4 26.7 %collective-permute-start.34 = (bf16[4,2,256,128]{3,2,1,0:T(8,128)(2,1)}, bf16[4,2,256,128]{3,2,1,0:T(8,128)(2,1)}, u32[]{:S(2)}, u32[]{:S(2)}) collective-permute-start(bf16[4,2,256,128]{3,2,1,0:T(8,128)(2,1)} %copy-done.10), channel_id=1, source_target_pairs={{0,64},{4,68},{8,72},{12,76},{16,80},{20,84},{24,88},{28,92},{32,9... | collective-permute-start | bytes 1572872 | tf_op jit(solution)/shard_map/ppermute | solution.py:84
  229.4 23.7 %collective-permute-start.35 = (bf16[4,2,256,128]{3,2,1,0:T(8,128)(2,1)}, bf16[4,2,256,128]{3,2,1,0:T(8,128)(2,1)}, u32[]{:S(2)}, u32[]{:S(2)}) collective-permute-start(bf16[4,2,256,128]{3,2,1,0:T(8,128)(2,1)} %copy-done.9), channel_id=1, source_target_pairs={{0,96},{4,100},{8,104},{12,108},{16,112},{20,116},{24,120},{28,124... | collective-permute-start | bytes 1572872 | tf_op jit(solution)/shard_map/ppermute | solution.py:84
  232.8 28.4 %collective-permute-start.39 = (bf16[4,2,256,128]{3,2,1,0:T(8,128)(2,1)}, bf16[4,2,256,128]{3,2,1,0:T(8,128)(2,1)S(1)}, u32[]{:S(2)}, u32[]{:S(2)}) collective-permute-start(bf16[4,2,256,128]{3,2,1,0:T(8,128)(2,1)} %get-tuple-element.150), channel_id=1, source_target_pairs={{0,8},{4,12},{8,16},{12,20},{16,24},{20,28},{24,0},{28,4},{32,40},... | collective-permute-start | bytes 1572872 | tf_op jit(solution)/shard_map/ppermute | solution.py:84
  234.1 30.5 %collective-permute-start.40 = (bf16[4,2,256,128]{3,2,1,0:T(8,128)(2,1)}, bf16[4,2,256,128]{3,2,1,0:T(8,128)(2,1)S(1)}, u32[]{:S(2)}, u32[]{:S(2)}) collective-permute-start(bf16[4,2,256,128]{3,2,1,0:T(8,128)(2,1)} %get-tuple-element.151), channel_id=1, source_target_pairs={{0,16},{4,20},{8,24},{12,28},{16,0},{20,4},{24,8},{28,12},{32,48},... | collective-permute-start | bytes 1572872 | tf_op jit(solution)/shard_map/ppermute | solution.py:84
  240.7 23.9 %collective-permute-start.41 = (bf16[4,2,256,128]{3,2,1,0:T(8,128)(2,1)}, bf16[4,2,256,128]{3,2,1,0:T(8,128)(2,1)S(1)}, u32[]{:S(2)}, u32[]{:S(2)}) collective-permute-start(bf16[4,2,256,128]{3,2,1,0:T(8,128)(2,1)} %get-tuple-element.152), channel_id=1, source_target_pairs={{0,24},{4,28},{8,0},{12,4},{16,8},{20,12},{24,16},{28,20},{32,56},... | collective-permute-start | bytes 1572872 | tf_op jit(solution)/shard_map/ppermute | solution.py:84
  254.7 16.6 %collective-permute-start.36 = (bf16[2,256,128]{2,1,0:T(8,128)(2,1)S(1)}, bf16[2,256,128]{2,1,0:T(8,128)(2,1)S(1)}, u32[]{:S(2)}, u32[]{:S(2)}) collective-permute-start(bf16[2,256,128]{2,1,0:T(8,128)(2,1)S(1)} %get-tuple-element.147), channel_id=1, source_target_pairs={{0,8},{4,12},{8,16},{12,20},{16,24},{20,28},{24,0},{28,4},{32,40},... | collective-permute-start | bytes 393224 | tf_op jit(solution)/shard_map/ppermute | solution.py:84
  255.2 16.1 %collective-permute-start.37 = (bf16[2,256,128]{2,1,0:T(8,128)(2,1)S(1)}, bf16[2,256,128]{2,1,0:T(8,128)(2,1)S(1)}, u32[]{:S(2)}, u32[]{:S(2)}) collective-permute-start(bf16[2,256,128]{2,1,0:T(8,128)(2,1)S(1)} %get-tuple-element.148), channel_id=1, source_target_pairs={{0,16},{4,20},{8,24},{12,28},{16,0},{20,4},{24,8},{28,12},{32,48},... | collective-permute-start | bytes 393224 | tf_op jit(solution)/shard_map/ppermute | solution.py:84
  261.2 12.9 %collective-permute-start.38 = (bf16[2,256,128]{2,1,0:T(8,128)(2,1)S(1)}, bf16[2,256,128]{2,1,0:T(8,128)(2,1)S(1)}, u32[]{:S(2)}, u32[]{:S(2)}) collective-permute-start(bf16[2,256,128]{2,1,0:T(8,128)(2,1)S(1)} %get-tuple-element.149), channel_id=1, source_target_pairs={{0,24},{4,28},{8,0},{12,4},{16,8},{20,12},{24,16},{28,20},{32,56},... | collective-permute-start | bytes 393224 | tf_op jit(solution)/shard_map/ppermute | solution.py:84
  265.4 11.8 %collective-permute-start.42 = (bf16[2,256,128]{2,1,0:T(8,128)(2,1)S(1)}, bf16[2,256,128]{2,1,0:T(8,128)(2,1)S(1)}, u32[]{:S(2)}, u32[]{:S(2)}) collective-permute-start(bf16[2,256,128]{2,1,0:T(8,128)(2,1)S(1)} %get-tuple-element.154), channel_id=1, source_target_pairs={{0,32},{4,36},{8,40},{12,44},{16,48},{20,52},{24,56},{28,60},{32,6... | collective-permute-start | bytes 393224 | tf_op jit(solution)/shard_map/ppermute | solution.py:84
  270.2 12.0 %collective-permute-start.48 = (bf16[3,4,32,256]{3,2,1,0:T(8,128)(2,1)S(1)}, bf16[3,4,32,256]{3,2,1,0:T(8,128)(2,1)S(1)}, u32[]{:S(2)}, u32[]{:S(2)}) collective-permute-start(bf16[3,4,32,256]{3,2,1,0:T(8,128)(2,1)S(1)} %get-tuple-element.161), channel_id=1, source_target_pairs={{0,1},{1,2},{2,3},{3,0},{4,5},{5,6},{6,7},{7,4},{8,9},{9,10},{10,1... | collective-permute-start | bytes 589832 | tf_op jit(solution)/shard_map/ppermute | solution.py:88
  271.3 7.5 %collective-permute-start.43 = (bf16[2,256,128]{2,1,0:T(8,128)(2,1)S(1)}, bf16[2,256,128]{2,1,0:T(8,128)(2,1)S(1)}, u32[]{:S(2)}, u32[]{:S(2)}) collective-permute-start(bf16[2,256,128]{2,1,0:T(8,128)(2,1)S(1)} %get-tuple-element.155), channel_id=1, source_target_pairs={{0,64},{4,68},{8,72},{12,76},{16,80},{20,84},{24,88},{28,92},{32,9... | collective-permute-start | bytes 393224 | tf_op jit(solution)/shard_map/ppermute | solution.py:84
  271.3 7.5 %collective-permute-start.44 = (bf16[2,256,128]{2,1,0:T(8,128)(2,1)S(1)}, bf16[2,256,128]{2,1,0:T(8,128)(2,1)S(1)}, u32[]{:S(2)}, u32[]{:S(2)}) collective-permute-start(bf16[2,256,128]{2,1,0:T(8,128)(2,1)S(1)} %get-tuple-element.156), channel_id=1, source_target_pairs={{0,96},{4,100},{8,104},{12,108},{16,112},{20,116},{24,120},{28,124... | collective-permute-start | bytes 393224 | tf_op jit(solution)/shard_map/ppermute | solution.py:84
  274.1 10.3 %collective-permute-start.49 = (bf16[3,4,32,256]{3,2,1,0:T(8,128)(2,1)S(1)}, bf16[3,4,32,256]{3,2,1,0:T(8,128)(2,1)S(1)}, u32[]{:S(2)}, u32[]{:S(2)}) collective-permute-start(bf16[3,4,32,256]{3,2,1,0:T(8,128)(2,1)S(1)} %get-tuple-element.162), channel_id=1, source_target_pairs={{0,2},{1,3},{2,0},{3,1},{4,6},{5,7},{6,4},{7,5},{8,10},{9,11},{10,... | collective-permute-start | bytes 589832 | tf_op jit(solution)/shard_map/ppermute | solution.py:88
  277.2 7.1 %collective-permute-start.50 = (bf16[3,4,32,256]{3,2,1,0:T(8,128)(2,1)S(1)}, bf16[3,4,32,256]{3,2,1,0:T(8,128)(2,1)S(1)}, u32[]{:S(2)}, u32[]{:S(2)}) collective-permute-start(bf16[3,4,32,256]{3,2,1,0:T(8,128)(2,1)S(1)} %get-tuple-element.163), channel_id=1, source_target_pairs={{0,3},{1,0},{2,1},{3,2},{4,7},{5,4},{6,5},{7,6},{8,11},{9,8},{10,9... | collective-permute-start | bytes 589832 | tf_op jit(solution)/shard_map/ppermute | solution.py:88
  (39 other events, 199.5 us)

commit v6 on v5

--- a/solution.py
+++ b/solution.py
@@ -470,19 +470,21 @@
 def put_forward(message, layer_in, up_matrix):
     wide = layer_in.astype(f32)
     squares = jnp.sum(wide * wide, axis=1, keepdims=True)
-    high = squares.astype(bf16)
-    low = (squares - high.astype(f32)).astype(bf16)
-    lane = lax.broadcasted_iota(jnp.int32, (TOK, 128), 1)
-    message[:, 0:HID] = jnp.dot(layer_in, up_matrix, preferred_element_type=f32).astype(bf16)
-    message[:, HID : HID + 128] = jnp.where(
-        lane == 0, high.astype(f32), jnp.where(lane == 1, low.astype(f32), 0.0)
-    ).astype(bf16)
+    along = jnp.broadcast_to(squares, (TOK, 128)).T[0:16]
+    high = along.astype(bf16)
+    low = (along - high.astype(f32)).astype(bf16)
+    row = lax.broadcasted_iota(jnp.int32, (16, 128), 0)
+    both = jnp.where(row == 0, high.astype(f32), jnp.where(row == 1, low.astype(f32), 0.0))
+    message[0:TOK, 0:HID] = jnp.dot(layer_in, up_matrix, preferred_element_type=f32).astype(bf16)
+    message[TOK:, 0:128] = both.astype(bf16)
+    message[TOK:, 128:] = jnp.zeros((16, message.shape[1] - 128), bf16)
 
 
 def take_forward(total):
-    squares = total[:, HID : HID + 1] + total[:, HID + 1 : HID + 2]
+    along = total[TOK : TOK + 1, 0:128] + total[TOK + 1 : TOK + 2, 0:128]
+    squares = jnp.broadcast_to(along, (128, 128)).T[:, 0:1]
     inverse = lax.rsqrt(squares * (1.0 / D) + rms_eps)
-    pre = total[:, 0:HID] * inverse * SCALE_IN
+    pre = total[0:TOK, 0:HID] * inverse * SCALE_IN
     return pre, jax.nn.gelu(pre, approximate=True).astype(bf16), inverse
 
 
@@ -525,7 +527,7 @@
     messages, (act, pre, inverse, layer_out, message) = refs[:4], refs[4:]
     result = forward_step(messages, layer_in, out_matrix, act, pre, inverse, layer_out)
     put_forward(message, result, flat(up_next))
-    message[:, HID + 128 :] = jnp.dot(
+    message[0:TOK, HID:] = jnp.dot(
         cots[...], flat(out_next), preferred_element_type=f32
     ).astype(bf16)
 
@@ -537,7 +539,7 @@
         grad_out, layer_in, up_matrix, out_next, back, grad_in, message = refs
         pre_value, act_value, inverse_value = take_forward(total)
         back[:, LEFT:] = act_value
-        grad_act = total[:, HID + 128 :] * SCALE_OUT
+        grad_act = total[0:TOK, HID:] * SCALE_OUT
     else:
         act, pre, inverse, grad_out, layer_in, up_matrix, out_next, back, grad_in, message = refs
         back[:, LEFT:] = act[...]
@@ -785,7 +787,7 @@
     slots = jnp.arange(SECTIONS * OWN, dtype=jnp.int32)
     source = jnp.sum(jnp.where(table.reshape(1, -1) == slots[:, None], held[None, :], 0), axis=1)
     message = call(
-        open_kernel, struct((TOK, HID + 128), bf16), [VMEM] * 2, VMEM, us=0.3)(layer_0, weights[0][0])
+        open_kernel, struct((TOK + 16, HID), bf16), [VMEM] * 2, VMEM, us=0.3)(layer_0, weights[0][0])
     layers = [layer_0]
     acts, pres, inverses = [], [], []
     wide = struct((TOK, LEFT + HID), bf16)
@@ -802,7 +804,7 @@
                 struct((TOK, HID), f32),
                 struct((TOK, 128), f32),
                 narrow,
-                struct((TOK, 2 * HID + 128 if turn else HID + 128), bf16),
+                struct((TOK + 16, 2 * HID if turn else HID), bf16),
             ],
             [VMEM] * (7 + len(extra)),
             [VMEM] * 5,

time: 292 us -> 291 us (level)
  starting transfers between devices: 101 us -> 97.7 us
  waiting for transfers between devices: 122 us -> 125 us
    ppermute x12, starting transfers between devices: 32.4 us -> 29.1 us  [shift_xy(): return lax.ppermute(block, 'replica', route)]
  transfers between devices with their start and end apart: 54 -> 54, of which waited for: 19 -> 22; matrix products, arithmetic and copies ran while one was open for 1% -> 1% of each run, Pallas kernels for 13% -> 13%
where the time goes in v6:
time: 291 us; the launch traced here: 288 us
  waiting for transfers between devices  125 us (43%)
  starting transfers between devices  97.7 us (34%)
  Pallas kernels  52.7 us (18%)
  local copies, waits for them, and re-layouts  7.3 us (3%)
    pallas_call x34, Pallas kernels, call(): return lambda *arrays: run(*after, *arrays)  52.7 us
    all_to_all x1, waiting for transfers between devices, route_blocks(): lax.all_to_all(buffer.reshape(DEVICES, EXTRA + 16, HID), EVERY, 0, 0, til...  48 us
    ppermute x30, starting transfers between devices, shift_z(): lax.ppermute(block, 'section', [(i, (i + step) % 4) for i in range(4)])  40.1 us
    all_to_all x1, waiting for transfers between devices, route_blocks(): lax.all_to_all(early.reshape(DEVICES, EXTRA, HID), EVERY, 0, 0, tiled=True)  39.1 us
    ppermute x12, starting transfers between devices, shift_xy(): return lax.ppermute(block, 'replica', route)  29.1 us
    ppermute x30, waiting for transfers between devices, shift_z(): lax.ppermute(block, 'section', [(i, (i + step) % 4) for i in range(4)])  20.8 us
    all_to_all x1, starting transfers between devices, route_blocks(): lax.all_to_all(early.reshape(DEVICES, EXTRA, HID), EVERY, 0, 0, tiled=True)  11 us
    ppermute x12, waiting for transfers between devices, shift_xy(): return lax.ppermute(block, 'replica', route)  8.46 us
  transfers between devices with their start and end apart: 54, of which 22 were waited for; matrix products, arithmetic and copies ran while one was open for 1% of the time, Pallas kernels for 13%

profile of v6, /device:TPU:8, one launch (start us, length us, event | category | flops | bytes accessed | tf_op | source)
XLA Modules:
  0.0 288.1 jit_solution(11479206496951713663)
XLA Ops:
  2.3 4.7 %shard_map.115 = bf16[32,4,64,256]{3,2,1,0:T(8,128)(2,1)} custom-call(s32[8,128]{1,0:T(8,128)S(1)} %get-tuple-element.113.refs_0_.refs_1_, bf16[112,4,32,256]{3,2,1,0:T(8,128)(2,1)} %bitcast.38), custom_call_target="tpu_custom_call" | custom-call | bytes 12580000 | tf_op jit(solution)/shard_map/pallas_call | solution.py:70
  7.8 11.0 %all-to-all-start.1 = ((bf16[128,64,256]{2,1,0:T(8,128)(2,1)}), bf16[128,64,256]{2,1,0:T(8,128)(2,1)}, u32[]{:S(2)}, u32[]{:S(2)}) async-start(bf16[128,64,256]{2,1,0:T(8,128)(2,1)} %bitcast.45), calls=%async_computation.1 | async-start | bytes 8388608 | tf_op jit(solution)/shard_map/all_to_all | solution.py:404
  26.2 4.8 %shard_map.116.refs_6_ = bf16[32,4,80,256]{3,2,1,0:T(8,128)(2,1)} custom-call(s32[8,128]{1,0:T(8,128)S(1)} %get-tuple-element.113.refs_0_.refs_1_, bf16[112,4,32,256]{3,2,1,0:T(8,128)(2,1)} %bitcast.41), custom_call_target="tpu_custom_call" | custom-call | bytes 12580000 | tf_op jit(solution)/shard_map/pallas_call | solution.py:70
  31.0 39.1 %all-to-all-done.1.refs_2_.refs_4_ = bf16[128,64,256]{2,1,0:T(8,128)(2,1)} async-done(((bf16[128,64,256]{2,1,0:T(8,128)(2,1)}), bf16[128,64,256]{2,1,0:T(8,128)(2,1)}, u32[]{:S(2)}, u32[]{:S(2)}) %all-to-all-start.1) | async-done | bytes 4194336 | tf_op jit(solution)/shard_map/all_to_all | solution.py:404
  70.1 5.6 %all-to-all-start.2 = ((s32[128,1,16]{2,1,0:T(1,128)}), s32[128,1,16]{2,1,0:T(1,128)S(1)}, u32[]{:S(2)}, u32[]{:S(2)}) async-start(s32[128,1,16]{2,1,0:T(1,128)} %bitcast.11), calls=%async_computation.2 | async-start | bytes 131072 | tf_op jit(solution)/shard_map/all_to_all | solution.py:407
  76.4 8.1 %all-to-all-done.2 = s32[128,1,16]{2,1,0:T(1,128)S(1)} async-done(((s32[128,1,16]{2,1,0:T(1,128)}), s32[128,1,16]{2,1,0:T(1,128)S(1)}, u32[]{:S(2)}, u32[]{:S(2)}) %all-to-all-start.2) | async-done | bytes 8224 | tf_op jit(solution)/shard_map/all_to_all | solution.py:407
  86.6 6.7 %all-to-all-start.3 = ((bf16[128,80,256]{2,1,0:T(8,128)(2,1)}), bf16[128,80,256]{2,1,0:T(8,128)(2,1)}, u32[]{:S(2)}, u32[]{:S(2)}) async-start(bf16[128,80,256]{2,1,0:T(8,128)(2,1)} %bitcast.43), calls=%async_computation.3 | async-start | bytes 10485760 | tf_op jit(solution)/shard_map/all_to_all | solution.py:417
  96.9 3.2 %collective-permute-start.1 = (bf16[2,4,32,256]{3,2,1,0:T(8,128)(2,1)}, bf16[2,4,32,256]{3,2,1,0:T(8,128)(2,1)S(1)}, u32[]{:S(2)}, u32[]{:S(2)}) collective-permute-start(bf16[2,4,32,256]{3,2,1,0:T(8,128)(2,1)} %get-tuple-element.91), channel_id=1, source_target_pairs={{0,2},{1,3},{2,0},{3,1},{4,6},{5,7},{6,4},{7,5},{8,10},{9,11},{10,... | collective-permute-start | bytes 393224 | tf_op jit(solution)/shard_map/ppermute | solution.py:88
  107.7 48.0 %all-to-all-done.3.refs_3_.refs_5_ = bf16[128,80,256]{2,1,0:T(8,128)(2,1)} async-done(((bf16[128,80,256]{2,1,0:T(8,128)(2,1)}), bf16[128,80,256]{2,1,0:T(8,128)(2,1)}, u32[]{:S(2)}, u32[]{:S(2)}) %all-to-all-start.3) | async-done | bytes 5242912 | tf_op jit(solution)/shard_map/all_to_all | solution.py:417
  156.3 2.2 shard_map.123.refs_1_
  159.5 2.9 %collective-permute-start.9 = (bf16[144,256]{1,0:T(8,128)(2,1)S(1)}, bf16[144,256]{1,0:T(8,128)(2,1)S(1)}, u32[]{:S(2)}, u32[]{:S(2)}) collective-permute-start(bf16[144,256]{1,0:T(8,128)(2,1)S(1)} %shard_map.124.refs_6_), channel_id=1, source_target_pairs={{0,3},{1,0},{2,1},{3,2},{4,7},{5,4},{6,5},{7,6},{8,11},{9,8},{10,9... | collective-permute-start | bytes 221192 | tf_op jit(solution)/shard_map/ppermute | solution.py:88
  162.5 2.0 shard_map.121.refs_4_.refs_12_
  177.0 2.2 collective-permute-start.16
  183.2 2.0 shard_map.131.refs_3_
  185.2 2.0 shard_map.129.refs_1_.refs_7_
  191.9 3.0 %collective-permute-done.19.refs_3_ = bf16[144,512]{1,0:T(8,128)(2,1)S(1)} collective-permute-done((bf16[144,512]{1,0:T(8,128)(2,1)S(1)}, bf16[144,512]{1,0:T(8,128)(2,1)S(1)}, u32[]{:S(2)}, u32[]{:S(2)}) %collective-permute-start.19) | collective-permute-done | bytes 147488 | tf_op jit(solution)/shard_map/ppermute | solution.py:88
  202.2 2.1 collective-permute-done.22.refs_3_
  210.3 2.8 collective-permute-done.27.refs_5_
  213.2 2.4 collective-permute-done.25.refs_3_
  220.0 3.0 %shard_map.137 = (bf16[4,2,256,128]{3,2,1,0:T(8,128)(2,1)S(1)}, bf16[4,2,256,128]{3,2,1,0:T(8,128)(2,1)}, bf16[4,2,256,128]{3,2,1,0:T(8,128)(2,1)S(1)}, bf16[4,2,256,128]{3,2,1,0:T(8,128)(2,1)S(1)}) custom-call(s32[5]{0:T(128)S(1)} %copy-done.8, bf16[128,4096]{1,0:T(8,128)(2,1)S(1)} %get-tuple-element.127.refs_1_, ...), custom_call_target="tpu_custom_call" | custom-call | bytes 11220000 | tf_op jit(solution)/shard_map/pallas_call | solution.py:70
  228.9 3.4 %shard_map.139 = (bf16[4,2,256,128]{3,2,1,0:T(8,128)(2,1)S(1)}, bf16[4,2,256,128]{3,2,1,0:T(8,128)(2,1)}, bf16[4,2,256,128]{3,2,1,0:T(8,128)(2,1)}, bf16[4,2,256,128]{3,2,1,0:T(8,128)(2,1)}) custom-call(s32[5]{0:T(128)S(1)} %copy-done.8, bf16[16,256,128]{2,1,0:T(8,128)(2,1)S(1)} %shard_map.135.refs_1_, bf16[128,4096]{1,0:T(8,128)(2,1)S(1)} %shard_map.138.refs_2_, ...), custom_call_target="tpu_custom_call" | custom-call | bytes 6800000 | tf_op jit(solution)/shard_map/pallas_call | solution.py:70
  233.6 4.7 %collective-permute-start.40 = (bf16[4,2,256,128]{3,2,1,0:T(8,128)(2,1)}, bf16[4,2,256,128]{3,2,1,0:T(8,128)(2,1)S(1)}, u32[]{:S(2)}, u32[]{:S(2)}) collective-permute-start(bf16[4,2,256,128]{3,2,1,0:T(8,128)(2,1)} %get-tuple-element.151), channel_id=1, source_target_pairs={{0,16},{4,20},{8,24},{12,28},{16,0},{20,4},{24,8},{28,12},{32,48},... | collective-permute-start | bytes 1572872 | tf_op jit(solution)/shard_map/ppermute | solution.py:84
  238.2 2.6 collective-permute-done.33.refs_4_
  240.8 2.5 collective-permute-start.41
  246.5 5.4 %collective-permute-done.34.refs_5_ = bf16[4,2,256,128]{3,2,1,0:T(8,128)(2,1)} collective-permute-done((bf16[4,2,256,128]{3,2,1,0:T(8,128)(2,1)}, bf16[4,2,256,128]{3,2,1,0:T(8,128)(2,1)}, u32[]{:S(2)}, u32[]{:S(2)}) %collective-permute-start.34) | collective-permute-done | bytes 524320 | tf_op jit(solution)/shard_map/ppermute | solution.py:84
  255.1 4.3 %collective-permute-start.37 = (bf16[2,256,128]{2,1,0:T(8,128)(2,1)S(1)}, bf16[2,256,128]{2,1,0:T(8,128)(2,1)S(1)}, u32[]{:S(2)}, u32[]{:S(2)}) collective-permute-start(bf16[2,256,128]{2,1,0:T(8,128)(2,1)S(1)} %get-tuple-element.148), channel_id=1, source_target_pairs={{0,16},{4,20},{8,24},{12,28},{16,0},{20,4},{24,8},{28,12},{32,48},... | collective-permute-start | bytes 393224 | tf_op jit(solution)/shard_map/ppermute | solution.py:84
  259.4 3.6 %collective-permute-start.38 = (bf16[2,256,128]{2,1,0:T(8,128)(2,1)S(1)}, bf16[2,256,128]{2,1,0:T(8,128)(2,1)S(1)}, u32[]{:S(2)}, u32[]{:S(2)}) collective-permute-start(bf16[2,256,128]{2,1,0:T(8,128)(2,1)S(1)} %get-tuple-element.149), channel_id=1, source_target_pairs={{0,24},{4,28},{8,0},{12,4},{16,8},{20,12},{24,16},{28,20},{32,56},... | collective-permute-start | bytes 393224 | tf_op jit(solution)/shard_map/ppermute | solution.py:84
  264.2 2.2 collective-permute-start.48
  266.4 4.5 %collective-permute-start.43 = (bf16[2,256,128]{2,1,0:T(8,128)(2,1)S(1)}, bf16[2,256,128]{2,1,0:T(8,128)(2,1)S(1)}, u32[]{:S(2)}, u32[]{:S(2)}) collective-permute-start(bf16[2,256,128]{2,1,0:T(8,128)(2,1)S(1)} %get-tuple-element.155), channel_id=1, source_target_pairs={{0,64},{4,68},{8,72},{12,76},{16,80},{20,84},{24,88},{28,92},{32,9... | collective-permute-start | bytes 393224 | tf_op jit(solution)/shard_map/ppermute | solution.py:84
  270.9 2.5 collective-permute-start.44
  273.5 2.9 collective-permute-start.49
  286.0 2.1 shard_map.144
  (170 shorter events, 87.3 us)
Async XLA Ops:
  7.7 12.4 %collective-permute-start.4 = (bf16[4,32,4,16,256]{4,3,2,1,0:T(8,128)(2,1)}, bf16[4,32,4,16,256]{4,3,2,1,0:T(8,128)(2,1)}, u32[]{:S(2)}, u32[]{:S(2)}) collective-permute-start(bf16[4,32,4,16,256]{4,3,2,1,0:T(8,128)(2,1)} %shard_map.117.refs_0_), channel_id=1, source_target_pairs={{0,4},{4,0},{8,12},{12,8},{16,20},{20,16},{24,28},{28,24},{32,36},... | collective-permute-start | bytes 12582920 | tf_op jit(solution)/shard_map/ppermute | solution.py:110
  7.8 62.3 %all-to-all-start.1 = ((bf16[128,64,256]{2,1,0:T(8,128)(2,1)}), bf16[128,64,256]{2,1,0:T(8,128)(2,1)}, u32[]{:S(2)}, u32[]{:S(2)}) async-start(bf16[128,64,256]{2,1,0:T(8,128)(2,1)} %bitcast.45), calls=%async_computation.1 | async-start | bytes 8388608 | tf_op jit(solution)/shard_map/all_to_all | solution.py:404
  21.5 63.0 %collective-permute-start.5 = (bf16[32,4,16,256]{3,2,1,0:T(8,128)(2,1)}, bf16[32,4,16,256]{3,2,1,0:T(8,128)(2,1)S(1)}, u32[]{:S(2)}, u32[]{:S(2)}) collective-permute-start(bf16[32,4,16,256]{3,2,1,0:T(8,128)(2,1)} %get-tuple-element.104), channel_id=1, source_target_pairs={{0,32},{4,100},{8,40},{12,108},{16,48},{20,116},{24,56},{28,124},{... | collective-permute-start | bytes 3145736 | tf_op jit(solution)/shard_map/ppermute | solution.py:106
  23.0 61.4 %collective-permute-start.6 = (bf16[32,4,16,256]{3,2,1,0:T(8,128)(2,1)}, bf16[32,4,16,256]{3,2,1,0:T(8,128)(2,1)}, u32[]{:S(2)}, u32[]{:S(2)}) collective-permute-start(bf16[32,4,16,256]{3,2,1,0:T(8,128)(2,1)} %get-tuple-element.105), channel_id=1, source_target_pairs={{0,8},{4,28},{8,16},{12,4},{16,24},{20,12},{24,0},{28,20},{32,40},... | collective-permute-start | bytes 3145736 | tf_op jit(solution)/shard_map/ppermute | solution.py:106
  24.5 60.0 %collective-permute-start.7 = (bf16[32,4,16,256]{3,2,1,0:T(8,128)(2,1)}, bf16[32,4,16,256]{3,2,1,0:T(8,128)(2,1)}, u32[]{:S(2)}, u32[]{:S(2)}) collective-permute-start(bf16[32,4,16,256]{3,2,1,0:T(8,128)(2,1)} %get-tuple-element.106), channel_id=1, source_target_pairs={{0,1},{1,2},{2,3},{3,0},{4,7},{5,4},{6,5},{7,6},{8,9},{9,10},{10,1... | collective-permute-start | bytes 3145736 | tf_op jit(solution)/shard_map/ppermute | solution.py:98
  70.1 14.3 %all-to-all-start.2 = ((s32[128,1,16]{2,1,0:T(1,128)}), s32[128,1,16]{2,1,0:T(1,128)S(1)}, u32[]{:S(2)}, u32[]{:S(2)}) async-start(s32[128,1,16]{2,1,0:T(1,128)} %bitcast.11), calls=%async_computation.2 | async-start | bytes 131072 | tf_op jit(solution)/shard_map/all_to_all | solution.py:407
  86.6 69.1 %all-to-all-start.3 = ((bf16[128,80,256]{2,1,0:T(8,128)(2,1)}), bf16[128,80,256]{2,1,0:T(8,128)(2,1)}, u32[]{:S(2)}, u32[]{:S(2)}) async-start(bf16[128,80,256]{2,1,0:T(8,128)(2,1)} %bitcast.43), calls=%async_computation.3 | async-start | bytes 10485760 | tf_op jit(solution)/shard_map/all_to_all | solution.py:417
  95.3 67.2 %collective-permute-start = (bf16[2,4,32,256]{3,2,1,0:T(8,128)(2,1)}, bf16[2,4,32,256]{3,2,1,0:T(8,128)(2,1)S(1)}, u32[]{:S(2)}, u32[]{:S(2)}) collective-permute-start(bf16[2,4,32,256]{3,2,1,0:T(8,128)(2,1)} %get-tuple-element.90), channel_id=1, source_target_pairs={{0,1},{1,2},{2,3},{3,0},{4,5},{5,6},{6,7},{7,4},{8,9},{9,10},{10,1... | collective-permute-start | bytes 393224 | tf_op jit(solution)/shard_map/ppermute | solution.py:88
  96.9 69.5 %collective-permute-start.1 = (bf16[2,4,32,256]{3,2,1,0:T(8,128)(2,1)}, bf16[2,4,32,256]{3,2,1,0:T(8,128)(2,1)S(1)}, u32[]{:S(2)}, u32[]{:S(2)}) collective-permute-start(bf16[2,4,32,256]{3,2,1,0:T(8,128)(2,1)} %get-tuple-element.91), channel_id=1, source_target_pairs={{0,2},{1,3},{2,0},{3,1},{4,6},{5,7},{6,4},{7,5},{8,10},{9,11},{10,... | collective-permute-start | bytes 393224 | tf_op jit(solution)/shard_map/ppermute | solution.py:88
  100.1 66.3 %collective-permute-start.2 = (bf16[2,4,32,256]{3,2,1,0:T(8,128)(2,1)}, bf16[2,4,32,256]{3,2,1,0:T(8,128)(2,1)S(1)}, u32[]{:S(2)}, u32[]{:S(2)}) collective-permute-start(bf16[2,4,32,256]{3,2,1,0:T(8,128)(2,1)} %get-tuple-element.92), channel_id=1, source_target_pairs={{0,3},{1,0},{2,1},{3,2},{4,7},{5,4},{6,5},{7,6},{8,11},{9,8},{10,9... | collective-permute-start | bytes 393224 | tf_op jit(solution)/shard_map/ppermute | solution.py:88
  158.9 7.6 %collective-permute-start.10 = (bf16[144,256]{1,0:T(8,128)(2,1)S(1)}, bf16[144,256]{1,0:T(8,128)(2,1)S(1)}, u32[]{:S(2)}, u32[]{:S(2)}) collective-permute-start(bf16[144,256]{1,0:T(8,128)(2,1)S(1)} %shard_map.124.refs_6_), channel_id=1, source_target_pairs={{0,2},{1,3},{2,0},{3,1},{4,6},{5,7},{6,4},{7,5},{8,10},{9,11},{10,... | collective-permute-start | bytes 221192 | tf_op jit(solution)/shard_map/ppermute | solution.py:88
  177.0 10.2 %collective-permute-start.16 = (bf16[144,256]{1,0:T(8,128)(2,1)S(1)}, bf16[144,256]{1,0:T(8,128)(2,1)S(1)}, u32[]{:S(2)}, u32[]{:S(2)}) collective-permute-start(bf16[144,256]{1,0:T(8,128)(2,1)S(1)} %get-tuple-element.118.refs_5_), channel_id=1, source_target_pairs={{0,2},{1,3},{2,0},{3,1},{4,6},{5,7},{6,4},{7,5},{8,10},{9,11},{10,... | collective-permute-start | bytes 221192 | tf_op jit(solution)/shard_map/ppermute | solution.py:88
  179.3 8.0 %collective-permute-start.15 = (bf16[144,256]{1,0:T(8,128)(2,1)S(1)}, bf16[144,256]{1,0:T(8,128)(2,1)S(1)}, u32[]{:S(2)}, u32[]{:S(2)}) collective-permute-start(bf16[144,256]{1,0:T(8,128)(2,1)S(1)} %get-tuple-element.118.refs_5_), channel_id=1, source_target_pairs={{0,3},{1,0},{2,1},{3,2},{4,7},{5,4},{6,5},{7,6},{8,11},{9,8},{10,9... | collective-permute-start | bytes 221192 | tf_op jit(solution)/shard_map/ppermute | solution.py:88
  189.5 7.1 %collective-permute-start.18 = (bf16[144,512]{1,0:T(8,128)(2,1)S(1)}, bf16[144,512]{1,0:T(8,128)(2,1)S(1)}, u32[]{:S(2)}, u32[]{:S(2)}) collective-permute-start(bf16[144,512]{1,0:T(8,128)(2,1)S(1)} %get-tuple-element.119.refs_0_), channel_id=1, source_target_pairs={{0,3},{1,0},{2,1},{3,2},{4,7},{5,4},{6,5},{7,6},{8,11},{9,8},{10,9... | collective-permute-start | bytes 442376 | tf_op jit(solution)/shard_map/ppermute | solution.py:88
  202.2 13.4 %collective-permute-start.24 = (bf16[128,4096]{1,0:T(8,128)(2,1)S(1)}, bf16[128,4096]{1,0:T(8,128)(2,1)S(1)}, u32[]{:S(2)}, u32[]{:S(2)}) collective-permute-start(bf16[128,4096]{1,0:T(8,128)(2,1)S(1)} %get-tuple-element.127.refs_1_), channel_id=1, source_target_pairs={{0,4},{4,0},{8,12},{12,8},{16,20},{20,16},{24,28},{28,24},{32,36},... | collective-permute-start | bytes 3145736 | tf_op jit(solution)/shard_map/ppermute | solution.py:110
  207.1 8.5 %collective-permute-start.23 = (bf16[128,4096]{1,0:T(8,128)(2,1)S(1)}, bf16[128,4096]{1,0:T(8,128)(2,1)S(1)}, u32[]{:S(2)}, u32[]{:S(2)}) collective-permute-start(bf16[128,4096]{1,0:T(8,128)(2,1)S(1)} %get-tuple-element.126.refs_1_), channel_id=1, source_target_pairs={{0,4},{4,0},{8,12},{12,8},{16,20},{20,16},{24,28},{28,24},{32,36},... | collective-permute-start | bytes 3145736 | tf_op jit(solution)/shard_map/ppermute | solution.py:110
  216.5 7.2 %collective-permute-start.31 = (bf16[128,256]{1,0:T(8,128)(2,1)S(1)}, bf16[128,256]{1,0:T(8,128)(2,1)S(1)}, u32[]{:S(2)}, u32[]{:S(2)}) collective-permute-start(bf16[128,256]{1,0:T(8,128)(2,1)S(1)} %get-tuple-element.135.refs_2_), channel_id=1, source_target_pairs={{0,2},{1,3},{2,0},{3,1},{4,6},{5,7},{6,4},{7,5},{8,10},{9,11},{10,... | collective-permute-start | bytes 196616 | tf_op jit(solution)/shard_map/ppermute | solution.py:88
  216.7 7.1 %collective-permute-start.30 = (bf16[128,256]{1,0:T(8,128)(2,1)S(1)}, bf16[128,256]{1,0:T(8,128)(2,1)S(1)}, u32[]{:S(2)}, u32[]{:S(2)}) collective-permute-start(bf16[128,256]{1,0:T(8,128)(2,1)S(1)} %get-tuple-element.135.refs_2_), channel_id=1, source_target_pairs={{0,3},{1,0},{2,1},{3,2},{4,7},{5,4},{6,5},{7,6},{8,11},{9,8},{10,9... | collective-permute-start | bytes 196616 | tf_op jit(solution)/shard_map/ppermute | solution.py:88
  224.7 16.1 %collective-permute-start.33 = (bf16[4,2,256,128]{3,2,1,0:T(8,128)(2,1)}, bf16[4,2,256,128]{3,2,1,0:T(8,128)(2,1)}, u32[]{:S(2)}, u32[]{:S(2)}) collective-permute-start(bf16[4,2,256,128]{3,2,1,0:T(8,128)(2,1)} %get-tuple-element.143), channel_id=1, source_target_pairs={{0,32},{4,36},{8,40},{12,44},{16,48},{20,52},{24,56},{28,60},{32,6... | collective-permute-start | bytes 1572872 | tf_op jit(solution)/shard_map/ppermute | solution.py:84
  226.2 25.6 %collective-permute-start.34 = (bf16[4,2,256,128]{3,2,1,0:T(8,128)(2,1)}, bf16[4,2,256,128]{3,2,1,0:T(8,128)(2,1)}, u32[]{:S(2)}, u32[]{:S(2)}) collective-permute-start(bf16[4,2,256,128]{3,2,1,0:T(8,128)(2,1)} %copy-done.10), channel_id=1, source_target_pairs={{0,64},{4,68},{8,72},{12,76},{16,80},{20,84},{24,88},{28,92},{32,9... | collective-permute-start | bytes 1572872 | tf_op jit(solution)/shard_map/ppermute | solution.py:84
  228.1 24.2 %collective-permute-start.35 = (bf16[4,2,256,128]{3,2,1,0:T(8,128)(2,1)}, bf16[4,2,256,128]{3,2,1,0:T(8,128)(2,1)}, u32[]{:S(2)}, u32[]{:S(2)}) collective-permute-start(bf16[4,2,256,128]{3,2,1,0:T(8,128)(2,1)} %copy-done.9), channel_id=1, source_target_pairs={{0,96},{4,100},{8,104},{12,108},{16,112},{20,116},{24,120},{28,124... | collective-permute-start | bytes 1572872 | tf_op jit(solution)/shard_map/ppermute | solution.py:84
  232.3 27.2 %collective-permute-start.39 = (bf16[4,2,256,128]{3,2,1,0:T(8,128)(2,1)}, bf16[4,2,256,128]{3,2,1,0:T(8,128)(2,1)S(1)}, u32[]{:S(2)}, u32[]{:S(2)}) collective-permute-start(bf16[4,2,256,128]{3,2,1,0:T(8,128)(2,1)} %get-tuple-element.150), channel_id=1, source_target_pairs={{0,8},{4,12},{8,16},{12,20},{16,24},{20,28},{24,0},{28,4},{32,40},... | collective-permute-start | bytes 1572872 | tf_op jit(solution)/shard_map/ppermute | solution.py:84
  233.6 29.4 %collective-permute-start.40 = (bf16[4,2,256,128]{3,2,1,0:T(8,128)(2,1)}, bf16[4,2,256,128]{3,2,1,0:T(8,128)(2,1)S(1)}, u32[]{:S(2)}, u32[]{:S(2)}) collective-permute-start(bf16[4,2,256,128]{3,2,1,0:T(8,128)(2,1)} %get-tuple-element.151), channel_id=1, source_target_pairs={{0,16},{4,20},{8,24},{12,28},{16,0},{20,4},{24,8},{28,12},{32,48},... | collective-permute-start | bytes 1572872 | tf_op jit(solution)/shard_map/ppermute | solution.py:84
  240.8 22.2 %collective-permute-start.41 = (bf16[4,2,256,128]{3,2,1,0:T(8,128)(2,1)}, bf16[4,2,256,128]{3,2,1,0:T(8,128)(2,1)S(1)}, u32[]{:S(2)}, u32[]{:S(2)}) collective-permute-start(bf16[4,2,256,128]{3,2,1,0:T(8,128)(2,1)} %get-tuple-element.152), channel_id=1, source_target_pairs={{0,24},{4,28},{8,0},{12,4},{16,8},{20,12},{24,16},{28,20},{32,56},... | collective-permute-start | bytes 1572872 | tf_op jit(solution)/shard_map/ppermute | solution.py:84
  253.9 12.5 %collective-permute-start.36 = (bf16[2,256,128]{2,1,0:T(8,128)(2,1)S(1)}, bf16[2,256,128]{2,1,0:T(8,128)(2,1)S(1)}, u32[]{:S(2)}, u32[]{:S(2)}) collective-permute-start(bf16[2,256,128]{2,1,0:T(8,128)(2,1)S(1)} %get-tuple-element.147), channel_id=1, source_target_pairs={{0,8},{4,12},{8,16},{12,20},{16,24},{20,28},{24,0},{28,4},{32,40},... | collective-permute-start | bytes 393224 | tf_op jit(solution)/shard_map/ppermute | solution.py:84
  255.1 15.8 %collective-permute-start.37 = (bf16[2,256,128]{2,1,0:T(8,128)(2,1)S(1)}, bf16[2,256,128]{2,1,0:T(8,128)(2,1)S(1)}, u32[]{:S(2)}, u32[]{:S(2)}) collective-permute-start(bf16[2,256,128]{2,1,0:T(8,128)(2,1)S(1)} %get-tuple-element.148), channel_id=1, source_target_pairs={{0,16},{4,20},{8,24},{12,28},{16,0},{20,4},{24,8},{28,12},{32,48},... | collective-permute-start | bytes 393224 | tf_op jit(solution)/shard_map/ppermute | solution.py:84
  259.4 14.0 %collective-permute-start.38 = (bf16[2,256,128]{2,1,0:T(8,128)(2,1)S(1)}, bf16[2,256,128]{2,1,0:T(8,128)(2,1)S(1)}, u32[]{:S(2)}, u32[]{:S(2)}) collective-permute-start(bf16[2,256,128]{2,1,0:T(8,128)(2,1)S(1)} %get-tuple-element.149), channel_id=1, source_target_pairs={{0,24},{4,28},{8,0},{12,4},{16,8},{20,12},{24,16},{28,20},{32,56},... | collective-permute-start | bytes 393224 | tf_op jit(solution)/shard_map/ppermute | solution.py:84
  263.8 12.5 %collective-permute-start.42 = (bf16[2,256,128]{2,1,0:T(8,128)(2,1)S(1)}, bf16[2,256,128]{2,1,0:T(8,128)(2,1)S(1)}, u32[]{:S(2)}, u32[]{:S(2)}) collective-permute-start(bf16[2,256,128]{2,1,0:T(8,128)(2,1)S(1)} %get-tuple-element.154), channel_id=1, source_target_pairs={{0,32},{4,36},{8,40},{12,44},{16,48},{20,52},{24,56},{28,60},{32,6... | collective-permute-start | bytes 393224 | tf_op jit(solution)/shard_map/ppermute | solution.py:84
  264.2 16.9 %collective-permute-start.48 = (bf16[3,4,32,256]{3,2,1,0:T(8,128)(2,1)S(1)}, bf16[3,4,32,256]{3,2,1,0:T(8,128)(2,1)S(1)}, u32[]{:S(2)}, u32[]{:S(2)}) collective-permute-start(bf16[3,4,32,256]{3,2,1,0:T(8,128)(2,1)S(1)} %get-tuple-element.161), channel_id=1, source_target_pairs={{0,1},{1,2},{2,3},{3,0},{4,5},{5,6},{6,7},{7,4},{8,9},{9,10},{10,1... | collective-permute-start | bytes 589832 | tf_op jit(solution)/shard_map/ppermute | solution.py:88
  266.4 11.8 %collective-permute-start.43 = (bf16[2,256,128]{2,1,0:T(8,128)(2,1)S(1)}, bf16[2,256,128]{2,1,0:T(8,128)(2,1)S(1)}, u32[]{:S(2)}, u32[]{:S(2)}) collective-permute-start(bf16[2,256,128]{2,1,0:T(8,128)(2,1)S(1)} %get-tuple-element.155), channel_id=1, source_target_pairs={{0,64},{4,68},{8,72},{12,76},{16,80},{20,84},{24,88},{28,92},{32,9... | collective-permute-start | bytes 393224 | tf_op jit(solution)/shard_map/ppermute | solution.py:84
  270.9 7.3 %collective-permute-start.44 = (bf16[2,256,128]{2,1,0:T(8,128)(2,1)S(1)}, bf16[2,256,128]{2,1,0:T(8,128)(2,1)S(1)}, u32[]{:S(2)}, u32[]{:S(2)}) collective-permute-start(bf16[2,256,128]{2,1,0:T(8,128)(2,1)S(1)} %get-tuple-element.156), channel_id=1, source_target_pairs={{0,96},{4,100},{8,104},{12,108},{16,112},{20,116},{24,120},{28,124... | collective-permute-start | bytes 393224 | tf_op jit(solution)/shard_map/ppermute | solution.py:84
  273.5 9.2 %collective-permute-start.49 = (bf16[3,4,32,256]{3,2,1,0:T(8,128)(2,1)S(1)}, bf16[3,4,32,256]{3,2,1,0:T(8,128)(2,1)S(1)}, u32[]{:S(2)}, u32[]{:S(2)}) collective-permute-start(bf16[3,4,32,256]{3,2,1,0:T(8,128)(2,1)S(1)} %get-tuple-element.162), channel_id=1, source_target_pairs={{0,2},{1,3},{2,0},{3,1},{4,6},{5,7},{6,4},{7,5},{8,10},{9,11},{10,... | collective-permute-start | bytes 589832 | tf_op jit(solution)/shard_map/ppermute | solution.py:88
  (39 other events, 200.2 us)
